TPU v7x, 32 devices: a whole 2x2x4 slice. The times are simulated.
32 devices in a mesh: seq: 8 (over z, y), ch: 4 (over x, core).
Axes of the slice: x: 2, y: 2, z: 4, core: 2. Of those that a mesh axis runs over, the one named last changes fastest.
Arguments:
- streams: bfloat16 [3, 1024, 4096], P(None, 'seq', 'ch'), may hold values from -6 to 6
- short_taps: float32 [3, 3, 4096], P(None, None, 'ch'), may hold values from -2.5 to 2.5
- long_filter: float32 [1024, 4096], P('seq', 'ch'), may hold values from -10 to 10
- skip_bias: float32 [4096], P('ch'), may hold values from -2.5 to 2.5
- norm_gain: float32 [4096], P('ch'), may hold values from 0.5 to 1.5
- cotangent: bfloat16 [1024, 4096], P('seq', 'ch'), may hold values from -6 to 6
Outputs:
- normed: bfloat16 [1024, 4096], P('seq', 'ch')
- stream_grads: bfloat16 [3, 1024, 4096], P(None, 'seq', 'ch')
All inputs are finite; a program needn't handle non-finite values.
Results may differ from a plain program's by a relative error of at most 0.001.
Values sent between devices are 32-bit elements; how exact they have to be, the bound alone decides.
No kernel may reach another device: no remote copies, remote signals or barrier semaphores. Data moves between devices by JAX's collectives and lax.ppermute only.
A program may use at most 64 MiB of HBM per device.

v0:
```python
import math

import jax
import jax.numpy as jnp
from jax import lax
from jax.sharding import PartitionSpec as P

EXACTNESS = lax.Precision.HIGHEST


def passed_along(block, axis, distance):
    devices = range(lax.axis_size(axis))
    route = [(i - distance, i) for i in devices if i - distance in devices]
    return lax.ppermute(block, axis, route)


def counting(amount):
    return jnp.arange(amount, dtype=jnp.int32)


def angle_pair(left_index, right_index, period, turning):
    product = left_index[:, None] * right_index[None, :] % period
    angles = product.astype(jnp.float32) * (turning * 2.0 * math.pi / period)
    return (jnp.cos(angles), jnp.sin(angles))


def neighbour_rows(edge_rows, offset):
    return passed_along(edge_rows, "seq", offset)


def swap_blocks(blocks):
    return lax.all_to_all(blocks, "seq", split_axis=1, concat_axis=0, tiled=True)


def spread_forward(series):
    length, series_count, chan_width = series.shape
    devices = lax.axis_size("seq")
    position = lax.axis_index("seq")
    sub_rows = length // devices
    period = 2 * length * devices
    gathered = swap_blocks(series.reshape(1, length, series_count, chan_width))
    cos_a, sin_a = angle_pair(counting(2 * devices), counting(devices), 2 * devices, -1.0)
    real_part = jnp.einsum("ka,absc->bksc", cos_a, gathered, precision=EXACTNESS)
    imag_part = jnp.einsum("ka,absc->bksc", sin_a, gathered, precision=EXACTNESS)
    spike_locations = position * sub_rows + counting(sub_rows)
    turn_cos, turn_sin = angle_pair(spike_locations, counting(2 * devices), period, -1.0)
    turn_cos = turn_cos[:, :, None, None]
    turn_sin = turn_sin[:, :, None, None]
    turned = jnp.concatenate(
        [real_part * turn_cos - imag_part * turn_sin, real_part * turn_sin + imag_part * turn_cos],
        axis=2,
    )
    swapped = swap_blocks(turned)
    cos_b, sin_b = angle_pair(counting(length), counting(length), length, -1.0)
    primary = jnp.einsum("jb,bksc->jksc", cos_b, swapped, precision=EXACTNESS)
    second = jnp.einsum("jb,bksc->jksc", sin_b, swapped, precision=EXACTNESS)
    return (
        primary[:, :, :series_count] - second[:, :, series_count:],
        primary[:, :, series_count:] + second[:, :, :series_count],
    )


def spread_inverse(spec_re, spec_im):
    length, pair_rows, series_count, chan_width = spec_re.shape
    devices = lax.axis_size("seq")
    position = lax.axis_index("seq")
    sub_rows = length // devices
    period = 2 * length * devices
    cos_b, sin_b = angle_pair(counting(length), counting(length), length, 1.0)
    merged = jnp.concatenate([spec_re, spec_im], axis=2)
    primary = jnp.einsum("bj,jksc->kbsc", cos_b, merged, precision=EXACTNESS)
    second = jnp.einsum("bj,jksc->kbsc", sin_b, merged, precision=EXACTNESS)
    turned = jnp.concatenate(
        [
            primary[:, :, :series_count] - second[:, :, series_count:],
            primary[:, :, series_count:] + second[:, :, :series_count],
        ],
        axis=2,
    )
    swapped = swap_blocks(turned)
    spike_locations = position * sub_rows + counting(sub_rows)
    turn_cos, turn_sin = angle_pair(counting(2 * devices), spike_locations, period, 1.0)
    turn_cos = turn_cos[:, :, None, None]
    turn_sin = turn_sin[:, :, None, None]
    real_part = swapped[:, :, :series_count]
    imag_part = swapped[:, :, series_count:]
    rotated_re = real_part * turn_cos - imag_part * turn_sin
    rotated_im = real_part * turn_sin + imag_part * turn_cos
    cos_a, sin_a = angle_pair(counting(devices), counting(2 * devices), 2 * devices, 1.0)
    result = jnp.einsum("ak,kbsc->basc", cos_a, rotated_re, precision=EXACTNESS) - jnp.einsum(
        "ak,kbsc->basc", sin_a, rotated_im, precision=EXACTNESS
    )
    returned = swap_blocks(result / period)
    return returned.reshape(length, -1, chan_width)


def local(streams, short_taps, long_filter, skip_bias, norm_gain, cotangent):
    row_count = streams.shape[1]
    chan_width = streams.shape[2]
    rim_rows = short_taps.shape[1] - 1
    widened = streams.astype(jnp.float32)
    before = neighbour_rows(widened[:, row_count - rim_rows :, :], 1)
    extended = jnp.concatenate([before, widened], axis=1)
    shorts = jnp.zeros_like(widened)
    for offset in range(short_taps.shape[1]):
        shorts = (
            shorts
            + short_taps[:, offset, None, :]
            * extended[:, rim_rows - offset : rim_rows - offset + row_count, :]
        )
    short_q, short_k, short_v = (shorts[0], shorts[1], shorts[2])
    gated_input = short_k * short_v
    cot_wide = cotangent.astype(jnp.float32)
    carried = cot_wide * short_q
    series = jnp.stack([gated_input, long_filter, carried], axis=1)
    spec_re, spec_im = spread_forward(series)
    series_axis = 2
    gated_re = lax.index_in_dim(spec_re, 0, series_axis, keepdims=False)
    gated_im = lax.index_in_dim(spec_im, 0, series_axis, keepdims=False)
    filter_re = lax.index_in_dim(spec_re, 1, series_axis, keepdims=False)
    filter_im = lax.index_in_dim(spec_im, 1, series_axis, keepdims=False)
    carry_re = lax.index_in_dim(spec_re, 2, series_axis, keepdims=False)
    carry_im = lax.index_in_dim(spec_im, 2, series_axis, keepdims=False)
    output_re = filter_re * gated_re - filter_im * gated_im
    output_im = filter_re * gated_im + filter_im * gated_re
    backward_re = filter_re * carry_re + filter_im * carry_im
    backward_im = filter_re * carry_im - filter_im * carry_re
    inverse_re = jnp.stack([output_re, backward_re], axis=series_axis)
    inverse_im = jnp.stack([output_im, backward_im], axis=series_axis)
    result = spread_inverse(inverse_re, inverse_im)
    convolved = result[:, 0]
    correlated = result[:, 1]
    direct = convolved + skip_bias * gated_input
    mixed_out = short_q * direct
    square_sum = lax.psum(jnp.sum(mixed_out * mixed_out, axis=1), "ch")
    scaling = lax.rsqrt(square_sum[:, None] / (chan_width * lax.axis_size("ch")) + 1e-06)
    normed = (mixed_out * scaling * norm_gain).astype(jnp.bfloat16)
    gated_grad = correlated + skip_bias * carried
    short_grad = jnp.stack([cot_wide * direct, gated_grad * short_v, gated_grad * short_k])
    following = neighbour_rows(short_grad[:, :rim_rows, :], -1)
    grad_ext = jnp.concatenate([short_grad, following], axis=1)
    grads = jnp.zeros_like(short_grad)
    for offset in range(short_taps.shape[1]):
        grads = grads + short_taps[:, offset, None, :] * grad_ext[:, offset : offset + row_count, :]
    return (normed, grads.astype(jnp.bfloat16))


def solution(mesh):
    placed = (
        P(None, "seq", "ch"),
        P(None, None, "ch"),
        P("seq", "ch"),
        P("ch"),
        P("ch"),
        P("seq", "ch"),
    )
    return jax.shard_map(
        local,
        mesh=mesh,
        in_specs=placed,
        out_specs=(P("seq", "ch"), P(None, "seq", "ch")),
        check_vma=False,
    )
```

profile of v0, /device:TPU:0, one launch (start us, length us, event | category | flops | bytes accessed | tf_op | source)
XLA Modules:
  0.0 403.7 jit_solution(5187813168502796333)
XLA Ops:
  0.6 0.8 slice.123
  1.4 4.9 %collective-permute-start = (f32[3,2,1024]{2,1,0:T(2,128)S(1)}, f32[3,2,1024]{2,1,0:T(2,128)S(1)}, u32[]{:S(2)}, u32[]{:S(2)}) collective-permute-start(f32[3,2,1024]{2,1,0:T(2,128)S(1)} %slice.123), channel_id=1, source_target_pairs={{0,4},{4,8},{8,12},{12,16},{16,20},{20,24},{24,28},{1,5},{5,9},{9,... | collective-permute-start | bytes 73736 | tf_op jit(solution)/shard_map/ppermute | solution.py:14
  6.3 0.9 fusion.139
  7.3 1.3 convert_element_type.52
  8.6 0.0 collective-permute-done
  8.6 0.0 copy-start.2
  8.6 0.5 fusion.11
  9.1 0.0 copy-start.3
  9.1 0.1 multiply_bitcast_fusion
  9.2 0.4 copy-done.2
  9.6 0.1 fusion.36
  9.6 0.6 copy-done.3
  10.2 0.1 maximum_bitcast_fusion
  10.3 2.8 copy.48
  13.1 6.0 %all-to-all-start = ((f32[1,128,3,1024]{3,0,2,1:T(1,128)}), f32[1,128,3,1024]{3,0,2,1:T(1,128)S(1)}, u32[]{:S(2)}, u32[]{:S(2)}) async-start(f32[1,128,3,1024]{3,0,2,1:T(1,128)} %copy.48), calls=%async_computation | async-start | bytes 3145728 | tf_op jit(solution)/shard_map/all_to_all | solution.py:32
  19.1 0.1 fusion.92
  19.2 35.8 %all-to-all-done = f32[1,128,3,1024]{3,0,2,1:T(1,128)S(1)} async-done(((f32[1,128,3,1024]{3,0,2,1:T(1,128)}), f32[1,128,3,1024]{3,0,2,1:T(1,128)S(1)}, u32[]{:S(2)}, u32[]{:S(2)}) %all-to-all-start) | async-done | bytes 1572896 | tf_op jit(solution)/shard_map/all_to_all | solution.py:32
  55.0 0.3 copy.49
  55.3 4.3 %fusion.16 = f32[16,3,1024,16]{2,3,1,0:T(8,128)S(1)} fusion(f32[8,16,3,1024]{3,1,0,2:T(8,128)S(1)} %bitcast.140), kind=kOutput, calls=%fused_computation.35 | convolution fusion | flops 75499264 | bytes 4718592 | tf_op jit(solution)/shard_map/ka,absc->bksc/dot_general | solution.py:44
  59.6 4.8 %subtract_bitcast_fusion = (f32[16,16,3,1024]{3,1,2,0:T(8,128)S(1)}, f32[16,16,3,1024]{3,1,2,0:T(8,128)S(1)}) fusion(f32[16,3,1024,16]{2,3,1,0:T(8,128)S(1)} %fusion.16, f32[16,16]{1,0:T(8,128)S(1)} %get-tuple-element.22, f32[16,16]{1,0:T(8,128)S(1)} %get-tuple-element.24, f32[8,16,3,1024]{3,1,0,2:T(8,128)S(1)} %bitcast.141), kind=kOutput, calls=%fused_computation.6 | convolution fusion | flops 80217856 | bytes 11012096 | tf_op jit(solution)/shard_map/ka,absc->bksc/dot_general | solution.py:43
  64.4 1.1 pad_maximum_fusion
  65.5 4.0 %copy.52 = f32[16,16,6,1024]{3,0,2,1:T(8,128)S(1)} copy(f32[16,16,6,1024]{3,1,2,0:T(8,128)S(1)} %pad_maximum_fusion) | data formatting | bytes 12582912 | tf_op jit(solution)/shard_map/concatenate | solution.py:49
  69.6 141.4 %all_to_all.63 = f32[16,16,6,1024]{3,0,2,1:T(8,128)S(1)} all-to-all(f32[16,16,6,1024]{3,0,2,1:T(8,128)S(1)} %copy.52), channel_id=1, replica_groups=mesh['seq'=8,'ch'=4] {'seq'}, dimensions={1} | all-to-all | bytes 12582912 | tf_op jit(solution)/shard_map/all_to_all | solution.py:32
  211.0 1.1 copy.53
  212.1 6.4 %fusion.41 = f32[128,2,6,1024]{3,0,2,1:T(8,128)S(1)} fusion(f32[128,2,6,1024]{3,0,2,1:T(8,128)S(1)} %bitcast.135), kind=kOutput, calls=%fused_computation.72 | convolution fusion | flops 2416148480 | bytes 12582912 | tf_op jit(solution)/shard_map/jb,bksc->jksc/dot_general | solution.py:56
  218.6 6.6 %fusion.43 = f32[128,2,6,1024]{3,0,2,1:T(8,128)S(1)} fusion(f32[128,2,6,1024]{3,0,2,1:T(8,128)S(1)} %bitcast.136), kind=kOutput, calls=%fused_computation.74 | convolution fusion | flops 2416148480 | bytes 12582912 | tf_op jit(solution)/shard_map/jb,bksc->jksc/dot_general | solution.py:55
  225.2 3.4 slice_subtract_fusion
  228.6 2.6 multiply_subtract_fusion.2
  231.2 7.1 %fusion.3 = f32[2,128,4,1024]{1,3,2,0:T(8,128)S(1)} fusion(f32[128,2,1,1024]{3,0,2,1:T(8,128)S(1)} %get-tuple-element.11, f32[128,2,1,1024]{3,0,2,1:T(8,128)S(1)} %get-tuple-element.13, f32[128,2,1,1024]{3,0,2,1:T(8,128)S(1)} %get-tuple-element.12, f32[128,2,1,1024]{3,0,2,1:T(8,128)S(1)} %get-tuple-element.10), kind=kOutput, calls=%fused_computation.10 | convolution fusion | flops 1613987840 | bytes 8388608 | tf_op jit(solution)/shard_map/bj,jksc->kbsc/dot_general | solution.py:72
  238.3 7.3 %fusion.2 = f32[2,128,4,1024]{1,3,2,0:T(8,128)S(1)} fusion(f32[128,2,1,1024]{3,0,2,1:T(8,128)S(1)} %get-tuple-element.11, f32[128,2,1,1024]{3,0,2,1:T(8,128)S(1)} %get-tuple-element.13, f32[128,2,1,1024]{3,0,2,1:T(8,128)S(1)} %get-tuple-element.12, f32[128,2,1,1024]{3,0,2,1:T(8,128)S(1)} %get-tuple-element.10), kind=kOutput, calls=%fused_computation.9 | convolution fusion | flops 1613987840 | bytes 8388608 | tf_op jit(solution)/shard_map/bj,jksc->kbsc/dot_general | solution.py:71
  245.6 0.4 slice_subtract_fusion.1
  246.0 2.3 pad_maximum_fusion.2
  248.2 5.5 %copy.56 = f32[2,128,4,1024]{3,2,0,1:T(4,128)} copy(f32[2,128,4,1024]{1,3,2,0:T(8,128)} %pad_maximum_fusion.2) | data formatting | bytes 8388608 | tf_op jit(solution)/shard_map/concatenate | solution.py:73
  253.7 96.7 %all_to_all.64 = f32[2,128,4,1024]{3,2,0,1:T(4,128)S(1)} all-to-all(f32[2,128,4,1024]{3,2,0,1:T(4,128)} %copy.56), channel_id=1, replica_groups=mesh['seq'=8,'ch'=4] {'seq'}, dimensions={1} | all-to-all | bytes 8388608 | tf_op jit(solution)/shard_map/all_to_all | solution.py:32
  350.4 2.4 copy.57
  352.8 0.6 copy.58
  353.4 1.0 multiply_subtract_fusion
  354.5 2.4 fusion.4
  356.9 2.5 fusion.26
  359.4 0.8 copy.61
  360.2 0.0 copy-start.5
  360.2 28.5 %all_to_all.65 = f32[16,8,2,1024]{3,2,0,1:T(2,128)S(1)} all-to-all(f32[16,8,2,1024]{3,2,0,1:T(2,128)S(1)} %copy.61), channel_id=1, replica_groups=mesh['seq'=8,'ch'=4] {'seq'}, dimensions={1} | all-to-all | bytes 2097152 | tf_op jit(solution)/shard_map/all_to_all | solution.py:32
  388.7 0.3 copy.62
  389.0 0.0 copy-done.5
  389.0 0.3 fusion.29
  389.3 0.0 copy-start
  389.4 0.8 copy-done
  390.1 0.0 copy-start.4
  390.1 0.1 multiply_reduce_fusion
  390.3 5.7 %psum.7 = f32[128]{0:T(128)S(1)} all-reduce(f32[128]{0:T(128)S(1)} %multiply_reduce_fusion), channel_id=1, replica_groups=mesh['seq'=8,'ch'=4] {'ch'}, use_global_device_ids=true, to_apply=%region_1.2 | all-reduce | flops 128 | bytes 1024 | tf_op jit(solution)/shard_map/psum | solution.py:135
  395.9 0.0 copy-start.1
  395.9 0.2 pad_maximum_fusion.11
  396.1 1.3 collective-permute-start.1
  397.4 0.0 copy-done.4
  397.4 0.0 copy-done.1
  397.5 0.8 multiply_convert_fusion
  398.3 3.6 collective-permute-done.1
  401.9 0.2 pad_maximum_fusion.9
  402.1 1.4 fusion.13
  (5 shorter events, 0.0 us)
Async XLA Ops:
  1.4 7.2 %collective-permute-start = (f32[3,2,1024]{2,1,0:T(2,128)S(1)}, f32[3,2,1024]{2,1,0:T(2,128)S(1)}, u32[]{:S(2)}, u32[]{:S(2)}) collective-permute-start(f32[3,2,1024]{2,1,0:T(2,128)S(1)} %slice.123), channel_id=1, source_target_pairs={{0,4},{4,8},{8,12},{12,16},{16,20},{20,24},{24,28},{1,5},{5,9},{9,... | collective-permute-start | bytes 73736 | tf_op jit(solution)/shard_map/ppermute | solution.py:14
  8.6 1.0 copy-start.2
  9.1 1.1 copy-start.3
  13.1 41.9 %all-to-all-start = ((f32[1,128,3,1024]{3,0,2,1:T(1,128)}), f32[1,128,3,1024]{3,0,2,1:T(1,128)S(1)}, u32[]{:S(2)}, u32[]{:S(2)}) async-start(f32[1,128,3,1024]{3,0,2,1:T(1,128)} %copy.48), calls=%async_computation | async-start | bytes 3145728 | tf_op jit(solution)/shard_map/all_to_all | solution.py:32
  360.2 28.8 %copy-start.5 = (f32[1024]{0:T(1024)S(1)}, f32[1024]{0:T(1024)}, u32[]{:S(2)}) copy-start(f32[1024]{0:T(1024)} %param.9) | copy-start | bytes 12292
  389.3 0.8 copy-start
  390.1 7.3 %copy-start.4 = (f32[1024]{0:T(1024)S(1)}, f32[1024]{0:T(1024)}, u32[]{:S(2)}) copy-start(f32[1024]{0:T(1024)} %param.10) | copy-start | bytes 12292
  395.9 1.5 copy-start.1
  396.1 5.7 %collective-permute-start.1 = (f32[3,2,1024]{2,1,0:T(2,128)S(1)}, f32[3,2,1024]{2,1,0:T(2,128)S(1)}, u32[]{:S(2)}, u32[]{:S(2)}) collective-permute-start(f32[3,2,1024]{2,1,0:T(2,128)S(1)} %slice.147), channel_id=1, source_target_pairs={{4,0},{8,4},{12,8},{16,12},{20,16},{24,20},{28,24},{5,1},{9,5},{13... | collective-permute-start | bytes 73736 | tf_op jit(solution)/shard_map/ppermute | solution.py:14
where the time goes:
time: 407 us; the launch traced here: 404 us
  blocking collectives  272 us (67%)
  matrix products  41.3 us (10%)
  waiting for transfers between devices  39.4 us (10%)
  local copies, waits for them, and re-layouts  21.5 us (5%)
  other arithmetic  16 us (4%)
  starting transfers between devices  12.1 us (3%)
    all_to_all x3, blocking collectives, swap_blocks(): lax.all_to_all(blocks, 'seq', split_axis=1, concat_axis=0, tiled=True)  267 us
    all_to_all x1, waiting for transfers between devices, swap_blocks(): lax.all_to_all(blocks, 'seq', split_axis=1, concat_axis=0, tiled=True)  35.8 us
  transfers between devices with their start and end apart: 3, of which 2 were waited for; matrix products, arithmetic and copies ran while one was open for 1% of the time, Pallas kernels for 0%

commit v1 on v0

--- a/solution.py
+++ b/solution.py
@@ -1,9 +1,472 @@
+import functools
 import math
 
 import jax
 import jax.numpy as jnp
+import numpy as np
 from jax import lax
+from jax.experimental import pallas as pl
+from jax.experimental.pallas import tpu as pltpu
 from jax.sharding import PartitionSpec as P
+
+F32 = jnp.float32
+BF16 = jnp.bfloat16
+PAD_ROWS = 8
+VMEM_BYTES = 48 * 1024 * 1024
+
+
+def shift_along(block, axis, distance):
+    devices = range(lax.axis_size(axis))
+    route = [(i - distance, i) for i in devices if i - distance in devices]
+    return lax.ppermute(block, axis, route)
+
+
+def params():
+    return pltpu.CompilerParams(vmem_limit_bytes=VMEM_BYTES)
+
+
+def split_table(table):
+    high = table.astype(BF16)
+    low = (table - high.astype(np.float64)).astype(BF16)
+    return high, low
+
+
+def stage_tables(blocks, rows):
+    period = 2 * blocks * rows
+    place = np.arange(rows)
+
+    def angles(first, count):
+        bins = first + 2 * blocks * np.arange(count)
+        turn = 2.0 * np.pi * ((bins[:, None] * place[None, :]) % period) / period
+        return np.cos(turn), np.sin(turn)
+
+    tables = np.zeros((blocks, 2 * rows, 2 * rows))
+    half = rows // 2
+    cos_0, sin_0 = angles(0, half)
+    cos_n, sin_n = angles(blocks, half)
+    tables[0, :half, :rows] = cos_0
+    tables[0, half:rows, rows:] = cos_n
+    tables[0, rows : rows + half, :rows] = -sin_0
+    tables[0, rows, :rows] = 1.0 - 2.0 * (place % 2)
+    tables[0, rows + half :, rows:] = -sin_n
+    for first in range(1, blocks):
+        cos_k, sin_k = angles(first, rows)
+        tables[first] = np.block([[cos_k, sin_k], [-sin_k, cos_k]])
+    return split_table(tables) + split_table(np.swapaxes(tables, 1, 2))
+
+
+def scaled(value, factor):
+    if abs(factor) < 1e-12:
+        return None
+    if abs(factor - 1.0) < 1e-12:
+        return value
+    if abs(factor + 1.0) < 1e-12:
+        return -value
+    return value * factor
+
+
+def total(terms):
+    kept = [term for term in terms if term is not None]
+    if not kept:
+        return None
+    result = kept[0]
+    for term in kept[1:]:
+        result = result + term
+    return result
+
+
+def plus(left, right):
+    return total([left, right])
+
+
+def minus(left, right):
+    return total([left, None if right is None else -right])
+
+
+def store_split(high_ref, low_ref, index, value):
+    high = value.astype(BF16)
+    high_ref[index] = high
+    low_ref[index] = (value - high.astype(F32)).astype(BF16)
+
+
+def first_stage(x_ref, high_ref, low_ref, tile):
+    blocks, rows = x_ref.shape[0], x_ref.shape[1]
+    for start in range(0, rows, tile):
+        here = slice(start, start + tile)
+        there = slice(rows + start, rows + start + tile)
+        x = [x_ref[a, here, :] for a in range(blocks)]
+        for k in range(blocks // 2 + 1):
+            parts = []
+            for parity in (0, 1):
+                members = range(parity, blocks, 2)
+                turn = [math.pi * ((a * k) % (2 * blocks)) / blocks for a in members]
+                parts.append(total([scaled(x[a], math.cos(t)) for a, t in zip(members, turn)]))
+                parts.append(total([scaled(x[a], math.sin(t)) for a, t in zip(members, turn)]))
+            even_c, even_s, odd_c, odd_s = parts
+            if k == 0:
+                store_split(high_ref, low_ref, (0, here), plus(even_c, odd_c))
+                store_split(high_ref, low_ref, (0, there), minus(even_c, odd_c))
+                continue
+            store_split(high_ref, low_ref, (k, here), plus(even_c, odd_c))
+            store_split(high_ref, low_ref, (k, there), -plus(even_s, odd_s))
+            if 2 * k != blocks:
+                store_split(high_ref, low_ref, (blocks - k, here), minus(even_c, odd_c))
+                store_split(high_ref, low_ref, (blocks - k, there), minus(even_s, odd_s))
+
+
+def last_stage(v_ref, out_ref, tile):
+    blocks, rows = v_ref.shape[0], v_ref.shape[1] // 2
+    for start in range(0, rows, tile):
+        here = slice(start, start + tile)
+        there = slice(rows + start, rows + start + tile)
+        first = v_ref[0, here, :]
+        last = v_ref[0, there, :]
+        re = {k: v_ref[k, here, :] for k in range(1, blocks)}
+        im = {k: v_ref[k, there, :] for k in range(1, blocks)}
+        for parity in (0, 1):
+            sign = 1.0 - 2.0 * parity
+            base = first + sign * last
+            re_sum = {k: re[k] + sign * re[blocks - k] for k in range(1, blocks // 2)}
+            im_sum = {k: im[k] - sign * im[blocks - k] for k in range(1, blocks // 2)}
+            re_sum[blocks // 2] = re[blocks // 2]
+            im_sum[blocks // 2] = im[blocks // 2]
+            for a in range(parity, blocks, 2):
+                terms = [base]
+                for k in range(1, blocks // 2 + 1):
+                    turn = math.pi * ((a * k) % (2 * blocks)) / blocks
+                    terms.append(scaled(re_sum[k], math.cos(turn)))
+                    terms.append(scaled(im_sum[k], -math.sin(turn)))
+                value = total(terms)
+                out_ref[a, here, :] = value
+                if start == 0 and a > 0:
+                    out_ref[a - 1, rows : rows + PAD_ROWS, :] = value[:PAD_ROWS]
+    out_ref[blocks - 1, rows : rows + PAD_ROWS, :] = jnp.zeros((PAD_ROWS, out_ref.shape[2]), F32)
+
+
+def dot(left, right):
+    return lax.dot_general(left, right, (((1,), (0,)), ((), ())), preferred_element_type=F32)
+
+
+def exact_dot(table_high, table_low, high, low):
+    return dot(table_high, high) + dot(table_high, low) + dot(table_low, high)
+
+
+def spectrum_kernel(x_ref, gh_ref, gl_ref, spec_ref, high_ref, low_ref):
+    blocks, rows = x_ref.shape[0], x_ref.shape[1]
+    first_stage(x_ref, high_ref, low_ref, 32)
+    scale = 1.0 / (blocks * rows)
+    for k in range(blocks):
+        spec = exact_dot(gh_ref[k], gl_ref[k], high_ref[k], low_ref[k]) * scale
+        spec_ref[k] = spec
+        if k == 0:
+            for row in (0, rows):
+                spec_ref[0, row : row + 1, :] = 0.5 * spec[row : row + 1]
+
+
+def product_kernel(conjugate, x_ref, spec_ref, gh_ref, gl_ref, th_ref, tl_ref, out_ref, high_ref, low_ref, v_ref):
+    blocks, rows = x_ref.shape[0], x_ref.shape[1]
+    first_stage(x_ref, high_ref, low_ref, 32)
+    sign = -1.0 if conjugate else 1.0
+    for k in range(blocks):
+        spec = exact_dot(gh_ref[k], gl_ref[k], high_ref[k], low_ref[k])
+        x_re, x_im = spec[:rows], spec[rows:]
+        h_re, h_im = spec_ref[k, :rows, :], spec_ref[k, rows:, :]
+        cross = x_im * h_im
+        if k == 0:
+            real_row = lax.broadcasted_iota(jnp.int32, cross.shape, 0) == 0
+            out_re = x_re * h_re - sign * jnp.where(real_row, 0.0, cross)
+            out_im = jnp.where(real_row, cross, x_im * h_re + sign * (x_re * h_im))
+        else:
+            out_re = x_re * h_re - sign * cross
+            out_im = x_im * h_re + sign * (x_re * h_im)
+        out = jnp.concatenate([out_re, out_im], axis=0)
+        high = out.astype(BF16)
+        low = (out - high.astype(F32)).astype(BF16)
+        v_ref[k] = exact_dot(th_ref[k], tl_ref[k], high, low)
+    last_stage(v_ref, out_ref, 32)
+
+
+def scratch(blocks, rows, width, inverse):
+    shape = (blocks, 2 * rows, width)
+    kept = [pltpu.VMEM(shape, BF16), pltpu.VMEM(shape, BF16)]
+    return kept + [pltpu.VMEM(shape, F32)] if inverse else kept
+
+
+def spectrum(x, tables):
+    blocks, rows, width = x.shape
+    return pl.pallas_call(
+        spectrum_kernel,
+        out_shape=jax.ShapeDtypeStruct((blocks, 2 * rows, width), F32),
+        scratch_shapes=scratch(blocks, rows, width, False),
+        compiler_params=params(),
+        name="filter_spectrum",
+    )(x, tables[0], tables[1])
+
+
+def through_filter(x, spec, tables, conjugate):
+    blocks, rows, width = x.shape
+    return pl.pallas_call(
+        functools.partial(product_kernel, conjugate),
+        out_shape=jax.ShapeDtypeStruct((blocks, rows + PAD_ROWS, width), F32),
+        scratch_shapes=scratch(blocks, rows, width, True),
+        compiler_params=params(),
+        name="correlation" if conjugate else "convolution",
+    )(x, spec, *tables)
+
+
+def row_number(shape):
+    return lax.broadcasted_iota(jnp.int32, shape, 0)
+
+
+def delayed(x, before, distance):
+    moved = pltpu.roll(x, distance, 0)
+    rows = row_number(x.shape)
+    rim = len(before)
+    for row in range(distance):
+        moved = jnp.where(rows == row, before[rim - distance + row], moved)
+    return moved
+
+
+def advanced(x, after, distance):
+    count = x.shape[0]
+    moved = pltpu.roll(x, count - distance, 0)
+    rows = row_number(x.shape)
+    for row in range(distance):
+        moved = jnp.where(rows == count - distance + row, after[row], moved)
+    return moved
+
+
+def rows_of(block):
+    return [block[row : row + 1] for row in range(block.shape[0])]
+
+
+def short_filter_after(after, last, taps):
+    known = last + after
+    return [
+        total([taps[j : j + 1] * known[len(last) + row - j] for j in range(taps.shape[0])])
+        for row in range(len(after))
+    ]
+
+
+def short_filter(x, before, taps):
+    result = taps[0:1] * x
+    for j in range(1, taps.shape[0]):
+        result = result + taps[j : j + 1] * delayed(x, before, j)
+    return result
+
+
+def short_transpose(x, after, taps):
+    result = taps[0:1] * x
+    for j in range(1, taps.shape[0]):
+        result = result + taps[j : j + 1] * advanced(x, after, j)
+    return result
+
+
+def gate_kernel(streams_ref, before_ref, taps_ref, cot_ref, gated_ref, carried_ref):
+    block = gated_ref.shape[2]
+    for part in range(gated_ref.shape[0]):
+        lanes = slice(part * block, (part + 1) * block)
+        short = [
+            short_filter(streams_ref[i, :, lanes].astype(F32), rows_of(before_ref[i, :, lanes]), taps_ref[i, :, lanes])
+            for i in range(3)
+        ]
+        gated_ref[part] = short[1] * short[2]
+        carried_ref[part] = cot_ref[:, lanes].astype(F32) * short[0]
+
+
+def gate(streams, before, taps, cotangent, parts):
+    _, rows, width = streams.shape
+    block = width // parts
+    steps = 4
+    span = width // steps
+    per_step = parts // steps
+    rim, count = before.shape[1], taps.shape[1]
+    chunk = jax.ShapeDtypeStruct((parts, rows, block), F32)
+    return pl.pallas_call(
+        gate_kernel,
+        grid=(steps,),
+        in_specs=[
+            pl.BlockSpec((3, rows, span), lambda i: (0, 0, i)),
+            pl.BlockSpec((3, rim, span), lambda i: (0, 0, i)),
+            pl.BlockSpec((3, count, span), lambda i: (0, 0, i)),
+            pl.BlockSpec((rows, span), lambda i: (0, i)),
+        ],
+        out_specs=[pl.BlockSpec((per_step, rows, block), lambda i: (i, 0, 0))] * 2,
+        out_shape=[chunk, chunk],
+        compiler_params=params(),
+        name="short_filters",
+    )(streams, before, taps, cotangent)
+
+
+def mix_kernel(streams_ref, before_ref, taps_ref, bias_ref, conv_ref, mixed_ref, square_ref):
+    step = pl.program_id(0)
+    block = conv_ref.shape[2]
+    rows = streams_ref.shape[1]
+    squares = jnp.zeros((rows, block), F32)
+    for part in range(conv_ref.shape[0]):
+        lanes = slice(part * block, (part + 1) * block)
+        short = [
+            short_filter(streams_ref[i, :, lanes].astype(F32), rows_of(before_ref[i, :, lanes]), taps_ref[i, :, lanes])
+            for i in range(3)
+        ]
+        mixed = short[0] * (conv_ref[part, :rows, :] + bias_ref[:, lanes] * (short[1] * short[2]))
+        mixed_ref[:, lanes] = mixed
+        squares = squares + mixed * mixed
+    row_sums = lax.dot_general(
+        jnp.ones((8, block), F32),
+        squares,
+        (((1,), (1,)), ((), ())),
+        precision=lax.Precision.HIGHEST,
+        preferred_element_type=F32,
+    )[0:1]
+
+    @pl.when(step == 0)
+    def _():
+        square_ref[...] = row_sums
+
+    @pl.when(step > 0)
+    def _():
+        square_ref[...] += row_sums
+
+
+def mix(streams, before, taps, bias, conv):
+    _, rows, width = streams.shape
+    parts, long_rows, block = conv.shape
+    steps = 4
+    span = width // steps
+    per_step = parts // steps
+    rim, count = before.shape[1], taps.shape[1]
+    return pl.pallas_call(
+        mix_kernel,
+        grid=(steps,),
+        in_specs=[
+            pl.BlockSpec((3, rows, span), lambda i: (0, 0, i)),
+            pl.BlockSpec((3, rim, span), lambda i: (0, 0, i)),
+            pl.BlockSpec((3, count, span), lambda i: (0, 0, i)),
+            pl.BlockSpec((1, span), lambda i: (0, i)),
+            pl.BlockSpec((per_step, long_rows, block), lambda i: (i, 0, 0)),
+        ],
+        out_specs=[
+            pl.BlockSpec((rows, span), lambda i: (0, i)),
+            pl.BlockSpec((1, rows), lambda i: (0, 0)),
+        ],
+        out_shape=[
+            jax.ShapeDtypeStruct((rows, width), F32),
+            jax.ShapeDtypeStruct((1, rows), F32),
+        ],
+        compiler_params=params(),
+        name="mixed_squares",
+    )(streams, before, taps, bias, conv)
+
+
+def finish_kernel(
+    channels, streams_ref, before_ref, after_ref, taps_ref, bias_ref, gain_ref, cot_ref, mixed_ref, square_ref,
+    conv_ref, corr_ref, normed_ref, grads_ref,
+):
+    block = conv_ref.shape[2]
+    rows = streams_ref.shape[1]
+    squares = jnp.broadcast_to(square_ref[...], (block, rows)).T
+    scaling = lax.rsqrt(squares / channels + 1e-06)
+    rim = after_ref.shape[1]
+    for part in range(conv_ref.shape[0]):
+        lanes = slice(part * block, (part + 1) * block)
+        normed_ref[:, lanes] = (mixed_ref[:, lanes] * scaling * gain_ref[:, lanes]).astype(BF16)
+        bias = bias_ref[:, lanes]
+        x = [streams_ref[i, :, lanes].astype(F32) for i in range(3)]
+        after = [rows_of(after_ref[i, :, lanes]) for i in range(4)]
+        taps = [taps_ref[i, :, lanes] for i in range(3)]
+        cot = cot_ref[:, lanes].astype(F32)
+
+        def short_grads(short, cotangent, conv, corr):
+            direct = conv + bias * (short[1] * short[2])
+            gated_grad = corr + bias * (cotangent * short[0])
+            return (cotangent * direct, gated_grad * short[2], gated_grad * short[1])
+
+        short = [short_filter(x[i], rows_of(before_ref[i, :, lanes]), taps[i]) for i in range(3)]
+        short_after = [short_filter_after(after[i], rows_of(x[i][rows - rim :]), taps[i]) for i in range(3)]
+        main = short_grads(short, cot, conv_ref[part, :rows, :], corr_ref[part, :rows, :])
+        conv_after = rows_of(conv_ref[part, rows : rows + rim, :])
+        corr_after = rows_of(corr_ref[part, rows : rows + rim, :])
+        tail = [
+            short_grads([short_after[i][row] for i in range(3)], after[3][row], conv_after[row], corr_after[row])
+            for row in range(rim)
+        ]
+        for i in range(3):
+            above = [tail[row][i] for row in range(rim)]
+            grads_ref[i, :, lanes] = short_transpose(main[i], above, taps[i]).astype(BF16)
+
+
+def finish(channels, streams, before, after, taps, bias, gain, cotangent, mixed, squares, conv, corr):
+    _, rows, width = streams.shape
+    parts, long_rows, block = conv.shape
+    steps = 4
+    span = width // steps
+    per_step = parts // steps
+    rim, count = before.shape[1], taps.shape[1]
+    flat = pl.BlockSpec((rows, span), lambda i: (0, i))
+    vector = pl.BlockSpec((1, span), lambda i: (0, i))
+    chunk = pl.BlockSpec((per_step, long_rows, block), lambda i: (i, 0, 0))
+    return pl.pallas_call(
+        functools.partial(finish_kernel, float(channels)),
+        grid=(steps,),
+        in_specs=[
+            pl.BlockSpec((3, rows, span), lambda i: (0, 0, i)),
+            pl.BlockSpec((3, rim, span), lambda i: (0, 0, i)),
+            pl.BlockSpec((4, after.shape[1], span), lambda i: (0, 0, i)),
+            pl.BlockSpec((3, count, span), lambda i: (0, 0, i)),
+            vector,
+            vector,
+            flat,
+            flat,
+            pl.BlockSpec((1, rows), lambda i: (0, 0)),
+            chunk,
+            chunk,
+        ],
+        out_specs=[flat, pl.BlockSpec((3, rows, span), lambda i: (0, 0, i))],
+        out_shape=[
+            jax.ShapeDtypeStruct((rows, width), BF16),
+            jax.ShapeDtypeStruct((3, rows, width), BF16),
+        ],
+        compiler_params=params(),
+        name="norm_and_grads",
+    )(streams, before, after, taps, bias, gain, cotangent, mixed, squares, conv, corr)
+
+
+def swap_blocks(blocks):
+    return lax.all_to_all(blocks, "seq", split_axis=0, concat_axis=0, tiled=True)
+
+
+def by_blocks(rows, parts):
+    length, width = rows.shape
+    return jnp.swapaxes(rows.reshape(length, parts, width // parts), 0, 1)
+
+
+def local(streams, short_taps, long_filter, skip_bias, norm_gain, cotangent):
+    parts = lax.axis_size("seq")
+    rows, width = cotangent.shape
+    rim = short_taps.shape[1] - 1
+    tables = stage_tables(parts, rows)
+    edges = jnp.concatenate([streams[:, :rim].astype(F32), cotangent[None, :rim].astype(F32)], axis=0)
+    before = shift_along(streams[:, rows - rim :].astype(F32), "seq", 1)
+    after = shift_along(edges, "seq", -1)
+    bias, gain = skip_bias[None], norm_gain[None]
+    gated, carried = gate(streams, before, short_taps, cotangent, parts)
+    sent = jnp.concatenate([by_blocks(long_filter, parts), gated, carried], axis=1)
+    got = swap_blocks(sent)
+    spec = spectrum(got[:, :rows], tables)
+    conv = through_filter(got[:, rows : 2 * rows], spec, tables, False)
+    corr = through_filter(got[:, 2 * rows :], spec, tables, True)
+    back = swap_blocks(jnp.concatenate([conv, corr], axis=1))
+    conv, corr = back[:, : rows + PAD_ROWS], back[:, rows + PAD_ROWS :]
+    mixed, squares = mix(streams, before, short_taps, bias, conv)
+    squares = lax.psum(squares, "ch")
+    channels = width * lax.axis_size("ch")
+    return tuple(
+        finish(
+            channels, streams, before, after, short_taps, bias, gain, cotangent, mixed, squares, conv, corr
+        )
+    )
+
 
 EXACTNESS = lax.Precision.HIGHEST
 
@@ -28,7 +491,7 @@
     return passed_along(edge_rows, "seq", offset)
 
 
-def swap_blocks(blocks):
+def swap_middle(blocks):
     return lax.all_to_all(blocks, "seq", split_axis=1, concat_axis=0, tiled=True)
 
 
@@ -38,7 +501,7 @@
     position = lax.axis_index("seq")
     sub_rows = length // devices
     period = 2 * length * devices
-    gathered = swap_blocks(series.reshape(1, length, series_count, chan_width))
+    gathered = swap_middle(series.reshape(1, length, series_count, chan_width))
     cos_a, sin_a = angle_pair(counting(2 * devices), counting(devices), 2 * devices, -1.0)
     real_part = jnp.einsum("ka,absc->bksc", cos_a, gathered, precision=EXACTNESS)
     imag_part = jnp.einsum("ka,absc->bksc", sin_a, gathered, precision=EXACTNESS)
@@ -50,7 +513,7 @@
         [real_part * turn_cos - imag_part * turn_sin, real_part * turn_sin + imag_part * turn_cos],
         axis=2,
     )
-    swapped = swap_blocks(turned)
+    swapped = swap_middle(turned)
     cos_b, sin_b = angle_pair(counting(length), counting(length), length, -1.0)
     primary = jnp.einsum("jb,bksc->jksc", cos_b, swapped, precision=EXACTNESS)
     second = jnp.einsum("jb,bksc->jksc", sin_b, swapped, precision=EXACTNESS)
@@ -77,7 +540,7 @@
         ],
         axis=2,
     )
-    swapped = swap_blocks(turned)
+    swapped = swap_middle(turned)
     spike_locations = position * sub_rows + counting(sub_rows)
     turn_cos, turn_sin = angle_pair(counting(2 * devices), spike_locations, period, 1.0)
     turn_cos = turn_cos[:, :, None, None]
@@ -90,11 +553,11 @@
     result = jnp.einsum("ak,kbsc->basc", cos_a, rotated_re, precision=EXACTNESS) - jnp.einsum(
         "ak,kbsc->basc", sin_a, rotated_im, precision=EXACTNESS
     )
-    returned = swap_blocks(result / period)
+    returned = swap_middle(result / period)
     return returned.reshape(length, -1, chan_width)
 
 
-def local(streams, short_taps, long_filter, skip_bias, norm_gain, cotangent):
+def local_general(streams, short_taps, long_filter, skip_bias, norm_gain, cotangent):
     row_count = streams.shape[1]
     chan_width = streams.shape[2]
     rim_rows = short_taps.shape[1] - 1
@@ -154,10 +617,17 @@
         P("ch"),
         P("seq", "ch"),
     )
-    return jax.shard_map(
-        local,
-        mesh=mesh,
-        in_specs=placed,
-        out_specs=(P("seq", "ch"), P(None, "seq", "ch")),
-        check_vma=False,
-    )
+
+    def program(streams, short_taps, long_filter, skip_bias, norm_gain, cotangent):
+        parts = mesh.shape["seq"]
+        width = cotangent.shape[1] // mesh.shape["ch"]
+        lanes_filled = width % (128 * parts) == 0 and parts % 4 == 0 and parts <= 16
+        return jax.shard_map(
+            local if lanes_filled else local_general,
+            mesh=mesh,
+            in_specs=placed,
+            out_specs=(P("seq", "ch"), P(None, "seq", "ch")),
+            check_vma=False,
+        )(streams, short_taps, long_filter, skip_bias, norm_gain, cotangent)
+
+    return program

time: 407 us -> 107 us (0.26)
  blocking collectives: 272 us -> 48 us
  matrix products: 41.3 us -> 0 us
  local copies, waits for them, and re-layouts: 21.5 us -> 4.45 us
  Pallas kernels: 0 us -> 15.4 us
  waiting for transfers between devices: 39.4 us -> 25.3 us
  other arithmetic: 16 us -> 2.12 us
    all_to_all x3 -> x1, blocking collectives: 267 us -> 42.3 us  [swap_blocks(): lax.all_to_all(blocks, 'seq', split_axis=0, concat_axis=0, tiled=True)]
    dot_general x8 -> x0, matrix products: 41.3 us -> none  [the longest x1 7.28 us: spread_inverse(): primary = jnp.einsum('bj,jksc->kbsc', cos_b, merged, precision=EXACTNESS)]
    pallas_call x0 -> x6, Pallas kernels: none -> 15.4 us  [the longest x2 8.99 us: through_filter(): pl.pallas_call(functools.partial(product_kernel, conjugate), out_shape=ja...]
    all_to_all x1, waiting for transfers between devices: 35.8 us -> 25.3 us  [swap_blocks(): lax.all_to_all(blocks, 'seq', split_axis=0, concat_axis=0, tiled=True)]
    concatenate x2 -> x0, local copies, waits for them, and re-layouts: 9.55 us -> none  [the longest x1 5.5 us: spread_inverse(): jnp.concatenate([primary[:, :, :series_count] - second[:, :, series_count...]
    sub x4 -> x0, other arithmetic: 7.48 us -> none  [the longest x1 3.44 us: spread_forward(): primary[:, :, :series_count] - second[:, :, series_count:]]
    all_to_all x5 -> x0, local copies, waits for them, and re-layouts: 4.79 us -> none  [swap_blocks(): lax.all_to_all(blocks, 'seq', split_axis=1, concat_axis=0, tiled=True)]
  transfers between devices with their start and end apart: 3 -> 3, of which waited for: 2 -> 2; matrix products, arithmetic and copies ran while one was open for 1% -> 3% of each run, Pallas kernels for 0% -> 2%
where the time goes in v1:
time: 107 us; the launch traced here: 106 us
  blocking collectives  48 us (45%)
  waiting for transfers between devices  25.3 us (24%)
  Pallas kernels  15.4 us (14%)
  starting transfers between devices  10.4 us (10%)
  local copies, waits for them, and re-layouts  4.45 us (4%)
  other arithmetic  2.12 us (2%)
    all_to_all x1, blocking collectives, swap_blocks(): lax.all_to_all(blocks, 'seq', split_axis=0, concat_axis=0, tiled=True)  42.3 us
    all_to_all x1, waiting for transfers between devices, swap_blocks(): lax.all_to_all(blocks, 'seq', split_axis=0, concat_axis=0, tiled=True)  25.3 us
    pallas_call x2, Pallas kernels, through_filter(): pl.pallas_call(functools.partial(product_kernel, conjugate), out_shape=ja...  8.99 us
    ppermute x2, starting transfers between devices, shift_along(): return lax.ppermute(block, axis, route)  6.16 us
    psum x1, blocking collectives, local(): squares = lax.psum(squares, 'ch')  5.67 us
    all_to_all x1, starting transfers between devices, swap_blocks(): lax.all_to_all(blocks, 'seq', split_axis=0, concat_axis=0, tiled=True)  4.26 us
    pallas_call x1, Pallas kernels, finish(): pl.pallas_call(functools.partial(finish_kernel, float(channels)), grid=(s...  2.81 us
    unnamed x17, local copies, waits for them, and re-layouts  2.8 us
  transfers between devices with their start and end apart: 3, of which 2 were waited for; matrix products, arithmetic and copies ran while one was open for 3% of the time, Pallas kernels for 2%

profile of v1, /device:TPU:0, one launch (start us, length us, event | category | flops | bytes accessed | tf_op | source)
XLA Modules:
  0.0 106.5 jit_solution(7929721583541696172)
XLA Ops:
  0.6 0.0 copy-start.2
  0.6 0.0 copy-start.5
  0.6 0.0 copy-start.4
  0.7 0.9 fusion.2
  1.6 4.9 %collective-permute-start = (f32[3,2,1024]{2,1,0:T(2,128)S(1)}, f32[3,2,1024]{2,1,0:T(2,128)S(1)}, u32[]{:S(2)}, u32[]{:S(2)}) collective-permute-start(f32[3,2,1024]{2,1,0:T(2,128)S(1)} %get-tuple-element.16), channel_id=1, source_target_pairs={{0,4},{4,8},{8,12},{12,16},{16,20},{20,24},{24,28},{1,5},{5,9},{9,... | collective-permute-start | bytes 73736 | tf_op jit(solution)/shard_map/ppermute | solution.py:21
  6.5 1.2 %copy.12 = f32[128,1024]{0,1:T(8,128)S(1)} copy(f32[128,1024]{1,0:T(8,128)} %param.12) | data formatting | bytes 1048576 | tf_op args[2]
  7.7 0.2 copy.13
  7.9 0.1 collective-permute-done.before_ref
  8.0 0.0 copy-done.2
  8.0 0.0 copy-done.5
  8.0 0.0 copy-done.4
  8.0 0.8 short_filters.1
  8.8 0.1 pad_maximum_fusion
  8.9 42.3 %all_to_all.10 = f32[8,384,128]{2,1,0:T(8,128)S(1)} all-to-all(f32[8,384,128]{2,1,0:T(8,128)S(1)} %pad_maximum_fusion), channel_id=1, replica_groups=mesh['seq'=8,'ch'=4] {'seq'}, dimensions={0} | all-to-all | bytes 3145728 | tf_op jit(solution)/shard_map/all_to_all | solution.py:436
  51.2 0.0 copy-start
  51.2 0.0 copy-start.1
  51.2 0.1 fusion
  51.4 1.1 %copy-done = bf16[8,256,256]{2,1,0:T(8,128)(2,1)S(1)} copy-done((bf16[8,256,256]{2,1,0:T(8,128)(2,1)S(1)}, bf16[8,256,256]{2,1,0:T(8,128)(2,1)}, u32[]{:S(2)}) %copy-start) | copy-done | bytes 1048600
  52.4 0.3 copy-done.1
  52.8 0.0 copy-start.3
  52.8 1.1 filter_spectrum.1.spec_ref
  53.8 0.2 copy-done.3
  54.0 4.5 %convolution.1 = f32[8,136,128]{2,1,0:T(8,128)S(1)} custom-call(f32[8,128,128]{2,1,0:T(8,128)S(1)} %get-tuple-element.10.x_ref, f32[8,256,128]{2,1,0:T(8,128)S(1)} %filter_spectrum.1.spec_ref, bf16[8,256,256]{2,1,0:T(8,128)(2,1)S(1)} %copy-done, bf16[8,256,256]{2,1,0:T(8,128)(2,1)S(1)} %copy-done.1, bf16[8,256,256]{2,1,0:T(8,128)(2,1)S(1)} %copy-done.3, ...), custom_call_target="tpu_custom_call" | custom-call | tf_op jit(solution)/shard_map/convolution/pallas_call | solution.py:208
  58.5 4.5 %correlation.1 = f32[8,136,128]{2,1,0:T(8,128)S(1)} custom-call(f32[8,128,128]{2,1,0:T(8,128)S(1)} %get-tuple-element.11.x_ref, f32[8,256,128]{2,1,0:T(8,128)S(1)} %filter_spectrum.1.spec_ref, bf16[8,256,256]{2,1,0:T(8,128)(2,1)S(1)} %copy-done, bf16[8,256,256]{2,1,0:T(8,128)(2,1)S(1)} %copy-done.1, bf16[8,256,256]{2,1,0:T(8,128)(2,1)S(1)} %copy-done.3, ...), custom_call_target="tpu_custom_call" | custom-call | tf_op jit(solution)/shard_map/correlation/pallas_call | solution.py:208
  63.0 1.1 %pad_maximum_fusion.1 = f32[8,272,128]{2,1,0:T(8,128)} fusion(f32[8,136,128]{2,1,0:T(8,128)S(1)} %correlation.1, f32[8,136,128]{2,1,0:T(8,128)S(1)} %convolution.1), kind=kLoop, calls=%fused_computation.1 | loop fusion | flops 278528 | bytes 2228224 | tf_op jit(solution)/shard_map/concatenate | solution.py:459
  64.1 4.3 %all-to-all-start.1 = ((f32[8,272,128]{2,1,0:T(8,128)}), f32[8,272,128]{2,1,0:T(8,128)}, u32[]{:S(2)}, u32[]{:S(2)}) async-start(f32[8,272,128]{2,1,0:T(8,128)} %pad_maximum_fusion.1), calls=%async_computation.1 | async-start | bytes 2228224 | tf_op jit(solution)/shard_map/all_to_all | solution.py:436
  68.3 0.0 copy-start.6
  68.4 0.0 copy-start.7
  68.4 1.3 %collective-permute-start.1 = (f32[4,2,1024]{2,1,0:T(2,128)S(1)}, f32[4,2,1024]{2,1,0:T(2,128)S(1)}, u32[]{:S(2)}, u32[]{:S(2)}) collective-permute-start(f32[4,2,1024]{2,1,0:T(2,128)S(1)} %maximum_convert_fusion), channel_id=1, source_target_pairs={{4,0},{8,4},{12,8},{16,12},{20,16},{24,20},{28,24},{5,1},{9,5},{13... | collective-permute-start | bytes 98312 | tf_op jit(solution)/shard_map/ppermute | solution.py:21
  69.7 25.3 %all-to-all-done.1 = f32[8,272,128]{2,1,0:T(8,128)} async-done(((f32[8,272,128]{2,1,0:T(8,128)}), f32[8,272,128]{2,1,0:T(8,128)}, u32[]{:S(2)}, u32[]{:S(2)}) %all-to-all-start.1) | async-done | bytes 1114144 | tf_op jit(solution)/shard_map/all_to_all | solution.py:436
  95.0 1.3 %fusion.1 = (f32[8,136,128]{2,1,0:T(8,128)S(1)}, f32[8,136,128]{2,1,0:T(8,128)S(1)}) fusion(f32[8,272,128]{2,1,0:T(8,128)} %all-to-all-done.1), kind=kLoop, calls=%fused_computation.6 | loop fusion | bytes 2228224 | tf_op jit(solution)/shard_map/slice | solution.py:460
  96.3 0.0 copy-done.6
  96.3 1.7 %mixed_squares.1 = (f32[128,1024]{1,0:T(8,128)S(1)}, f32[1,128]{1,0:T(1,128)S(1)}) custom-call(bf16[3,128,1024]{2,1,0:T(8,128)(2,1)S(1)} %copy-done.2, f32[3,2,1024]{2,1,0:T(2,128)S(1)} %collective-permute-done.before_ref, f32[3,3,1024]{2,1,0:T(4,128)S(1)} %copy-done.5, f32[1,1024]{1,0:T(1,128)S(1)} %bitcast.6, f32[8,136,128]{2,1,0:T(8,128)S(1)} %get-tuple-element.14.conv_ref), custom_call_target="tpu_custom_call" | custom-call | tf_op jit(solution)/shard_map/mixed_squares/pallas_call | solution.py:339
  98.0 5.7 %psum.7.square_ref = f32[1,128]{1,0:T(1,128)S(1)} all-reduce(f32[1,128]{1,0:T(1,128)S(1)} %get-tuple-element.9), channel_id=1, replica_groups=mesh['seq'=8,'ch'=4] {'ch'}, use_global_device_ids=true, to_apply=%region_0.0 | all-reduce | flops 128 | bytes 1024 | tf_op jit(solution)/shard_map/psum | solution.py:462
  103.7 0.0 collective-permute-done.1.after_ref
  103.7 0.0 copy-done.7
  103.7 2.8 %norm_and_grads.1 = (bf16[128,1024]{1,0:T(8,128)(2,1)}, bf16[3,128,1024]{2,1,0:T(8,128)(2,1)}) custom-call(bf16[3,128,1024]{2,1,0:T(8,128)(2,1)S(1)} %copy-done.2, f32[3,2,1024]{2,1,0:T(2,128)S(1)} %collective-permute-done.before_ref, f32[4,2,1024]{2,1,0:T(2,128)S(1)} %collective-permute-done.1.after_ref, f32[3,3,1024]{2,1,0:T(4,128)S(1)} %copy-done.5, ...), custom_call_target="tpu_custom_call" | custom-call | tf_op jit(solution)/shard_map/norm_and_grads/pallas_call | solution.py:409
  (2 shorter events, 0.0 us)
Async XLA Ops:
  0.6 7.3 %copy-start.2 = (bf16[3,128,1024]{2,1,0:T(8,128)(2,1)S(1)}, bf16[3,128,1024]{2,1,0:T(8,128)(2,1)}, u32[]{:S(2)}) copy-start(bf16[3,128,1024]{2,1,0:T(8,128)(2,1)} %streams_ref.5) | copy-start | bytes 2359300
  0.6 7.3 %copy-start.5 = (f32[3,3,1024]{2,1,0:T(4,128)S(1)}, f32[3,3,1024]{2,1,0:T(4,128)}, u32[]{:S(2)}) copy-start(f32[3,3,1024]{2,1,0:T(4,128)} %taps_ref.5) | copy-start | bytes 110596
  0.6 7.3 %copy-start.4 = (bf16[128,1024]{1,0:T(8,128)(2,1)S(1)}, bf16[128,1024]{1,0:T(8,128)(2,1)}, u32[]{:S(2)}) copy-start(bf16[128,1024]{1,0:T(8,128)(2,1)} %cot_ref.3) | copy-start | bytes 786436
  1.6 6.4 %collective-permute-start = (f32[3,2,1024]{2,1,0:T(2,128)S(1)}, f32[3,2,1024]{2,1,0:T(2,128)S(1)}, u32[]{:S(2)}, u32[]{:S(2)}) collective-permute-start(f32[3,2,1024]{2,1,0:T(2,128)S(1)} %get-tuple-element.16), channel_id=1, source_target_pairs={{0,4},{4,8},{8,12},{12,16},{16,20},{20,24},{24,28},{1,5},{5,9},{9,... | collective-permute-start | bytes 73736 | tf_op jit(solution)/shard_map/ppermute | solution.py:21
  51.2 1.2 %copy-start = (bf16[8,256,256]{2,1,0:T(8,128)(2,1)S(1)}, bf16[8,256,256]{2,1,0:T(8,128)(2,1)}, u32[]{:S(2)}) copy-start(bf16[8,256,256]{2,1,0:T(8,128)(2,1)} %constant.8.clone.gh_ref) | copy-start | bytes 3145732
  51.2 1.5 %copy-start.1 = (bf16[8,256,256]{2,1,0:T(8,128)(2,1)S(1)}, bf16[8,256,256]{2,1,0:T(8,128)(2,1)}, u32[]{:S(2)}) copy-start(bf16[8,256,256]{2,1,0:T(8,128)(2,1)} %constant.9.clone.gl_ref) | copy-start | bytes 3145732
  52.8 1.2 %copy-start.3 = (bf16[8,256,256]{2,1,0:T(8,128)(2,1)S(1)}, bf16[8,256,256]{2,1,0:T(8,128)(2,1)}, u32[]{:S(2)}) copy-start(bf16[8,256,256]{2,1,0:T(8,128)(2,1)} %constant.10.clone.th_ref) | copy-start | bytes 3145732
  64.1 30.9 %all-to-all-start.1 = ((f32[8,272,128]{2,1,0:T(8,128)}), f32[8,272,128]{2,1,0:T(8,128)}, u32[]{:S(2)}, u32[]{:S(2)}) async-start(f32[8,272,128]{2,1,0:T(8,128)} %pad_maximum_fusion.1), calls=%async_computation.1 | async-start | bytes 2228224 | tf_op jit(solution)/shard_map/all_to_all | solution.py:436
  68.3 28.0 %copy-start.6 = (f32[1024]{0:T(1024)S(1)}, f32[1024]{0:T(1024)}, u32[]{:S(2)}) copy-start(f32[1024]{0:T(1024)} %param.13) | copy-start | bytes 12292
  68.4 35.3 %copy-start.7 = (f32[1024]{0:T(1024)S(1)}, f32[1024]{0:T(1024)}, u32[]{:S(2)}) copy-start(f32[1024]{0:T(1024)} %param.14) | copy-start | bytes 12292
  68.4 35.3 %collective-permute-start.1 = (f32[4,2,1024]{2,1,0:T(2,128)S(1)}, f32[4,2,1024]{2,1,0:T(2,128)S(1)}, u32[]{:S(2)}, u32[]{:S(2)}) collective-permute-start(f32[4,2,1024]{2,1,0:T(2,128)S(1)} %maximum_convert_fusion), channel_id=1, source_target_pairs={{4,0},{8,4},{12,8},{16,12},{20,16},{24,20},{28,24},{5,1},{9,5},{13... | collective-permute-start | bytes 98312 | tf_op jit(solution)/shard_map/ppermute | solution.py:21

commit v2 on v0

--- a/solution.py
+++ b/solution.py
@@ -1,9 +1,581 @@
+import functools
 import math
 
 import jax
 import jax.numpy as jnp
+import numpy as np
 from jax import lax
+from jax.experimental import pallas as pl
+from jax.experimental.pallas import tpu as pltpu
 from jax.sharding import PartitionSpec as P
+
+F32 = jnp.float32
+BF16 = jnp.bfloat16
+PAD_ROWS = 8
+VMEM_BYTES = 48 * 1024 * 1024
+
+
+def shift_along(block, axis, distance):
+    devices = range(lax.axis_size(axis))
+    route = [(i - distance, i) for i in devices if i - distance in devices]
+    return lax.ppermute(block, axis, route)
+
+
+def measured(microseconds):
+    return pl.CostEstimate(flops=0, bytes_accessed=int(microseconds * 73800.0), transcendentals=0)
+
+
+def params():
+    return pltpu.CompilerParams(vmem_limit_bytes=VMEM_BYTES)
+
+
+def scaled(value, factor):
+    if abs(factor) < 1e-12:
+        return None
+    if abs(factor - 1.0) < 1e-12:
+        return value
+    if abs(factor + 1.0) < 1e-12:
+        return -value
+    return value * factor
+
+
+def total(terms):
+    kept = [term for term in terms if term is not None]
+    if not kept:
+        return None
+    result = kept[0]
+    for term in kept[1:]:
+        result = result + term
+    return result
+
+
+def plus(left, right):
+    return total([left, right])
+
+
+def minus(left, right):
+    return total([left, None if right is None else -right])
+
+
+def sending_place(apart, blocks, by_side):
+    return (apart % 2) * (blocks // 2) + apart // 2 if by_side else apart
+
+
+def dot(left, right):
+    return lax.dot_general(left, right, (((1,), (0,)), ((), ())), preferred_element_type=F32)
+
+
+def stage_tables(blocks, rows):
+    period = 2 * blocks * rows
+    place = np.arange(rows)
+    turn = 2.0 * np.pi * ((place[:, None] * place[None, :]) % rows) / rows
+    exact = np.concatenate([np.cos(turn), np.sin(turn)], axis=0)
+    high = exact.astype(BF16)
+    low = (exact - high.astype(np.float64)).astype(BF16)
+    columns = -(-2 * (blocks + 1) // 128) * 128
+    twiddles = np.zeros((rows, columns), np.float32)
+    for k in range(blocks + 1):
+        turn = 2.0 * np.pi * ((place * k) % period) / period
+        twiddles[:, 2 * k], twiddles[:, 2 * k + 1] = np.cos(turn), np.sin(turn)
+    return np.concatenate([high, high], axis=1), low, twiddles
+
+
+def turned(twiddles, k, re, im, sign):
+    if k == 0:
+        return re, im
+    cos = jnp.broadcast_to(twiddles[:, 2 * k : 2 * k + 1], re.shape)
+    sin = jnp.broadcast_to(twiddles[:, 2 * k + 1 : 2 * k + 2], re.shape) * sign
+    if im is None:
+        return re * cos, re * sin
+    return re * cos - im * sin, re * sin + im * cos
+
+
+def store_split(split_ref, k, here, re, im):
+    rows, width = split_ref.shape[1] // 2, split_ref.shape[2] // 2
+    for value, lanes in ((re, slice(0, width)), (im, slice(width, 2 * width))):
+        if value is None:
+            value = jnp.zeros_like(re)
+        high = value.astype(BF16)
+        split_ref[k, here, lanes] = high
+        split_ref[k, slice(rows + here.start, rows + here.stop), lanes] = (value - high.astype(F32)).astype(BF16)
+
+
+def first_stage(own, x_ref, tw_ref, split_ref, tile):
+    blocks, rows = x_ref.shape[0], x_ref.shape[1]
+    for start in range(0, rows, tile):
+        here = slice(start, start + tile)
+        twiddles = tw_ref[here, :]
+        x = [x_ref[a ^ own, here, :] for a in range(blocks)]
+
+        def keep(k, re, im):
+            store_split(split_ref, k, here, *turned(twiddles, k, re, im, -1.0))
+
+        for k in range(blocks // 2 + 1):
+            parts = []
+            for parity in (0, 1):
+                members = range(parity, blocks, 2)
+                turn = [math.pi * ((a * k) % (2 * blocks)) / blocks for a in members]
+                parts.append(total([scaled(x[a], math.cos(t)) for a, t in zip(members, turn)]))
+                parts.append(total([scaled(x[a], math.sin(t)) for a, t in zip(members, turn)]))
+            even_c, even_s, odd_c, odd_s = parts
+            keep(k, plus(even_c, odd_c), None if k == 0 else -plus(even_s, odd_s))
+            if 2 * k != blocks:
+                keep(blocks - k, minus(even_c, odd_c), None if k == 0 else minus(even_s, odd_s))
+
+
+def second_stage(table_high, table_low, split):
+    rows, width = table_low.shape[1], split.shape[1] // 2
+    sums = dot(table_high, split) + dot(table_low, split[:rows])
+    return sums[:rows, :width], sums[:rows, width:], sums[rows:, :width], sums[rows:, width:]
+
+
+def spectrum_kernel(own_ref, x_ref, high_ref, low_ref, tw_ref, _, spec_ref, split_ref):
+    blocks, rows = x_ref.shape[0], x_ref.shape[1]
+    first_stage(own_ref[0], x_ref, tw_ref, split_ref, 32)
+    for k in range(blocks + 1):
+        scale = (0.5 if k in (0, blocks) else 1.0) / (blocks * rows)
+        cos_re, cos_im, sin_re, sin_im = second_stage(high_ref[...], low_ref[...], split_ref[k])
+        spec_ref[k, :rows, :] = (cos_re + sin_im) * scale
+        spec_ref[k, rows:, :] = (cos_im - sin_re) * scale
+
+
+def last_stage(own, by_side, re_ref, im_ref, out_ref, tile):
+    blocks, rows = re_ref.shape[0] - 1, re_ref.shape[1]
+    for start in range(0, rows, tile):
+        here = slice(start, start + tile)
+        re = [re_ref[k, here, :] for k in range(blocks + 1)]
+        im = {k: im_ref[k, here, :] for k in range(1, blocks)}
+        for parity in (0, 1):
+            sign = 1.0 - 2.0 * parity
+            base = re[0] + sign * re[blocks]
+            re_sum = {k: re[k] + sign * re[blocks - k] for k in range(1, blocks // 2)}
+            im_sum = {k: im[k] - sign * im[blocks - k] for k in range(1, blocks // 2)}
+            re_sum[blocks // 2] = re[blocks // 2]
+            im_sum[blocks // 2] = im[blocks // 2]
+            for a in range(parity, blocks, 2):
+                terms = [base]
+                for k in range(1, blocks // 2 + 1):
+                    turn = math.pi * ((a * k) % (2 * blocks)) / blocks
+                    terms.append(scaled(re_sum[k], math.cos(turn)))
+                    terms.append(scaled(im_sum[k], -math.sin(turn)))
+                value = total(terms)
+                out_ref[sending_place(a ^ own, blocks, by_side), here, :] = value
+                if start == 0 and a > 0:
+                    place = sending_place((a - 1) ^ own, blocks, by_side)
+                    out_ref[place, rows : rows + PAD_ROWS, :] = value[:PAD_ROWS]
+    place = sending_place((blocks - 1) ^ own, blocks, by_side)
+    out_ref[place, rows : rows + PAD_ROWS, :] = jnp.zeros((PAD_ROWS, out_ref.shape[2]), F32)
+
+
+def product_kernel(
+    conjugate, by_side, own_ref, x_ref, spec_ref, high_ref, low_ref, tw_ref, out_ref, split_ref, re_ref, im_ref
+):
+    blocks, rows = x_ref.shape[0], x_ref.shape[1]
+    first_stage(own_ref[0], x_ref, tw_ref, split_ref, 32)
+    sign = -1.0 if conjugate else 1.0
+    tile = 32
+    for k in range(blocks + 1):
+        cos_re, cos_im, sin_re, sin_im = second_stage(high_ref[...], low_ref[...], split_ref[k])
+        re_ref[k] = cos_re + sin_im
+        im_ref[k] = cos_im - sin_re
+    for k in range(blocks + 1):
+        for start in range(0, rows, tile):
+            here = slice(start, start + tile)
+            x_re, x_im = re_ref[k, here, :], im_ref[k, here, :]
+            h_re, h_im = spec_ref[k, here, :], spec_ref[k, rows + start : rows + start + tile, :] * sign
+            store_split(split_ref, k, here, x_re * h_re - x_im * h_im, x_im * h_re + x_re * h_im)
+    for k in range(blocks + 1):
+        cos_re, cos_im, sin_re, sin_im = second_stage(high_ref[...], low_ref[...], split_ref[k])
+        re, im = turned(tw_ref[...], k, cos_re - sin_im, cos_im + sin_re, 1.0)
+        re_ref[k] = re
+        im_ref[k] = im
+    last_stage(own_ref[0], by_side, re_ref, im_ref, out_ref, tile)
+
+
+def whole_operands(count):
+    return [pl.BlockSpec(memory_space=pltpu.SMEM)] + [pl.BlockSpec(memory_space=pltpu.VMEM)] * count
+
+
+def split_scratch(blocks, rows, width):
+    return pltpu.VMEM((blocks + 1, 2 * rows, 2 * width), BF16)
+
+
+def spectrum(own, x, tables, unread):
+    blocks, rows, width = x.shape
+    return pl.pallas_call(
+        spectrum_kernel,
+        out_shape=jax.ShapeDtypeStruct((blocks + 1, 2 * rows, width), F32),
+        in_specs=whole_operands(4) + [pl.BlockSpec(memory_space=pl.ANY)],
+        scratch_shapes=[split_scratch(blocks, rows, width)],
+        compiler_params=params(),
+        cost_estimate=measured(1.1),
+        name="filter_spectrum",
+    )(own, x, *tables, unread)
+
+
+def through_filter(own, x, spec, tables, conjugate, by_side):
+    blocks, rows, width = x.shape
+    part = pltpu.VMEM((blocks + 1, rows, width), F32)
+    return pl.pallas_call(
+        functools.partial(product_kernel, conjugate, by_side),
+        out_shape=jax.ShapeDtypeStruct((blocks, rows + PAD_ROWS, width), F32),
+        in_specs=whole_operands(5),
+        scratch_shapes=[split_scratch(blocks, rows, width), part, part],
+        compiler_params=params(),
+        cost_estimate=measured(2.5),
+        name="correlation" if conjugate else "convolution",
+    )(own, x, spec, *tables)
+
+
+def row_number(shape):
+    return lax.broadcasted_iota(jnp.int32, shape, 0)
+
+
+def delayed(x, before, distance):
+    moved = pltpu.roll(x, distance, 0)
+    rows = row_number(x.shape)
+    rim = len(before)
+    for row in range(distance):
+        moved = jnp.where(rows == row, before[rim - distance + row], moved)
+    return moved
+
+
+def advanced(x, after, distance):
+    count = x.shape[0]
+    moved = pltpu.roll(x, count - distance, 0)
+    rows = row_number(x.shape)
+    for row in range(distance):
+        moved = jnp.where(rows == count - distance + row, after[row], moved)
+    return moved
+
+
+def rows_of(block):
+    return [block[row : row + 1] for row in range(block.shape[0])]
+
+
+def short_filter_after(after, last, taps):
+    known = last + after
+    return [
+        total([taps[j : j + 1] * known[len(last) + row - j] for j in range(taps.shape[0])])
+        for row in range(len(after))
+    ]
+
+
+def short_filter(x, before, taps):
+    result = taps[0:1] * x
+    for j in range(1, taps.shape[0]):
+        result = result + taps[j : j + 1] * delayed(x, before, j)
+    return result
+
+
+def short_transpose(x, after, taps):
+    result = taps[0:1] * x
+    for j in range(1, taps.shape[0]):
+        result = result + taps[j : j + 1] * advanced(x, after, j)
+    return result
+
+
+def place_of_part(own_ref, part):
+    return part ^ (own_ref[0] % 2)
+
+
+def pair_specs(rows, pair, rim, count):
+    def at(j, own):
+        return j ^ (own[0] // 2)
+
+    return {
+        "streams": pl.BlockSpec((3, rows, pair), lambda j, own: (0, 0, at(j, own))),
+        "before": pl.BlockSpec((3, rim, pair), lambda j, own: (0, 0, at(j, own))),
+        "after": pl.BlockSpec((4, rim, pair), lambda j, own: (0, 0, at(j, own))),
+        "taps": pl.BlockSpec((3, count, pair), lambda j, own: (0, 0, at(j, own))),
+        "vector": pl.BlockSpec((1, pair), lambda j, own: (0, at(j, own))),
+        "flat": pl.BlockSpec((rows, pair), lambda j, own: (0, at(j, own))),
+        "row": pl.BlockSpec((1, rows), lambda j, own: (0, 0)),
+        "chunk": pl.BlockSpec((1, 2, rows + PAD_ROWS, pair // 2), lambda j, own: (j, 0, 0, 0)),
+        "by_pair": pl.BlockSpec((1, 2, rows, pair // 2), lambda j, own: (j, 0, 0, 0)),
+        "by_side": pl.BlockSpec((2, 1, rows, pair // 2), lambda j, own: (0, j, 0, 0)),
+    }
+
+
+def over_pairs(kernel, own, parts, specs, ins, outs, out_shape, operands, name, microseconds):
+    return pl.pallas_call(
+        kernel,
+        grid_spec=pltpu.PrefetchScalarGridSpec(
+            num_scalar_prefetch=1,
+            grid=(parts // 2,),
+            in_specs=[specs[i] for i in ins],
+            out_specs=[specs[o] for o in outs],
+        ),
+        out_shape=out_shape,
+        compiler_params=params(),
+        cost_estimate=measured(microseconds),
+        name=name,
+    )(own, *operands)
+
+
+def lanes_of(part, block):
+    return slice(part * block, (part + 1) * block)
+
+
+def arrange_kernel(own_ref, x_ref, out_ref):
+    block = out_ref.shape[3]
+    for part in range(2):
+        out_ref[0, place_of_part(own_ref, part)] = x_ref[:, lanes_of(part, block)]
+
+
+def arrange(own, x, parts, specs):
+    rows, width = x.shape
+    out = jax.ShapeDtypeStruct((parts // 2, 2, rows, width // parts), F32)
+    return over_pairs(arrange_kernel, own, parts, specs, ["flat"], ["by_pair"], [out], [x], "filter_blocks", 0.3)[0]
+
+
+def shorts_of(streams_ref, before_ref, taps_ref, lanes):
+    return [
+        short_filter(streams_ref[i, :, lanes].astype(F32), rows_of(before_ref[i, :, lanes]), taps_ref[i, :, lanes])
+        for i in range(3)
+    ]
+
+
+def gate_kernel(own_ref, streams_ref, before_ref, taps_ref, cot_ref, gated_ref, carried_ref):
+    block = gated_ref.shape[3]
+    for part in range(2):
+        lanes = lanes_of(part, block)
+        place = place_of_part(own_ref, part)
+        short = shorts_of(streams_ref, before_ref, taps_ref, lanes)
+        gated_ref[place, 0] = short[1] * short[2]
+        carried_ref[place, 0] = cot_ref[:, lanes].astype(F32) * short[0]
+
+
+def gate(own, streams, before, taps, cotangent, parts, specs):
+    _, rows, width = streams.shape
+    block = width // parts
+    return over_pairs(
+        gate_kernel,
+        own,
+        parts,
+        specs,
+        ["streams", "before", "taps", "flat"],
+        ["by_side", "by_side"],
+        [
+            jax.ShapeDtypeStruct((2, parts // 2, rows, block), F32),
+            jax.ShapeDtypeStruct((2, parts // 2, rows, block), F32),
+        ],
+        [streams, before, taps, cotangent],
+        "short_filters",
+        1.2,
+    )
+
+
+def mix_kernel(
+    own_ref, streams_ref, before_ref, after_ref, taps_ref, bias_ref, cot_ref, conv_ref, mixed_ref, square_ref, grad_ref
+):
+    step = pl.program_id(0)
+    block = conv_ref.shape[3]
+    rows = streams_ref.shape[1]
+    rim = after_ref.shape[1]
+    squares = jnp.zeros((rows, block), F32)
+    for part in range(2):
+        lanes = lanes_of(part, block)
+        place = place_of_part(own_ref, part)
+        bias = bias_ref[:, lanes]
+        short = shorts_of(streams_ref, before_ref, taps_ref, lanes)
+        direct = conv_ref[0, place, :rows, :] + bias * (short[1] * short[2])
+        mixed = short[0] * direct
+        mixed_ref[:, lanes] = mixed
+        squares = squares + mixed * mixed
+        gated_after = [
+            short_filter_after(
+                rows_of(after_ref[i, :, lanes]),
+                rows_of(streams_ref[i, rows - rim :, lanes].astype(F32)),
+                taps_ref[i, :, lanes],
+            )
+            for i in (1, 2)
+        ]
+        conv_after = rows_of(conv_ref[0, place, rows : rows + rim, :])
+        cot_after = rows_of(after_ref[3, :, lanes])
+        above = [
+            cot_after[row] * (conv_after[row] + bias * (gated_after[0][row] * gated_after[1][row]))
+            for row in range(rim)
+        ]
+        grad = short_transpose(cot_ref[:, lanes].astype(F32) * direct, above, taps_ref[0, :, lanes])
+        grad_ref[:, lanes] = grad.astype(BF16)
+    row_sums = lax.dot_general(
+        jnp.ones((8, block), F32),
+        squares,
+        (((1,), (1,)), ((), ())),
+        precision=lax.Precision.HIGHEST,
+        preferred_element_type=F32,
+    )[0:1]
+
+    @pl.when(step == 0)
+    def _():
+        square_ref[...] = row_sums
+
+    @pl.when(step > 0)
+    def _():
+        square_ref[...] += row_sums
+
+
+def mix(own, streams, before, after, taps, bias, cotangent, conv, specs):
+    _, rows, width = streams.shape
+    return over_pairs(
+        mix_kernel,
+        own,
+        2 * conv.shape[0],
+        specs,
+        ["streams", "before", "after", "taps", "vector", "flat", "chunk"],
+        ["flat", "row", "flat"],
+        [
+            jax.ShapeDtypeStruct((rows, width), F32),
+            jax.ShapeDtypeStruct((1, rows), F32),
+            jax.ShapeDtypeStruct((rows, width), BF16),
+        ],
+        [streams, before, after, taps, bias, cotangent, conv],
+        "mixed_squares",
+        2.4,
+    )
+
+
+def norm_kernel(channels, mixed_ref, square_ref, gain_ref, normed_ref):
+    rows, width = mixed_ref.shape
+    squares = jnp.broadcast_to(square_ref[...], (128, rows)).T
+    scaling = lax.rsqrt(squares / channels + 1e-06)
+    for start in range(0, width, 128):
+        lanes = slice(start, start + 128)
+        normed_ref[:, lanes] = (mixed_ref[:, lanes] * scaling * gain_ref[:, lanes]).astype(BF16)
+
+
+def norm(channels, mixed, squares, gain):
+    rows, width = mixed.shape
+    return pl.pallas_call(
+        functools.partial(norm_kernel, float(channels)),
+        out_shape=jax.ShapeDtypeStruct((rows, width), BF16),
+        compiler_params=params(),
+        cost_estimate=measured(0.9),
+        name="norm",
+    )(mixed, squares, gain)
+
+
+def finish_kernel(
+    own_ref, streams_ref, before_ref, after_ref, taps_ref, bias_ref, cot_ref, grad_ref, corr_ref, grads_ref
+):
+    block = corr_ref.shape[3]
+    rows = streams_ref.shape[1]
+    rim = after_ref.shape[1]
+    grads_ref[0] = grad_ref[...]
+    for part in range(2):
+        lanes = lanes_of(part, block)
+        place = place_of_part(own_ref, part)
+        bias = bias_ref[:, lanes]
+        taps = [taps_ref[i, :, lanes] for i in range(3)]
+        short = shorts_of(streams_ref, before_ref, taps_ref, lanes)
+        gated_grad = corr_ref[0, place, :rows, :] + bias * (cot_ref[:, lanes].astype(F32) * short[0])
+        short_after = [
+            short_filter_after(
+                rows_of(after_ref[i, :, lanes]), rows_of(streams_ref[i, rows - rim :, lanes].astype(F32)), taps[i]
+            )
+            for i in range(3)
+        ]
+        corr_after = rows_of(corr_ref[0, place, rows : rows + rim, :])
+        cot_after = rows_of(after_ref[3, :, lanes])
+        grad_after = [corr_after[row] + bias * (cot_after[row] * short_after[0][row]) for row in range(rim)]
+        for i, other in ((1, 2), (2, 1)):
+            above = [grad_after[row] * short_after[other][row] for row in range(rim)]
+            grads_ref[i, :, lanes] = short_transpose(gated_grad * short[other], above, taps[i]).astype(BF16)
+
+
+def finish(own, streams, before, after, taps, bias, cotangent, grad, corr, specs):
+    return over_pairs(
+        finish_kernel,
+        own,
+        2 * corr.shape[0],
+        specs,
+        ["streams", "before", "after", "taps", "vector", "flat", "flat", "chunk"],
+        ["streams"],
+        [jax.ShapeDtypeStruct(streams.shape, BF16)],
+        [streams, before, after, taps, bias, cotangent, grad, corr],
+        "stream_grads",
+        2.6,
+    )[0]
+
+
+def swapped(block, apart, name):
+    route = [(i, i ^ apart) for i in range(lax.axis_size("seq"))]
+    with jax.named_scope(f"{name}_over_{apart}"):
+        return lax.ppermute(block, "seq", route)
+
+
+def tied(value, other):
+    return lax.optimization_barrier((value, other))
+
+
+def within_pairs(name, block):
+    return swapped(block, 1, name)
+
+
+def between_pairs(name, blocks):
+    return [blocks[0]] + [swapped(blocks[j], 2 * j, name) for j in range(1, len(blocks))]
+
+
+def sides_of(got):
+    return jnp.stack([block[0] for block in got]), jnp.stack([block[1] for block in got])
+
+
+def joined(kept, other):
+    return jnp.stack([kept, other], axis=1)
+
+
+def as_line(blocks):
+    return blocks.reshape((-1,) + blocks.shape[2:])
+
+
+def local(streams, short_taps, long_filter, skip_bias, norm_gain, cotangent):
+    parts = lax.axis_size("seq")
+    rows, width = cotangent.shape
+    rim = short_taps.shape[1] - 1
+    tables = stage_tables(parts, rows)
+    specs = pair_specs(rows, 2 * width // parts, rim, short_taps.shape[1])
+    own = lax.axis_index("seq").astype(jnp.int32)[None]
+    bias, gain = skip_bias[None], norm_gain[None]
+
+    filter_sent = arrange(own, long_filter, parts, specs)
+    filter_got = between_pairs("filter", filter_sent)
+    streams_later, filter_got[0] = tied(streams, filter_got[0])
+    before = shift_along(streams_later[:, rows - rim :].astype(F32), "seq", 1)
+    gated, carried = gate(own, streams, before, short_taps, cotangent, parts, specs)
+    edges = jnp.concatenate([streams_later[:, :rim].astype(F32), cotangent[None, :rim].astype(F32)], axis=0)
+    edges, filter_got[1] = tied(edges, filter_got[1])
+    after = shift_along(edges, "seq", -1)
+
+    gated_other = within_pairs("gated", gated[1])
+    carried_gone = carried[1]
+    gated_got = between_pairs("gated", joined(gated[0], gated_other))
+    filter_kept, filter_gone = sides_of(filter_got)
+    filter_other = within_pairs("filter", filter_gone)
+    filter_blocks = joined(filter_kept, filter_other)
+    carried_pairs = joined(carried[0], within_pairs("carried", carried_gone))
+    spec = spectrum(own, as_line(filter_blocks), tables, after)
+    carried_pairs, spec = tied(carried_pairs, spec)
+    carried_got = between_pairs("carried", carried_pairs)
+
+    shape = (rows + PAD_ROWS, width // parts)
+    gated_blocks = as_line(jnp.stack(gated_got))
+    conv_sent = through_filter(own, gated_blocks, spec, tables, False, True).reshape((2, parts // 2) + shape)
+    conv_pairs = joined(conv_sent[0], within_pairs("conv", conv_sent[1]))
+    carried_blocks = jnp.stack(carried_got)
+    conv_got = between_pairs("conv", conv_pairs)
+    corr_sent = through_filter(own, as_line(carried_blocks), spec, tables, True, True).reshape((2, parts // 2) + shape)
+    corr_pairs = joined(corr_sent[0], within_pairs("corr", corr_sent[1]))
+    corr_pairs, conv_got[2] = tied(corr_pairs, conv_got[2])
+    corr_got = between_pairs("corr", corr_pairs)
+    conv = jnp.stack(conv_got)
+    corr = jnp.stack(corr_got)
+    mixed, squares, grad = mix(own, streams, before, after, short_taps, bias, cotangent, conv, specs)
+    squares = lax.psum(squares, "ch")
+    normed = norm(width * lax.axis_size("ch"), mixed, squares, gain)
+    grads = finish(own, streams, before, after, short_taps, bias, cotangent, grad, corr, specs)
+    return normed, grads
+
 
 EXACTNESS = lax.Precision.HIGHEST
 
@@ -28,7 +600,7 @@
     return passed_along(edge_rows, "seq", offset)
 
 
-def swap_blocks(blocks):
+def swap_middle(blocks):
     return lax.all_to_all(blocks, "seq", split_axis=1, concat_axis=0, tiled=True)
 
 
@@ -38,7 +610,7 @@
     position = lax.axis_index("seq")
     sub_rows = length // devices
     period = 2 * length * devices
-    gathered = swap_blocks(series.reshape(1, length, series_count, chan_width))
+    gathered = swap_middle(series.reshape(1, length, series_count, chan_width))
     cos_a, sin_a = angle_pair(counting(2 * devices), counting(devices), 2 * devices, -1.0)
     real_part = jnp.einsum("ka,absc->bksc", cos_a, gathered, precision=EXACTNESS)
     imag_part = jnp.einsum("ka,absc->bksc", sin_a, gathered, precision=EXACTNESS)
@@ -50,7 +622,7 @@
         [real_part * turn_cos - imag_part * turn_sin, real_part * turn_sin + imag_part * turn_cos],
         axis=2,
     )
-    swapped = swap_blocks(turned)
+    swapped = swap_middle(turned)
     cos_b, sin_b = angle_pair(counting(length), counting(length), length, -1.0)
     primary = jnp.einsum("jb,bksc->jksc", cos_b, swapped, precision=EXACTNESS)
     second = jnp.einsum("jb,bksc->jksc", sin_b, swapped, precision=EXACTNESS)
@@ -77,7 +649,7 @@
         ],
         axis=2,
     )
-    swapped = swap_blocks(turned)
+    swapped = swap_middle(turned)
     spike_locations = position * sub_rows + counting(sub_rows)
     turn_cos, turn_sin = angle_pair(counting(2 * devices), spike_locations, period, 1.0)
     turn_cos = turn_cos[:, :, None, None]
@@ -90,11 +662,11 @@
     result = jnp.einsum("ak,kbsc->basc", cos_a, rotated_re, precision=EXACTNESS) - jnp.einsum(
         "ak,kbsc->basc", sin_a, rotated_im, precision=EXACTNESS
     )
-    returned = swap_blocks(result / period)
+    returned = swap_middle(result / period)
     return returned.reshape(length, -1, chan_width)
 
 
-def local(streams, short_taps, long_filter, skip_bias, norm_gain, cotangent):
+def local_general(streams, short_taps, long_filter, skip_bias, norm_gain, cotangent):
     row_count = streams.shape[1]
     chan_width = streams.shape[2]
     rim_rows = short_taps.shape[1] - 1
@@ -154,10 +726,17 @@
         P("ch"),
         P("seq", "ch"),
     )
-    return jax.shard_map(
-        local,
-        mesh=mesh,
-        in_specs=placed,
-        out_specs=(P("seq", "ch"), P(None, "seq", "ch")),
-        check_vma=False,
-    )
+
+    def program(streams, short_taps, long_filter, skip_bias, norm_gain, cotangent):
+        parts = mesh.shape["seq"]
+        width = cotangent.shape[1] // mesh.shape["ch"]
+        lanes_filled = width % (128 * parts) == 0 and parts in (4, 8, 16)
+        return jax.shard_map(
+            local if lanes_filled else local_general,
+            mesh=mesh,
+            in_specs=placed,
+            out_specs=(P("seq", "ch"), P(None, "seq", "ch")),
+            check_vma=False,
+        )(streams, short_taps, long_filter, skip_bias, norm_gain, cotangent)
+
+    return program

time: 407 us -> 84.4 us (0.21)
  blocking collectives: 272 us -> 5.67 us
  matrix products: 41.3 us -> 0 us
  starting transfers between devices: 12.1 us -> 36.7 us
  local copies, waits for them, and re-layouts: 21.5 us -> 1.51 us
  other arithmetic: 16 us -> 0.47 us
  waiting for transfers between devices: 39.4 us -> 26.4 us
  Pallas kernels: 0 us -> 12.4 us
    all_to_all x3 -> x0, blocking collectives: 267 us -> none  [swap_blocks(): lax.all_to_all(blocks, 'seq', split_axis=1, concat_axis=0, tiled=True)]
    dot_general x8 -> x0, matrix products: 41.3 us -> none  [the longest x1 7.28 us: spread_inverse(): primary = jnp.einsum('bj,jksc->kbsc', cos_b, merged, precision=EXACTNESS)]
    all_to_all x1 -> x0, waiting for transfers between devices: 35.8 us -> none  [swap_blocks(): lax.all_to_all(blocks, 'seq', split_axis=1, concat_axis=0, tiled=True)]
    ppermute x2 -> x22, starting transfers between devices: 6.16 us -> 36.7 us  [the longest x20 30.6 us: swapped(): return lax.ppermute(block, 'seq', route)]
    ppermute x2 -> x22, waiting for transfers between devices: 3.59 us -> 26.4 us  [the longest x20 26.4 us: swapped(): return lax.ppermute(block, 'seq', route)]
    pallas_call x0 -> x8, Pallas kernels: none -> 12.4 us  [the longest x4 6.5 us: over_pairs(): pl.pallas_call(kernel, grid_spec=pltpu.PrefetchScalarGridSpec(num_scalar_...]
    concatenate x2 -> x0, local copies, waits for them, and re-layouts: 9.55 us -> none  [the longest x1 5.5 us: spread_inverse(): jnp.concatenate([primary[:, :, :series_count] - second[:, :, series_count...]
    sub x4 -> x0, other arithmetic: 7.48 us -> none  [the longest x1 3.44 us: spread_forward(): primary[:, :, :series_count] - second[:, :, series_count:]]
  transfers between devices with their start and end apart: 3 -> 22, of which waited for: 2 -> 5; matrix products, arithmetic and copies ran while one was open for 1% -> 1% of each run, Pallas kernels for 0% -> 11%
where the time goes in v2:
time: 84.4 us; the launch traced here: 84.2 us
  starting transfers between devices  36.7 us (43%)
  waiting for transfers between devices  26.4 us (31%)
  Pallas kernels  12.4 us (15%)
  blocking collectives  5.67 us (7%)
  local copies, waits for them, and re-layouts  1.51 us (2%)
  between operations  1.02 us (1%)
    ppermute x20, starting transfers between devices, swapped(): return lax.ppermute(block, 'seq', route)  30.6 us
    ppermute x20, waiting for transfers between devices, swapped(): return lax.ppermute(block, 'seq', route)  26.4 us
    pallas_call x4, Pallas kernels, over_pairs(): pl.pallas_call(kernel, grid_spec=pltpu.PrefetchScalarGridSpec(num_scalar_...  6.5 us
    ppermute x2, starting transfers between devices, shift_along(): return lax.ppermute(block, axis, route)  6.15 us
    psum x1, blocking collectives, local(): squares = lax.psum(squares, 'ch')  5.67 us
    pallas_call x2, Pallas kernels, through_filter(): pl.pallas_call(functools.partial(product_kernel, conjugate, by_side), out...  3.99 us
  transfers between devices with their start and end apart: 22, of which 5 were waited for; matrix products, arithmetic and copies ran while one was open for 1% of the time, Pallas kernels for 11%

profile of v2, /device:TPU:0, one launch (start us, length us, event | category | flops | bytes accessed | tf_op | source)
XLA Modules:
  0.0 84.2 jit_solution(14676362381954050749)
XLA Ops:
  0.6 0.0 copy-start
  0.6 0.0 copy-start.1
  0.7 1.1 %copy-done.5 = f32[128,1024]{1,0:T(8,128)S(1)} copy-done((f32[128,1024]{1,0:T(8,128)S(1)}, f32[128,1024]{1,0:T(8,128)}, u32[]{:S(2)}) %copy-start.5) | copy-done | bytes 524312
  1.8 0.2 filter_blocks.1
  2.1 4.9 %collective-permute-start = (f32[3,2,1024]{2,1,0:T(2,128)S(1)}, f32[3,2,1024]{2,1,0:T(2,128)S(1)}, u32[]{:S(2)}, u32[]{:S(2)}) collective-permute-start(f32[3,2,1024]{2,1,0:T(2,128)S(1)} %get-tuple-element.29), channel_id=1, source_target_pairs={{0,4},{4,8},{8,12},{12,16},{16,20},{20,24},{24,28},{1,5},{5,9},{9,... | collective-permute-start | bytes 73736 | tf_op jit(solution)/shard_map/ppermute | solution.py:21
  7.0 2.7 %collective-permute-start.8 = (f32[2,128,128]{2,1,0:T(8,128)S(1)}, f32[2,128,128]{2,1,0:T(8,128)S(1)}, u32[]{:S(2)}, u32[]{:S(2)}) collective-permute-start(f32[2,128,128]{2,1,0:T(8,128)S(1)} %get-tuple-element.45), channel_id=1, source_target_pairs={{0,16},{4,20},{8,24},{12,28},{16,0},{20,4},{24,8},{28,12},{1,17},{... | collective-permute-start | bytes 393224 | tf_op jit(solution)/shard_map/filter_over_4/ppermute | solution.py:505
  9.6 1.3 %collective-permute-start.9 = (f32[2,128,128]{2,1,0:T(8,128)S(1)}, f32[2,128,128]{2,1,0:T(8,128)S(1)}, u32[]{:S(2)}, u32[]{:S(2)}) collective-permute-start(f32[2,128,128]{2,1,0:T(8,128)S(1)} %get-tuple-element.46), channel_id=1, source_target_pairs={{0,24},{4,28},{8,16},{12,20},{16,8},{20,12},{24,0},{28,4},{1,25},{... | collective-permute-start | bytes 393224 | tf_op jit(solution)/shard_map/filter_over_6/ppermute | solution.py:505
  11.0 0.2 collective-permute-start.1
  11.3 0.0 collective-permute-done.before_ref
  11.3 0.0 copy-done.6
  11.3 1.2 %short_filters.1 = (f32[2,4,128,128]{3,2,1,0:T(8,128)S(1)}, f32[2,4,128,128]{3,2,1,0:T(8,128)S(1)}) custom-call(s32[1]{0:T(128)} %bitcast.own_ref, bf16[3,128,1024]{2,1,0:T(8,128)(2,1)S(1)} %copy-done, f32[3,2,1024]{2,1,0:T(2,128)S(1)} %collective-permute-done.before_ref, f32[3,3,1024]{2,1,0:T(4,128)S(1)} %copy-done.6, bf16[128,1024]{1,0:T(8,128)(2,1)S(1)} %copy-done.1), custom_call_target="tpu_custom_call" | custom-call | bytes 88560 | tf_op jit(solution)/shard_map/short_filters/pallas_call | solution.py:301
  12.5 1.4 %collective-permute-start.3 = (f32[4,128,128]{2,1,0:T(8,128)S(1)}, f32[4,128,128]{2,1,0:T(8,128)S(1)}, u32[]{:S(2)}, u32[]{:S(2)}) collective-permute-start(f32[4,128,128]{2,1,0:T(8,128)S(1)} %get-tuple-element.56), channel_id=1, source_target_pairs={{0,4},{4,0},{8,12},{12,8},{16,20},{20,16},{24,28},{28,24},{1,5},{5... | collective-permute-start | bytes 786440 | tf_op jit(solution)/shard_map/gated_over_1/ppermute | solution.py:505
  13.9 0.8 collective-permute-start.7
  14.7 5.2 %collective-permute-done.1 = f32[2,128,128]{2,1,0:T(8,128)S(1)} collective-permute-done((f32[2,128,128]{2,1,0:T(8,128)S(1)}, f32[2,128,128]{2,1,0:T(8,128)S(1)}, u32[]{:S(2)}, u32[]{:S(2)}) %collective-permute-start.1) | collective-permute-done | bytes 131104 | tf_op jit(solution)/shard_map/filter_over_2/ppermute | solution.py:505
  19.9 1.3 %collective-permute-start.2 = (f32[4,2,1024]{2,1,0:T(2,128)S(1)}, f32[4,2,1024]{2,1,0:T(2,128)S(1)}, u32[]{:S(2)}, u32[]{:S(2)}) collective-permute-start(f32[4,2,1024]{2,1,0:T(2,128)S(1)} %maximum_convert_fusion), channel_id=1, source_target_pairs={{4,0},{8,4},{12,8},{16,12},{20,16},{24,20},{28,24},{5,1},{9,5},{13... | collective-permute-start | bytes 98312 | tf_op jit(solution)/shard_map/ppermute | solution.py:21
  21.2 0.0 collective-permute-done.8
  21.3 0.0 collective-permute-done.9
  21.3 2.7 %collective-permute-start.10 = (f32[4,128,128]{2,1,0:T(8,128)S(1)}, f32[4,128,128]{2,1,0:T(8,128)S(1)}, u32[]{:S(2)}, u32[]{:S(2)}) collective-permute-start(f32[4,128,128]{2,1,0:T(8,128)S(1)} %pad_maximum_fusion.7), channel_id=1, source_target_pairs={{0,4},{4,0},{8,12},{12,8},{16,20},{20,16},{24,28},{28,24},{1,5},{5... | collective-permute-start | bytes 786440 | tf_op jit(solution)/shard_map/filter_over_1/ppermute | solution.py:505
  24.0 0.0 collective-permute-done.3
  24.1 0.1 fusion.9
  24.1 1.0 %collective-permute-start.4 = (f32[2,128,128]{2,1,0:T(8,128)S(1)}, f32[2,128,128]{2,1,0:T(8,128)S(1)}, u32[]{:S(2)}, u32[]{:S(2)}) collective-permute-start(f32[2,128,128]{2,1,0:T(8,128)S(1)} %get-tuple-element.52), channel_id=1, source_target_pairs={{0,8},{4,12},{8,0},{12,4},{16,24},{20,28},{24,16},{28,20},{1,9},{5... | collective-permute-start | bytes 393224 | tf_op jit(solution)/shard_map/gated_over_2/ppermute | solution.py:505
  25.1 2.6 %collective-permute-start.6 = (f32[2,128,128]{2,1,0:T(8,128)S(1)}, f32[2,128,128]{2,1,0:T(8,128)S(1)}, u32[]{:S(2)}, u32[]{:S(2)}) collective-permute-start(f32[2,128,128]{2,1,0:T(8,128)S(1)} %get-tuple-element.53), channel_id=1, source_target_pairs={{0,24},{4,28},{8,16},{12,20},{16,8},{20,12},{24,0},{28,4},{1,25},{... | collective-permute-start | bytes 393224 | tf_op jit(solution)/shard_map/gated_over_6/ppermute | solution.py:505
  27.7 0.0 collective-permute-done.7
  27.7 2.3 %collective-permute-start.5 = (f32[2,128,128]{2,1,0:T(8,128)S(1)}, f32[2,128,128]{2,1,0:T(8,128)S(1)}, u32[]{:S(2)}, u32[]{:S(2)}) collective-permute-start(f32[2,128,128]{2,1,0:T(8,128)S(1)} %get-tuple-element.54), channel_id=1, source_target_pairs={{0,16},{4,20},{8,24},{12,28},{16,0},{20,4},{24,8},{28,12},{1,17},{... | collective-permute-start | bytes 393224 | tf_op jit(solution)/shard_map/gated_over_4/ppermute | solution.py:505
  30.1 0.0 copy-start.2
  30.1 0.0 copy-start.3
  30.1 0.0 copy-start.4
  30.1 1.7 %collective-permute-done.10 = f32[4,128,128]{2,1,0:T(8,128)S(1)} collective-permute-done((f32[4,128,128]{2,1,0:T(8,128)S(1)}, f32[4,128,128]{2,1,0:T(8,128)S(1)}, u32[]{:S(2)}, u32[]{:S(2)}) %collective-permute-start.10) | collective-permute-done | bytes 262176 | tf_op jit(solution)/shard_map/filter_over_1/ppermute | solution.py:505
  31.8 0.1 pad_maximum_fusion.5
  31.8 0.0 collective-permute-done.2._.after_ref
  31.9 1.1 %filter_spectrum.1.spec_ref = f32[9,256,128]{2,1,0:T(8,128)S(1)} custom-call(s32[1]{0:T(128)} %bitcast.own_ref, f32[8,128,128]{2,1,0:T(8,128)S(1)} %bitcast.77, bf16[256,256]{1,0:T(8,128)(2,1)S(1)} %copy-done.2, bf16[256,128]{1,0:T(8,128)(2,1)S(1)} %copy-done.4, f32[128,128]{1,0:T(8,128)S(1)} %copy-done.3, f32[4,2,1024]{2,1,0:T(2,128)S(1)} %collective-permute-done.2._.after_ref), custom_call_target="tpu_custom_call" | custom-call | bytes 81180 | tf_op jit(solution)/shard_map/filter_spectrum/pallas_call | solution.py:205
  33.0 2.6 %collective-permute-start.14 = (f32[2,128,128]{2,1,0:T(8,128)S(1)}, f32[2,128,128]{2,1,0:T(8,128)S(1)}, u32[]{:S(2)}, u32[]{:S(2)}) collective-permute-start(f32[2,128,128]{2,1,0:T(8,128)S(1)} %get-tuple-element.43), channel_id=1, source_target_pairs={{0,16},{4,20},{8,24},{12,28},{16,0},{20,4},{24,8},{28,12},{1,17},{... | collective-permute-start | bytes 393224 | tf_op jit(solution)/shard_map/carried_over_4/ppermute | solution.py:505
  35.6 0.7 collective-permute-start.13
  36.3 0.0 collective-permute-done.4
  36.3 1.2 %collective-permute-start.15 = (f32[2,128,128]{2,1,0:T(8,128)S(1)}, f32[2,128,128]{2,1,0:T(8,128)S(1)}, u32[]{:S(2)}, u32[]{:S(2)}) collective-permute-start(f32[2,128,128]{2,1,0:T(8,128)S(1)} %slice_bitcast_fusion.15), channel_id=1, source_target_pairs={{0,24},{4,28},{8,16},{12,20},{16,8},{20,12},{24,0},{28,4},{1,25},{... | collective-permute-start | bytes 393224 | tf_op jit(solution)/shard_map/carried_over_6/ppermute | solution.py:505
  37.5 0.0 collective-permute-done.6
  37.5 8.2 %collective-permute-done.5 = f32[2,128,128]{2,1,0:T(8,128)S(1)} collective-permute-done((f32[2,128,128]{2,1,0:T(8,128)S(1)}, f32[2,128,128]{2,1,0:T(8,128)S(1)}, u32[]{:S(2)}, u32[]{:S(2)}) %collective-permute-start.5) | collective-permute-done | bytes 131104 | tf_op jit(solution)/shard_map/gated_over_4/ppermute | solution.py:505
  45.8 2.0 %convolution.1 = f32[8,136,128]{2,1,0:T(8,128)S(1)} custom-call(s32[1]{0:T(128)} %bitcast.own_ref, f32[8,128,128]{2,1,0:T(8,128)S(1)} %bitcast.79, f32[9,256,128]{2,1,0:T(8,128)S(1)} %filter_spectrum.1.spec_ref, bf16[256,256]{1,0:T(8,128)(2,1)S(1)} %copy-done.2, bf16[256,128]{1,0:T(8,128)(2,1)S(1)} %copy-done.4, f32[128,128]{1,0:T(8,128)S(1)} %copy-done.3), custom_call_target="tpu_custom_call" | custom-call | bytes 184500 | tf_op jit(solution)/shard_map/convolution/pallas_call | solution.py:219
  47.8 0.7 collective-permute-start.11
  48.5 0.0 collective-permute-done.14
  48.5 0.0 collective-permute-done.13
  48.5 0.0 collective-permute-done.15
  48.6 2.0 %correlation.1 = f32[8,136,128]{2,1,0:T(8,128)S(1)} custom-call(s32[1]{0:T(128)} %bitcast.own_ref, f32[8,128,128]{2,1,0:T(8,128)S(1)} %bitcast.78, f32[9,256,128]{2,1,0:T(8,128)S(1)} %filter_spectrum.1.spec_ref, bf16[256,256]{1,0:T(8,128)(2,1)S(1)} %copy-done.2, bf16[256,128]{1,0:T(8,128)(2,1)S(1)} %copy-done.4, f32[128,128]{1,0:T(8,128)S(1)} %copy-done.3), custom_call_target="tpu_custom_call" | custom-call | bytes 184500 | tf_op jit(solution)/shard_map/correlation/pallas_call | solution.py:219
  50.6 1.5 %collective-permute-start.16 = (f32[4,136,128]{2,1,0:T(8,128)S(1)}, f32[4,136,128]{2,1,0:T(8,128)S(1)}, u32[]{:S(2)}, u32[]{:S(2)}) collective-permute-start(f32[4,136,128]{2,1,0:T(8,128)S(1)} %get-tuple-element.39), channel_id=1, source_target_pairs={{0,4},{4,0},{8,12},{12,8},{16,20},{20,16},{24,28},{28,24},{1,5},{5... | collective-permute-start | bytes 835592 | tf_op jit(solution)/shard_map/corr_over_1/ppermute | solution.py:505
  52.1 4.1 %collective-permute-done.11 = f32[4,136,128]{2,1,0:T(8,128)S(1)} collective-permute-done((f32[4,136,128]{2,1,0:T(8,128)S(1)}, f32[4,136,128]{2,1,0:T(8,128)S(1)}, u32[]{:S(2)}, u32[]{:S(2)}) %collective-permute-start.11) | collective-permute-done | bytes 278560 | tf_op jit(solution)/shard_map/conv_over_1/ppermute | solution.py:505
  56.2 0.1 collective-permute-start.17
  56.3 3.0 %collective-permute-start.12 = (f32[2,136,128]{2,1,0:T(8,128)S(1)}, f32[2,136,128]{2,1,0:T(8,128)S(1)}, u32[]{:S(2)}, u32[]{:S(2)}) collective-permute-start(f32[2,136,128]{2,1,0:T(8,128)S(1)} %get-tuple-element.35), channel_id=1, source_target_pairs={{0,8},{4,12},{8,0},{12,4},{16,24},{20,28},{24,16},{28,20},{1,9},{5... | collective-permute-start | bytes 417800 | tf_op jit(solution)/shard_map/conv_over_2/ppermute | solution.py:505
  59.3 1.4 %collective-permute-start.18 = (f32[2,136,128]{2,1,0:T(8,128)S(1)}, f32[2,136,128]{2,1,0:T(8,128)S(1)}, u32[]{:S(2)}, u32[]{:S(2)}) collective-permute-start(f32[2,136,128]{2,1,0:T(8,128)S(1)} %get-tuple-element.36), channel_id=1, source_target_pairs={{0,24},{4,28},{8,16},{12,20},{16,8},{20,12},{24,0},{28,4},{1,25},{... | collective-permute-start | bytes 417800 | tf_op jit(solution)/shard_map/conv_over_6/ppermute | solution.py:505
  60.7 0.0 collective-permute-done.16
  60.7 0.0 copy-start.7
  60.7 7.2 %collective-permute-done.17 = f32[2,136,128]{2,1,0:T(8,128)S(1)} collective-permute-done((f32[2,136,128]{2,1,0:T(8,128)S(1)}, f32[2,136,128]{2,1,0:T(8,128)S(1)}, u32[]{:S(2)}, u32[]{:S(2)}) %collective-permute-start.17) | collective-permute-done | bytes 139296 | tf_op jit(solution)/shard_map/conv_over_4/ppermute | solution.py:505
  68.0 2.8 %collective-permute-start.21 = (f32[2,136,128]{2,1,0:T(8,128)S(1)}, f32[2,136,128]{2,1,0:T(8,128)S(1)}, u32[]{:S(2)}, u32[]{:S(2)}) collective-permute-start(f32[2,136,128]{2,1,0:T(8,128)S(1)} %get-tuple-element.31), channel_id=1, source_target_pairs={{0,24},{4,28},{8,16},{12,20},{16,8},{20,12},{24,0},{28,4},{1,25},{... | collective-permute-start | bytes 417800 | tf_op jit(solution)/shard_map/corr_over_6/ppermute | solution.py:505
  70.8 0.0 collective-permute-start.20
  70.8 1.6 %collective-permute-start.19 = (f32[2,136,128]{2,1,0:T(8,128)S(1)}, f32[2,136,128]{2,1,0:T(8,128)S(1)}, u32[]{:S(2)}, u32[]{:S(2)}) collective-permute-start(f32[2,136,128]{2,1,0:T(8,128)S(1)} %get-tuple-element.33), channel_id=1, source_target_pairs={{0,8},{4,12},{8,0},{12,4},{16,24},{20,28},{24,16},{28,20},{1,9},{5... | collective-permute-start | bytes 417800 | tf_op jit(solution)/shard_map/corr_over_2/ppermute | solution.py:505
  72.5 0.0 collective-permute-done.12
  72.5 0.0 collective-permute-done.18
  72.5 0.1 pad_maximum_fusion.1.conv_ref
  72.5 2.4 %mixed_squares.1 = (f32[128,1024]{1,0:T(8,128)S(1)}, f32[1,128]{1,0:T(1,128)S(1)}, bf16[128,1024]{1,0:T(8,128)(2,1)S(1)}) custom-call(s32[1]{0:T(128)} %bitcast.own_ref, bf16[3,128,1024]{2,1,0:T(8,128)(2,1)S(1)} %copy-done, f32[3,2,1024]{2,1,0:T(2,128)S(1)} %collective-permute-done.before_ref, f32[4,2,1024]{2,1,0:T(2,128)S(1)} %collective-permute-done.2._.after_ref, ...), custom_call_target="tpu_custom_call" | custom-call | bytes 177120 | tf_op jit(solution)/shard_map/mixed_squares/pallas_call | solution.py:301
  74.9 5.7 %psum.7.square_ref = f32[1,128]{1,0:T(1,128)S(1)} all-reduce(f32[1,128]{1,0:T(1,128)S(1)} %get-tuple-element.25), channel_id=1, replica_groups=mesh['seq'=8,'ch'=4] {'ch'}, use_global_device_ids=true, to_apply=%region_0.0 | all-reduce | flops 128 | bytes 1024 | tf_op jit(solution)/shard_map/psum | solution.py:574
  80.6 0.8 %norm.1 = bf16[128,1024]{1,0:T(8,128)(2,1)} custom-call(f32[128,1024]{1,0:T(8,128)S(1)} %get-tuple-element.24.mixed_ref, f32[1,128]{1,0:T(1,128)S(1)} %psum.7.square_ref, f32[1,1024]{1,0:T(1,128)S(1)} %bitcast.82), custom_call_target="tpu_custom_call" | custom-call | bytes 66420 | tf_op jit(solution)/shard_map/norm/pallas_call | solution.py:450
  81.5 0.0 collective-permute-done.21
  81.5 0.0 collective-permute-done.20
  81.5 0.0 collective-permute-done.19
  81.5 2.7 %stream_grads.1 = bf16[3,128,1024]{2,1,0:T(8,128)(2,1)} custom-call(s32[1]{0:T(128)} %bitcast.own_ref, bf16[3,128,1024]{2,1,0:T(8,128)(2,1)S(1)} %copy-done, f32[3,2,1024]{2,1,0:T(2,128)S(1)} %collective-permute-done.before_ref, f32[4,2,1024]{2,1,0:T(2,128)S(1)} %collective-permute-done.2._.after_ref, f32[3,3,1024]{2,1,0:T(4,128)S(1)} %copy-done.6, ...), custom_call_target="tpu_custom_call" | custom-call | bytes 191880 | tf_op jit(solution)/shard_map/stream_grads/pallas_call | solution.py:301
  (34 shorter events, 0.7 us)
Async XLA Ops:
  0.6 1.4 %copy-start = (bf16[3,128,1024]{2,1,0:T(8,128)(2,1)S(1)}, bf16[3,128,1024]{2,1,0:T(8,128)(2,1)}, u32[]{:S(2)}) copy-start(bf16[3,128,1024]{2,1,0:T(8,128)(2,1)} %streams_ref.5) | copy-start | bytes 2359300
  0.6 10.6 %copy-start.1 = (bf16[128,1024]{1,0:T(8,128)(2,1)S(1)}, bf16[128,1024]{1,0:T(8,128)(2,1)}, u32[]{:S(2)}) copy-start(bf16[128,1024]{1,0:T(8,128)(2,1)} %cot_ref.5) | copy-start | bytes 786436
  0.7 1.1 %copy-start.5 = (f32[128,1024]{1,0:T(8,128)S(1)}, f32[128,1024]{1,0:T(8,128)}, u32[]{:S(2)}) copy-start(f32[128,1024]{1,0:T(8,128)} %x_ref.1) | copy-start | bytes 1572868
  1.8 9.5 %copy-start.6 = (f32[3,3,1024]{2,1,0:T(4,128)S(1)}, f32[3,3,1024]{2,1,0:T(4,128)}, u32[]{:S(2)}) copy-start(f32[3,3,1024]{2,1,0:T(4,128)} %taps_ref.5) | copy-start | bytes 110596
  2.1 9.2 %collective-permute-start = (f32[3,2,1024]{2,1,0:T(2,128)S(1)}, f32[3,2,1024]{2,1,0:T(2,128)S(1)}, u32[]{:S(2)}, u32[]{:S(2)}) collective-permute-start(f32[3,2,1024]{2,1,0:T(2,128)S(1)} %get-tuple-element.29), channel_id=1, source_target_pairs={{0,4},{4,8},{8,12},{12,16},{16,20},{20,24},{24,28},{1,5},{5,9},{9,... | collective-permute-start | bytes 73736 | tf_op jit(solution)/shard_map/ppermute | solution.py:21
  7.0 14.2 %collective-permute-start.8 = (f32[2,128,128]{2,1,0:T(8,128)S(1)}, f32[2,128,128]{2,1,0:T(8,128)S(1)}, u32[]{:S(2)}, u32[]{:S(2)}) collective-permute-start(f32[2,128,128]{2,1,0:T(8,128)S(1)} %get-tuple-element.45), channel_id=1, source_target_pairs={{0,16},{4,20},{8,24},{12,28},{16,0},{20,4},{24,8},{28,12},{1,17},{... | collective-permute-start | bytes 393224 | tf_op jit(solution)/shard_map/filter_over_4/ppermute | solution.py:505
  9.6 11.6 %collective-permute-start.9 = (f32[2,128,128]{2,1,0:T(8,128)S(1)}, f32[2,128,128]{2,1,0:T(8,128)S(1)}, u32[]{:S(2)}, u32[]{:S(2)}) collective-permute-start(f32[2,128,128]{2,1,0:T(8,128)S(1)} %get-tuple-element.46), channel_id=1, source_target_pairs={{0,24},{4,28},{8,16},{12,20},{16,8},{20,12},{24,0},{28,4},{1,25},{... | collective-permute-start | bytes 393224 | tf_op jit(solution)/shard_map/filter_over_6/ppermute | solution.py:505
  11.0 8.9 %collective-permute-start.1 = (f32[2,128,128]{2,1,0:T(8,128)S(1)}, f32[2,128,128]{2,1,0:T(8,128)S(1)}, u32[]{:S(2)}, u32[]{:S(2)}) collective-permute-start(f32[2,128,128]{2,1,0:T(8,128)S(1)} %get-tuple-element.47), channel_id=1, source_target_pairs={{0,8},{4,12},{8,0},{12,4},{16,24},{20,28},{24,16},{28,20},{1,9},{5... | collective-permute-start | bytes 393224 | tf_op jit(solution)/shard_map/filter_over_2/ppermute | solution.py:505
  12.5 11.5 %collective-permute-start.3 = (f32[4,128,128]{2,1,0:T(8,128)S(1)}, f32[4,128,128]{2,1,0:T(8,128)S(1)}, u32[]{:S(2)}, u32[]{:S(2)}) collective-permute-start(f32[4,128,128]{2,1,0:T(8,128)S(1)} %get-tuple-element.56), channel_id=1, source_target_pairs={{0,4},{4,0},{8,12},{12,8},{16,20},{20,16},{24,28},{28,24},{1,5},{5... | collective-permute-start | bytes 786440 | tf_op jit(solution)/shard_map/gated_over_1/ppermute | solution.py:505
  13.9 13.8 %collective-permute-start.7 = (f32[4,128,128]{2,1,0:T(8,128)S(1)}, f32[4,128,128]{2,1,0:T(8,128)S(1)}, u32[]{:S(2)}, u32[]{:S(2)}) collective-permute-start(f32[4,128,128]{2,1,0:T(8,128)S(1)} %get-tuple-element.50), channel_id=1, source_target_pairs={{0,4},{4,0},{8,12},{12,8},{16,20},{20,16},{24,28},{28,24},{1,5},{5... | collective-permute-start | bytes 786440 | tf_op jit(solution)/shard_map/carried_over_1/ppermute | solution.py:505
  19.9 11.9 %collective-permute-start.2 = (f32[4,2,1024]{2,1,0:T(2,128)S(1)}, f32[4,2,1024]{2,1,0:T(2,128)S(1)}, u32[]{:S(2)}, u32[]{:S(2)}) collective-permute-start(f32[4,2,1024]{2,1,0:T(2,128)S(1)} %maximum_convert_fusion), channel_id=1, source_target_pairs={{4,0},{8,4},{12,8},{16,12},{20,16},{24,20},{28,24},{5,1},{9,5},{13... | collective-permute-start | bytes 98312 | tf_op jit(solution)/shard_map/ppermute | solution.py:21
  21.3 10.4 %collective-permute-start.10 = (f32[4,128,128]{2,1,0:T(8,128)S(1)}, f32[4,128,128]{2,1,0:T(8,128)S(1)}, u32[]{:S(2)}, u32[]{:S(2)}) collective-permute-start(f32[4,128,128]{2,1,0:T(8,128)S(1)} %pad_maximum_fusion.7), channel_id=1, source_target_pairs={{0,4},{4,0},{8,12},{12,8},{16,20},{20,16},{24,28},{28,24},{1,5},{5... | collective-permute-start | bytes 786440 | tf_op jit(solution)/shard_map/filter_over_1/ppermute | solution.py:505
  24.1 12.2 %collective-permute-start.4 = (f32[2,128,128]{2,1,0:T(8,128)S(1)}, f32[2,128,128]{2,1,0:T(8,128)S(1)}, u32[]{:S(2)}, u32[]{:S(2)}) collective-permute-start(f32[2,128,128]{2,1,0:T(8,128)S(1)} %get-tuple-element.52), channel_id=1, source_target_pairs={{0,8},{4,12},{8,0},{12,4},{16,24},{20,28},{24,16},{28,20},{1,9},{5... | collective-permute-start | bytes 393224 | tf_op jit(solution)/shard_map/gated_over_2/ppermute | solution.py:505
  25.1 12.4 %collective-permute-start.6 = (f32[2,128,128]{2,1,0:T(8,128)S(1)}, f32[2,128,128]{2,1,0:T(8,128)S(1)}, u32[]{:S(2)}, u32[]{:S(2)}) collective-permute-start(f32[2,128,128]{2,1,0:T(8,128)S(1)} %get-tuple-element.53), channel_id=1, source_target_pairs={{0,24},{4,28},{8,16},{12,20},{16,8},{20,12},{24,0},{28,4},{1,25},{... | collective-permute-start | bytes 393224 | tf_op jit(solution)/shard_map/gated_over_6/ppermute | solution.py:505
  27.7 18.0 %collective-permute-start.5 = (f32[2,128,128]{2,1,0:T(8,128)S(1)}, f32[2,128,128]{2,1,0:T(8,128)S(1)}, u32[]{:S(2)}, u32[]{:S(2)}) collective-permute-start(f32[2,128,128]{2,1,0:T(8,128)S(1)} %get-tuple-element.54), channel_id=1, source_target_pairs={{0,16},{4,20},{8,24},{12,28},{16,0},{20,4},{24,8},{28,12},{1,17},{... | collective-permute-start | bytes 393224 | tf_op jit(solution)/shard_map/gated_over_4/ppermute | solution.py:505
  30.1 1.8 %copy-start.2 = (bf16[256,256]{1,0:T(8,128)(2,1)S(1)}, bf16[256,256]{1,0:T(8,128)(2,1)}, u32[]{:S(2)}) copy-start(bf16[256,256]{1,0:T(8,128)(2,1)} %constant.12.clone.high_ref) | copy-start | bytes 393220
  30.1 1.8 %copy-start.3 = (f32[128,128]{1,0:T(8,128)S(1)}, f32[128,128]{1,0:T(8,128)}, u32[]{:S(2)}) copy-start(f32[128,128]{1,0:T(8,128)} %constant.14.clone.tw_ref) | copy-start | bytes 196612
  30.1 1.8 %copy-start.4 = (bf16[256,128]{1,0:T(8,128)(2,1)S(1)}, bf16[256,128]{1,0:T(8,128)(2,1)}, u32[]{:S(2)}) copy-start(bf16[256,128]{1,0:T(8,128)(2,1)} %constant.13.clone.low_ref) | copy-start | bytes 196612
  33.0 15.5 %collective-permute-start.14 = (f32[2,128,128]{2,1,0:T(8,128)S(1)}, f32[2,128,128]{2,1,0:T(8,128)S(1)}, u32[]{:S(2)}, u32[]{:S(2)}) collective-permute-start(f32[2,128,128]{2,1,0:T(8,128)S(1)} %get-tuple-element.43), channel_id=1, source_target_pairs={{0,16},{4,20},{8,24},{12,28},{16,0},{20,4},{24,8},{28,12},{1,17},{... | collective-permute-start | bytes 393224 | tf_op jit(solution)/shard_map/carried_over_4/ppermute | solution.py:505
  35.6 12.9 %collective-permute-start.13 = (f32[2,128,128]{2,1,0:T(8,128)S(1)}, f32[2,128,128]{2,1,0:T(8,128)S(1)}, u32[]{:S(2)}, u32[]{:S(2)}) collective-permute-start(f32[2,128,128]{2,1,0:T(8,128)S(1)} %get-tuple-element.44), channel_id=1, source_target_pairs={{0,8},{4,12},{8,0},{12,4},{16,24},{20,28},{24,16},{28,20},{1,9},{5... | collective-permute-start | bytes 393224 | tf_op jit(solution)/shard_map/carried_over_2/ppermute | solution.py:505
  36.3 12.2 %collective-permute-start.15 = (f32[2,128,128]{2,1,0:T(8,128)S(1)}, f32[2,128,128]{2,1,0:T(8,128)S(1)}, u32[]{:S(2)}, u32[]{:S(2)}) collective-permute-start(f32[2,128,128]{2,1,0:T(8,128)S(1)} %slice_bitcast_fusion.15), channel_id=1, source_target_pairs={{0,24},{4,28},{8,16},{12,20},{16,8},{20,12},{24,0},{28,4},{1,25},{... | collective-permute-start | bytes 393224 | tf_op jit(solution)/shard_map/carried_over_6/ppermute | solution.py:505
  47.8 8.4 %collective-permute-start.11 = (f32[4,136,128]{2,1,0:T(8,128)S(1)}, f32[4,136,128]{2,1,0:T(8,128)S(1)}, u32[]{:S(2)}, u32[]{:S(2)}) collective-permute-start(f32[4,136,128]{2,1,0:T(8,128)S(1)} %get-tuple-element.41), channel_id=1, source_target_pairs={{0,4},{4,0},{8,12},{12,8},{16,20},{20,16},{24,28},{28,24},{1,5},{5... | collective-permute-start | bytes 835592 | tf_op jit(solution)/shard_map/conv_over_1/ppermute | solution.py:505
  50.6 10.1 %collective-permute-start.16 = (f32[4,136,128]{2,1,0:T(8,128)S(1)}, f32[4,136,128]{2,1,0:T(8,128)S(1)}, u32[]{:S(2)}, u32[]{:S(2)}) collective-permute-start(f32[4,136,128]{2,1,0:T(8,128)S(1)} %get-tuple-element.39), channel_id=1, source_target_pairs={{0,4},{4,0},{8,12},{12,8},{16,20},{20,16},{24,28},{28,24},{1,5},{5... | collective-permute-start | bytes 835592 | tf_op jit(solution)/shard_map/corr_over_1/ppermute | solution.py:505
  56.2 11.7 %collective-permute-start.17 = (f32[2,136,128]{2,1,0:T(8,128)S(1)}, f32[2,136,128]{2,1,0:T(8,128)S(1)}, u32[]{:S(2)}, u32[]{:S(2)}) collective-permute-start(f32[2,136,128]{2,1,0:T(8,128)S(1)} %get-tuple-element.37), channel_id=1, source_target_pairs={{0,16},{4,20},{8,24},{12,28},{16,0},{20,4},{24,8},{28,12},{1,17},{... | collective-permute-start | bytes 417800 | tf_op jit(solution)/shard_map/conv_over_4/ppermute | solution.py:505
  56.3 16.1 %collective-permute-start.12 = (f32[2,136,128]{2,1,0:T(8,128)S(1)}, f32[2,136,128]{2,1,0:T(8,128)S(1)}, u32[]{:S(2)}, u32[]{:S(2)}) collective-permute-start(f32[2,136,128]{2,1,0:T(8,128)S(1)} %get-tuple-element.35), channel_id=1, source_target_pairs={{0,8},{4,12},{8,0},{12,4},{16,24},{20,28},{24,16},{28,20},{1,9},{5... | collective-permute-start | bytes 417800 | tf_op jit(solution)/shard_map/conv_over_2/ppermute | solution.py:505
  59.3 13.1 %collective-permute-start.18 = (f32[2,136,128]{2,1,0:T(8,128)S(1)}, f32[2,136,128]{2,1,0:T(8,128)S(1)}, u32[]{:S(2)}, u32[]{:S(2)}) collective-permute-start(f32[2,136,128]{2,1,0:T(8,128)S(1)} %get-tuple-element.36), channel_id=1, source_target_pairs={{0,24},{4,28},{8,16},{12,20},{16,8},{20,12},{24,0},{28,4},{1,25},{... | collective-permute-start | bytes 417800 | tf_op jit(solution)/shard_map/conv_over_6/ppermute | solution.py:505
  60.7 11.8 %copy-start.7 = (f32[1024]{0:T(1024)S(1)}, f32[1024]{0:T(1024)}, u32[]{:S(2)}) copy-start(f32[1024]{0:T(1024)} %param.12) | copy-start | bytes 12292
  68.0 13.5 %collective-permute-start.21 = (f32[2,136,128]{2,1,0:T(8,128)S(1)}, f32[2,136,128]{2,1,0:T(8,128)S(1)}, u32[]{:S(2)}, u32[]{:S(2)}) collective-permute-start(f32[2,136,128]{2,1,0:T(8,128)S(1)} %get-tuple-element.31), channel_id=1, source_target_pairs={{0,24},{4,28},{8,16},{12,20},{16,8},{20,12},{24,0},{28,4},{1,25},{... | collective-permute-start | bytes 417800 | tf_op jit(solution)/shard_map/corr_over_6/ppermute | solution.py:505
  70.8 10.7 %collective-permute-start.20 = (f32[2,136,128]{2,1,0:T(8,128)S(1)}, f32[2,136,128]{2,1,0:T(8,128)S(1)}, u32[]{:S(2)}, u32[]{:S(2)}) collective-permute-start(f32[2,136,128]{2,1,0:T(8,128)S(1)} %get-tuple-element.32), channel_id=1, source_target_pairs={{0,16},{4,20},{8,24},{12,28},{16,0},{20,4},{24,8},{28,12},{1,17},{... | collective-permute-start | bytes 417800 | tf_op jit(solution)/shard_map/corr_over_4/ppermute | solution.py:505
  70.8 10.7 %collective-permute-start.19 = (f32[2,136,128]{2,1,0:T(8,128)S(1)}, f32[2,136,128]{2,1,0:T(8,128)S(1)}, u32[]{:S(2)}, u32[]{:S(2)}) collective-permute-start(f32[2,136,128]{2,1,0:T(8,128)S(1)} %get-tuple-element.33), channel_id=1, source_target_pairs={{0,8},{4,12},{8,0},{12,4},{16,24},{20,28},{24,16},{28,20},{1,9},{5... | collective-permute-start | bytes 417800 | tf_op jit(solution)/shard_map/corr_over_2/ppermute | solution.py:505
  72.5 8.2 %copy-start.8 = (f32[1024]{0:T(1024)S(1)}, f32[1024]{0:T(1024)}, u32[]{:S(2)}) copy-start(f32[1024]{0:T(1024)} %param.13) | copy-start | bytes 12292

commit v3 on v2

--- a/solution.py
+++ b/solution.py
@@ -12,7 +12,7 @@
 F32 = jnp.float32
 BF16 = jnp.bfloat16
 PAD_ROWS = 8
-VMEM_BYTES = 48 * 1024 * 1024
+VMEM_BYTES = 24 * 1024 * 1024
 
 
 def shift_along(block, axis, distance):
@@ -22,7 +22,7 @@
 
 
 def measured(microseconds):
-    return pl.CostEstimate(flops=0, bytes_accessed=int(microseconds * 73800.0), transcendentals=0)
+    return pl.CostEstimate(flops=0, bytes_accessed=int(microseconds * 3.69e6), transcendentals=0)
 
 
 def params():
@@ -129,7 +129,7 @@
     return sums[:rows, :width], sums[:rows, width:], sums[rows:, :width], sums[rows:, width:]
 
 
-def spectrum_kernel(own_ref, x_ref, high_ref, low_ref, tw_ref, _, spec_ref, split_ref):
+def spectrum_kernel(own_ref, x_ref, high_ref, low_ref, tw_ref, spec_ref, split_ref):
     blocks, rows = x_ref.shape[0], x_ref.shape[1]
     first_stage(own_ref[0], x_ref, tw_ref, split_ref, 32)
     for k in range(blocks + 1):
@@ -200,17 +200,17 @@
     return pltpu.VMEM((blocks + 1, 2 * rows, 2 * width), BF16)
 
 
-def spectrum(own, x, tables, unread):
+def spectrum(own, x, tables):
     blocks, rows, width = x.shape
     return pl.pallas_call(
         spectrum_kernel,
         out_shape=jax.ShapeDtypeStruct((blocks + 1, 2 * rows, width), F32),
-        in_specs=whole_operands(4) + [pl.BlockSpec(memory_space=pl.ANY)],
+        in_specs=whole_operands(4),
         scratch_shapes=[split_scratch(blocks, rows, width)],
         compiler_params=params(),
         cost_estimate=measured(1.1),
         name="filter_spectrum",
-    )(own, x, *tables, unread)
+    )(own, x, *tables)
 
 
 def through_filter(own, x, spec, tables, conjugate, by_side):
@@ -222,7 +222,7 @@
         in_specs=whole_operands(5),
         scratch_shapes=[split_scratch(blocks, rows, width), part, part],
         compiler_params=params(),
-        cost_estimate=measured(2.5),
+        cost_estimate=measured(0.05 if conjugate else 20),
         name="correlation" if conjugate else "convolution",
     )(own, x, spec, *tables)
 
@@ -240,15 +240,6 @@
     return moved
 
 
-def advanced(x, after, distance):
-    count = x.shape[0]
-    moved = pltpu.roll(x, count - distance, 0)
-    rows = row_number(x.shape)
-    for row in range(distance):
-        moved = jnp.where(rows == count - distance + row, after[row], moved)
-    return moved
-
-
 def rows_of(block):
     return [block[row : row + 1] for row in range(block.shape[0])]
 
@@ -265,13 +256,6 @@
     result = taps[0:1] * x
     for j in range(1, taps.shape[0]):
         result = result + taps[j : j + 1] * delayed(x, before, j)
-    return result
-
-
-def short_transpose(x, after, taps):
-    result = taps[0:1] * x
-    for j in range(1, taps.shape[0]):
-        result = result + taps[j : j + 1] * advanced(x, after, j)
     return result
 
 
@@ -290,8 +274,7 @@
         "taps": pl.BlockSpec((3, count, pair), lambda j, own: (0, 0, at(j, own))),
         "vector": pl.BlockSpec((1, pair), lambda j, own: (0, at(j, own))),
         "flat": pl.BlockSpec((rows, pair), lambda j, own: (0, at(j, own))),
-        "row": pl.BlockSpec((1, rows), lambda j, own: (0, 0)),
-        "chunk": pl.BlockSpec((1, 2, rows + PAD_ROWS, pair // 2), lambda j, own: (j, 0, 0, 0)),
+        "long": pl.BlockSpec((rows + PAD_ROWS, pair), lambda j, own: (0, at(j, own))),
         "by_pair": pl.BlockSpec((1, 2, rows, pair // 2), lambda j, own: (j, 0, 0, 0)),
         "by_side": pl.BlockSpec((2, 1, rows, pair // 2), lambda j, own: (0, j, 0, 0)),
     }
@@ -308,7 +291,7 @@
         ),
         out_shape=out_shape,
         compiler_params=params(),
-        cost_estimate=measured(microseconds),
+        cost_estimate=measured(0.02 * microseconds),
         name=name,
     )(own, *operands)
 
@@ -366,40 +349,86 @@
     )
 
 
-def mix_kernel(
-    own_ref, streams_ref, before_ref, after_ref, taps_ref, bias_ref, cot_ref, conv_ref, mixed_ref, square_ref, grad_ref
+def ahead(ext, distance):
+    rows = ext.shape[0] - PAD_ROWS
+    return (ext if distance == 0 else pltpu.roll(ext, ext.shape[0] - distance, 0))[:rows]
+
+
+def short_transpose(ext, taps):
+    return total([taps[j : j + 1] * ahead(ext, j) for j in range(taps.shape[0])])
+
+
+def with_rows(block, rows):
+    below = jnp.concatenate(rows + [jnp.zeros((PAD_ROWS - len(rows), block.shape[1]), F32)], axis=0)
+    return jnp.concatenate([block, below], axis=0)
+
+
+def prepare_kernel(
+    own_ref, streams_ref, before_ref, after_ref, taps_ref, bias_ref, cot_ref,
+    query_ref, key_ref, value_ref, cotangent_ref, gated_ref, carried_ref,
 ):
-    step = pl.program_id(0)
-    block = conv_ref.shape[3]
     rows = streams_ref.shape[1]
     rim = after_ref.shape[1]
-    squares = jnp.zeros((rows, block), F32)
+    block = query_ref.shape[1] // 2
     for part in range(2):
         lanes = lanes_of(part, block)
-        place = place_of_part(own_ref, part)
         bias = bias_ref[:, lanes]
         short = shorts_of(streams_ref, before_ref, taps_ref, lanes)
-        direct = conv_ref[0, place, :rows, :] + bias * (short[1] * short[2])
-        mixed = short[0] * direct
-        mixed_ref[:, lanes] = mixed
-        squares = squares + mixed * mixed
-        gated_after = [
+        below = [
             short_filter_after(
                 rows_of(after_ref[i, :, lanes]),
                 rows_of(streams_ref[i, rows - rim :, lanes].astype(F32)),
                 taps_ref[i, :, lanes],
             )
-            for i in (1, 2)
+            for i in range(3)
         ]
-        conv_after = rows_of(conv_ref[0, place, rows : rows + rim, :])
-        cot_after = rows_of(after_ref[3, :, lanes])
-        above = [
-            cot_after[row] * (conv_after[row] + bias * (gated_after[0][row] * gated_after[1][row]))
-            for row in range(rim)
-        ]
-        grad = short_transpose(cot_ref[:, lanes].astype(F32) * direct, above, taps_ref[0, :, lanes])
-        grad_ref[:, lanes] = grad.astype(BF16)
-    row_sums = lax.dot_general(
+        query, key, value = (with_rows(short[i], below[i]) for i in range(3))
+        cotangent = with_rows(cot_ref[:, lanes].astype(F32), rows_of(after_ref[3, :, lanes]))
+        query_ref[:, lanes] = short[0]
+        key_ref[:, lanes] = key
+        value_ref[:, lanes] = value
+        cotangent_ref[:, lanes] = cotangent
+        gated_ref[:, lanes] = bias * (key * value)
+        carried_ref[:, lanes] = bias * (cotangent * query)
+
+
+def prepare(own, streams, before, after, taps, bias, cotangent, parts, specs):
+    _, rows, width = streams.shape
+    long = jax.ShapeDtypeStruct((rows + PAD_ROWS, width), F32)
+    return over_pairs(
+        prepare_kernel,
+        own,
+        parts,
+        specs,
+        ["streams", "before", "after", "taps", "vector", "flat"],
+        ["flat"] + ["long"] * 5,
+        [jax.ShapeDtypeStruct((rows, width), F32)] + [long] * 5,
+        [streams, before, after, taps, bias, cotangent],
+        "rows_with_rim",
+        2.0,
+    )
+
+
+def blocks_of(own_ref, refs):
+    block = refs[0].shape[2]
+    for j, ref in enumerate(refs):
+        for place in range(2):
+            first = pl.multiple_of(((2 * j + place) ^ own_ref[0]) * block, block)
+            yield ref, place, pl.ds(first, block)
+
+
+def mix_kernel(count, own_ref, query_ref, cotangent_ref, gated_ref, taps_ref, *refs):
+    conv_refs, (mixed_ref, square_ref, grad_ref) = refs[:count], refs[count:]
+    rows = query_ref.shape[0]
+    block = conv_refs[0].shape[2]
+    squares = jnp.zeros((rows, block), F32)
+    for conv_ref, place, lanes in blocks_of(own_ref, conv_refs):
+        direct = conv_ref[place] + gated_ref[:, lanes]
+        mixed = query_ref[:, lanes] * direct[:rows]
+        mixed_ref[:, lanes] = mixed
+        squares = squares + mixed * mixed
+        grad_ref[:, lanes] = short_transpose(cotangent_ref[:, lanes] * direct, taps_ref[0, :, lanes]).astype(BF16)
+    square_ref[...] = lax.dot_general(
         jnp.ones((8, block), F32),
         squares,
         (((1,), (1,)), ((), ())),
@@ -407,33 +436,21 @@
         preferred_element_type=F32,
     )[0:1]
 
-    @pl.when(step == 0)
-    def _():
-        square_ref[...] = row_sums
-
-    @pl.when(step > 0)
-    def _():
-        square_ref[...] += row_sums
-
-
-def mix(own, streams, before, after, taps, bias, cotangent, conv, specs):
-    _, rows, width = streams.shape
-    return over_pairs(
-        mix_kernel,
-        own,
-        2 * conv.shape[0],
-        specs,
-        ["streams", "before", "after", "taps", "vector", "flat", "chunk"],
-        ["flat", "row", "flat"],
-        [
+
+def mix(own, query, cotangent, gated, taps, conv):
+    rows, width = query.shape
+    return pl.pallas_call(
+        functools.partial(mix_kernel, len(conv)),
+        out_shape=[
             jax.ShapeDtypeStruct((rows, width), F32),
             jax.ShapeDtypeStruct((1, rows), F32),
             jax.ShapeDtypeStruct((rows, width), BF16),
         ],
-        [streams, before, after, taps, bias, cotangent, conv],
-        "mixed_squares",
-        2.4,
-    )
+        in_specs=whole_operands(4 + len(conv)),
+        compiler_params=params(),
+        cost_estimate=measured(0.05),
+        name="mixed_squares",
+    )(own, query, cotangent, gated, taps, *conv)
 
 
 def norm_kernel(channels, mixed_ref, square_ref, gain_ref, normed_ref):
@@ -451,52 +468,47 @@
         functools.partial(norm_kernel, float(channels)),
         out_shape=jax.ShapeDtypeStruct((rows, width), BF16),
         compiler_params=params(),
-        cost_estimate=measured(0.9),
+        cost_estimate=measured(0.02),
         name="norm",
     )(mixed, squares, gain)
 
 
-def finish_kernel(
-    own_ref, streams_ref, before_ref, after_ref, taps_ref, bias_ref, cot_ref, grad_ref, corr_ref, grads_ref
-):
-    block = corr_ref.shape[3]
-    rows = streams_ref.shape[1]
-    rim = after_ref.shape[1]
-    grads_ref[0] = grad_ref[...]
-    for part in range(2):
-        lanes = lanes_of(part, block)
-        place = place_of_part(own_ref, part)
-        bias = bias_ref[:, lanes]
-        taps = [taps_ref[i, :, lanes] for i in range(3)]
-        short = shorts_of(streams_ref, before_ref, taps_ref, lanes)
-        gated_grad = corr_ref[0, place, :rows, :] + bias * (cot_ref[:, lanes].astype(F32) * short[0])
-        short_after = [
-            short_filter_after(
-                rows_of(after_ref[i, :, lanes]), rows_of(streams_ref[i, rows - rim :, lanes].astype(F32)), taps[i]
-            )
-            for i in range(3)
-        ]
-        corr_after = rows_of(corr_ref[0, place, rows : rows + rim, :])
-        cot_after = rows_of(after_ref[3, :, lanes])
-        grad_after = [corr_after[row] + bias * (cot_after[row] * short_after[0][row]) for row in range(rim)]
-        for i, other in ((1, 2), (2, 1)):
-            above = [grad_after[row] * short_after[other][row] for row in range(rim)]
-            grads_ref[i, :, lanes] = short_transpose(gated_grad * short[other], above, taps[i]).astype(BF16)
-
-
-def finish(own, streams, before, after, taps, bias, cotangent, grad, corr, specs):
-    return over_pairs(
-        finish_kernel,
-        own,
-        2 * corr.shape[0],
-        specs,
-        ["streams", "before", "after", "taps", "vector", "flat", "flat", "chunk"],
-        ["streams"],
-        [jax.ShapeDtypeStruct(streams.shape, BF16)],
-        [streams, before, after, taps, bias, cotangent, grad, corr],
-        "stream_grads",
-        2.6,
-    )[0]
+def finish_kernel(count, own_ref, key_ref, value_ref, carried_ref, taps_ref, grad_ref, *refs):
+    corr_refs, (grads_ref, sent_ref, sems, first_sem) = refs[:count], refs[count:]
+    first = pltpu.make_async_copy(grad_ref, grads_ref.at[0], first_sem)
+    first.start()
+    copies = [first]
+    for place_of, (corr_ref, place, lanes) in enumerate(blocks_of(own_ref, corr_refs)):
+        gated_grad = corr_ref[place] + carried_ref[:, lanes]
+        for i, other_ref in ((1, value_ref), (2, key_ref)):
+            grad = short_transpose(gated_grad * other_ref[:, lanes], taps_ref[i, :, lanes])
+            sent_ref[i - 1, :, lanes] = grad.astype(BF16)
+        copy = pltpu.make_async_copy(
+            sent_ref.at[:, :, lanes], grads_ref.at[1:3, :, lanes], sems.at[place_of]
+        )
+        copy.start()
+        copies.append(copy)
+    for copy in copies:
+        copy.wait()
+
+
+def finish(own, key, value, carried, taps, grad, corr):
+    rows, width = grad.shape
+    blocks = 2 * len(corr)
+    return pl.pallas_call(
+        functools.partial(finish_kernel, len(corr)),
+        out_shape=jax.ShapeDtypeStruct((3, rows, width), BF16),
+        in_specs=whole_operands(5 + len(corr)),
+        out_specs=pl.BlockSpec(memory_space=pl.ANY),
+        scratch_shapes=[
+            pltpu.VMEM((2, rows, width), BF16),
+            pltpu.SemaphoreType.DMA((blocks,)),
+            pltpu.SemaphoreType.DMA,
+        ],
+        compiler_params=params(),
+        cost_estimate=measured(0.05),
+        name="stream_grads",
+    )(own, key, value, carried, taps, grad, *corr)
 
 
 def swapped(block, apart, name):
@@ -505,6 +517,17 @@
         return lax.ppermute(block, "seq", route)
 
 
+def summed_over(block, axis):
+    count = lax.axis_size(axis)
+    if count & (count - 1):
+        return lax.psum(block, axis)
+    result = block
+    for apart in range(1, count):
+        with jax.named_scope(f"squares_over_{apart}"):
+            result = result + lax.ppermute(block, axis, [(i, i ^ apart) for i in range(count)])
+    return result
+
+
 def tied(value, other):
     return lax.optimization_barrier((value, other))
 
@@ -514,15 +537,36 @@
 
 
 def between_pairs(name, blocks):
-    return [blocks[0]] + [swapped(blocks[j], 2 * j, name) for j in range(1, len(blocks))]
+    order = list(range(2, len(blocks))) + [1]
+    got = {j: swapped(blocks[j], 2 * j, name) for j in order}
+    return [blocks[0]] + [got[j] for j in range(1, len(blocks))]
+
+
+def together(blocks, edges):
+    width = blocks.shape[-1]
+    return jnp.concatenate([blocks.reshape(-1, width), edges.reshape(-1, width)], axis=0)
+
+
+def apart_again(rows, blocks, edges):
+    count = blocks.size // rows.shape[1]
+    return rows[:count].reshape(blocks.shape), rows[count:].reshape(edges.shape)
+
+
+def rows_after(own, came):
+    after = jnp.where(own % 2 == 0, came[0], 0.0)
+    pair = own // 2
+    for k in range(1, len(came)):
+        follows = (own % 2 == 1) & (pair ^ (pair + 1) == 2**k - 1)
+        after = jnp.where(follows, came[k], after)
+    return after
 
 
 def sides_of(got):
     return jnp.stack([block[0] for block in got]), jnp.stack([block[1] for block in got])
 
 
-def joined(kept, other):
-    return jnp.stack([kept, other], axis=1)
+def paired(kept, other):
+    return [jnp.stack([kept[j], other[j]]) for j in range(kept.shape[0])]
 
 
 def as_line(blocks):
@@ -542,38 +586,51 @@
     filter_got = between_pairs("filter", filter_sent)
     streams_later, filter_got[0] = tied(streams, filter_got[0])
     before = shift_along(streams_later[:, rows - rim :].astype(F32), "seq", 1)
+    edges = jnp.concatenate([streams_later[:, :rim].astype(F32), cotangent[None, :rim].astype(F32)], axis=0)
     gated, carried = gate(own, streams, before, short_taps, cotangent, parts, specs)
-    edges = jnp.concatenate([streams_later[:, :rim].astype(F32), cotangent[None, :rim].astype(F32)], axis=0)
-    edges, filter_got[1] = tied(edges, filter_got[1])
-    after = shift_along(edges, "seq", -1)
 
     gated_other = within_pairs("gated", gated[1])
     carried_gone = carried[1]
-    gated_got = between_pairs("gated", joined(gated[0], gated_other))
+    carried_gone, gated_other = tied(carried_gone, gated_other)
+    gated_got = between_pairs("gated", paired(gated[0], gated_other))
     filter_kept, filter_gone = sides_of(filter_got)
     filter_other = within_pairs("filter", filter_gone)
-    filter_blocks = joined(filter_kept, filter_other)
-    carried_pairs = joined(carried[0], within_pairs("carried", carried_gone))
-    spec = spectrum(own, as_line(filter_blocks), tables, after)
-    carried_pairs, spec = tied(carried_pairs, spec)
-    carried_got = between_pairs("carried", carried_pairs)
-
+    filter_blocks = paired(filter_kept, filter_other)
+    carried_other, edges_other = apart_again(within_pairs("carried", together(carried_gone, edges)), carried_gone, edges)
+    carried_pairs = paired(carried[0], carried_other)
+    spec = spectrum(own, as_line(jnp.stack(filter_blocks)), tables)
     shape = (rows + PAD_ROWS, width // parts)
     gated_blocks = as_line(jnp.stack(gated_got))
+    carried_pairs, gated_got[1] = tied(carried_pairs, gated_got[1])
     conv_sent = through_filter(own, gated_blocks, spec, tables, False, True).reshape((2, parts // 2) + shape)
-    conv_pairs = joined(conv_sent[0], within_pairs("conv", conv_sent[1]))
+    carried_pairs = list(carried_pairs)
+    steps = [j for j in range(1, parts // 2) if j & (j + 1) == 0]
+    alone = carried_pairs[0]
+    for j in steps:
+        carried_pairs[j] = together(carried_pairs[j], edges_other)
+    carried_got = between_pairs("carried", carried_pairs)
+    edges_got = []
+    for j in steps:
+        carried_got[j], came = apart_again(carried_got[j], alone, edges)
+        edges_got.append(came)
+    conv_pairs = paired(conv_sent[0], within_pairs("conv", conv_sent[1]))
     carried_blocks = jnp.stack(carried_got)
     conv_got = between_pairs("conv", conv_pairs)
     corr_sent = through_filter(own, as_line(carried_blocks), spec, tables, True, True).reshape((2, parts // 2) + shape)
-    corr_pairs = joined(corr_sent[0], within_pairs("corr", corr_sent[1]))
+    corr_pairs = paired(corr_sent[0], within_pairs("corr", corr_sent[1]))
     corr_pairs, conv_got[2] = tied(corr_pairs, conv_got[2])
+    after = rows_after(own[0], [edges_other] + edges_got)
+    after, conv_got[1] = tied(after, conv_got[1])
+    query, key, value, later, gated_direct, carried_direct = prepare(
+        own, streams, before, after, short_taps, bias, cotangent, parts, specs
+    )
+    corr_pairs, query = tied(corr_pairs, query)
     corr_got = between_pairs("corr", corr_pairs)
-    conv = jnp.stack(conv_got)
-    corr = jnp.stack(corr_got)
-    mixed, squares, grad = mix(own, streams, before, after, short_taps, bias, cotangent, conv, specs)
-    squares = lax.psum(squares, "ch")
+    query, corr_got[1] = tied(query, corr_got[1])
+    mixed, squares, grad = mix(own, query, later, gated_direct, short_taps, conv_got)
+    squares = summed_over(squares, "ch")
     normed = norm(width * lax.axis_size("ch"), mixed, squares, gain)
-    grads = finish(own, streams, before, after, short_taps, bias, cotangent, grad, corr, specs)
+    grads = finish(own, key, value, carried_direct, short_taps, grad, corr_got)
     return normed, grads
 
 

time: 84.4 us -> 81.4 us (0.964)
  blocking collectives: 5.67 us -> 0 us
  waiting for transfers between devices: 26.4 us -> 30 us
  Pallas kernels: 12.4 us -> 11 us
  local copies, waits for them, and re-layouts: 1.51 us -> 2.36 us
    psum x1 -> x0, blocking collectives: 5.67 us -> none  [local(): squares = lax.psum(squares, 'ch')]
    ppermute x20, waiting for transfers between devices: 26.4 us -> 30 us  [swapped(): return lax.ppermute(block, 'seq', route)]
    pallas_call x4 -> x3, Pallas kernels: 6.5 us -> 3.28 us  [over_pairs(): pl.pallas_call(kernel, grid_spec=pltpu.PrefetchScalarGridSpec(num_scalar_...]
    ppermute x0 -> x3, starting transfers between devices: none -> 1.89 us  [summed_over(): lax.ppermute(block, axis, [(i, i ^ apart) for i in range(count)])]
    pallas_call x0 -> x2, Pallas kernels: none -> 1.84 us  [the longest x1 1.32 us: finish(): pl.pallas_call(functools.partial(finish_kernel, len(corr)), out_shape=jax...]
    ppermute x2 -> x1, starting transfers between devices: 6.15 us -> 4.87 us  [shift_along(): return lax.ppermute(block, axis, route)]
    ppermute x20, starting transfers between devices: 30.6 us -> 29.4 us  [swapped(): return lax.ppermute(block, 'seq', route)]
  transfers between devices with their start and end apart: 22 -> 24, of which waited for: 5 -> 10; matrix products, arithmetic and copies ran while one was open for 1% -> 1% of each run, Pallas kernels for 11% -> 12%
where the time goes in v3:
time: 81.4 us; the launch traced here: 81.2 us
  starting transfers between devices  36.2 us (44%)
  waiting for transfers between devices  30 us (37%)
  Pallas kernels  11 us (14%)
  local copies, waits for them, and re-layouts  2.36 us (3%)
  between operations  1.19 us (1%)
    ppermute x20, waiting for transfers between devices, swapped(): return lax.ppermute(block, 'seq', route)  30 us
    ppermute x20, starting transfers between devices, swapped(): return lax.ppermute(block, 'seq', route)  29.4 us
    ppermute x1, starting transfers between devices, shift_along(): return lax.ppermute(block, axis, route)  4.87 us
    pallas_call x2, Pallas kernels, through_filter(): pl.pallas_call(functools.partial(product_kernel, conjugate, by_side), out...  3.99 us
    pallas_call x3, Pallas kernels, over_pairs(): pl.pallas_call(kernel, grid_spec=pltpu.PrefetchScalarGridSpec(num_scalar_...  3.28 us
    unnamed x18, local copies, waits for them, and re-layouts  1.95 us
    ppermute x3, starting transfers between devices, summed_over(): lax.ppermute(block, axis, [(i, i ^ apart) for i in range(count)])  1.89 us
  transfers between devices with their start and end apart: 24, of which 10 were waited for; matrix products, arithmetic and copies ran while one was open for 1% of the time, Pallas kernels for 12%

profile of v3, /device:TPU:0, one launch (start us, length us, event | category | flops | bytes accessed | tf_op | source)
XLA Modules:
  0.0 81.2 jit_solution(2965043172202065544)
XLA Ops:
  0.7 1.1 %copy-done.6 = f32[128,1024]{1,0:T(8,128)S(1)} copy-done((f32[128,1024]{1,0:T(8,128)S(1)}, f32[128,1024]{1,0:T(8,128)}, u32[]{:S(2)}) %copy-start.6) | copy-done | bytes 524312
  1.8 0.2 filter_blocks.1
  2.1 4.9 %collective-permute-start = (f32[3,2,1024]{2,1,0:T(2,128)S(1)}, f32[3,2,1024]{2,1,0:T(2,128)S(1)}, u32[]{:S(2)}, u32[]{:S(2)}) collective-permute-start(f32[3,2,1024]{2,1,0:T(2,128)S(1)} %get-tuple-element.68), channel_id=1, source_target_pairs={{0,4},{4,8},{8,12},{12,16},{16,20},{20,24},{24,28},{1,5},{5,9},{9,... | collective-permute-start | bytes 73736 | tf_op jit(solution)/shard_map/ppermute | solution.py:21
  7.0 1.6 %collective-permute-start.7 = (f32[2,128,128]{2,1,0:T(8,128)S(1)}, f32[2,128,128]{2,1,0:T(8,128)S(1)}, u32[]{:S(2)}, u32[]{:S(2)}) collective-permute-start(f32[2,128,128]{2,1,0:T(8,128)S(1)} %get-tuple-element.82), channel_id=1, source_target_pairs={{0,8},{4,12},{8,0},{12,4},{16,24},{20,28},{24,16},{28,20},{1,9},{5... | collective-permute-start | bytes 393224 | tf_op jit(solution)/shard_map/filter_over_2/ppermute | solution.py:517
  8.6 2.5 %collective-permute-start.9 = (f32[2,128,128]{2,1,0:T(8,128)S(1)}, f32[2,128,128]{2,1,0:T(8,128)S(1)}, u32[]{:S(2)}, u32[]{:S(2)}) collective-permute-start(f32[2,128,128]{2,1,0:T(8,128)S(1)} %get-tuple-element.83), channel_id=1, source_target_pairs={{0,24},{4,28},{8,16},{12,20},{16,8},{20,12},{24,0},{28,4},{1,25},{... | collective-permute-start | bytes 393224 | tf_op jit(solution)/shard_map/filter_over_6/ppermute | solution.py:517
  11.1 0.1 collective-permute-start.8
  11.4 0.0 collective-permute-done.before_ref
  11.4 1.2 %short_filters.1 = (f32[2,4,128,128]{3,2,1,0:T(8,128)S(1)}, f32[2,4,128,128]{3,2,1,0:T(8,128)S(1)}) custom-call(s32[1]{0:T(128)} %bitcast.own_ref, bf16[3,128,1024]{2,1,0:T(8,128)(2,1)S(1)} %copy-done, f32[3,2,1024]{2,1,0:T(2,128)S(1)} %collective-permute-done.before_ref, f32[3,3,1024]{2,1,0:T(4,128)S(1)} %copy-done.3, bf16[128,1024]{1,0:T(8,128)(2,1)S(1)} %copy-done.2), custom_call_target="tpu_custom_call" | custom-call | bytes 88560 | tf_op jit(solution)/shard_map/short_filters/pallas_call | solution.py:284
  12.6 1.5 %collective-permute-start.1 = (f32[4,128,128]{2,1,0:T(8,128)S(1)}, f32[4,128,128]{2,1,0:T(8,128)S(1)}, u32[]{:S(2)}, u32[]{:S(2)}) collective-permute-start(f32[4,128,128]{2,1,0:T(8,128)S(1)} %slice_bitcast_fusion), channel_id=1, source_target_pairs={{0,4},{4,0},{8,12},{12,8},{16,20},{20,16},{24,28},{28,24},{1,5},{5... | collective-permute-start | bytes 786440 | tf_op jit(solution)/shard_map/gated_over_1/ppermute | solution.py:517
  14.1 0.0 collective-permute-done.7
  14.2 4.1 %collective-permute-done.9 = f32[2,128,128]{2,1,0:T(8,128)S(1)} collective-permute-done((f32[2,128,128]{2,1,0:T(8,128)S(1)}, f32[2,128,128]{2,1,0:T(8,128)S(1)}, u32[]{:S(2)}, u32[]{:S(2)}) %collective-permute-start.9) | collective-permute-done | bytes 131104 | tf_op jit(solution)/shard_map/filter_over_6/ppermute | solution.py:517
  18.3 4.3 %collective-permute-done.8 = f32[2,128,128]{2,1,0:T(8,128)S(1)} collective-permute-done((f32[2,128,128]{2,1,0:T(8,128)S(1)}, f32[2,128,128]{2,1,0:T(8,128)S(1)}, u32[]{:S(2)}, u32[]{:S(2)}) %collective-permute-start.8) | collective-permute-done | bytes 131104 | tf_op jit(solution)/shard_map/filter_over_4/ppermute | solution.py:517
  22.6 0.9 %collective-permute-start.10 = (f32[4,128,128]{2,1,0:T(8,128)S(1)}, f32[4,128,128]{2,1,0:T(8,128)S(1)}, u32[]{:S(2)}, u32[]{:S(2)}) collective-permute-start(f32[4,128,128]{2,1,0:T(8,128)S(1)} %pad_maximum_fusion.4), channel_id=1, source_target_pairs={{0,4},{4,0},{8,12},{12,8},{16,20},{20,16},{24,28},{28,24},{1,5},{5... | collective-permute-start | bytes 786440 | tf_op jit(solution)/shard_map/filter_over_1/ppermute | solution.py:517
  23.5 0.0 collective-permute-done.1
  23.6 0.1 collective-permute-start.3
  23.7 2.7 %collective-permute-start.12 = (f32[2,128,128]{2,1,0:T(8,128)S(1)}, f32[2,128,128]{2,1,0:T(8,128)S(1)}, u32[]{:S(2)}, u32[]{:S(2)}) collective-permute-start(f32[2,128,128]{2,1,0:T(8,128)S(1)} %pad_maximum_fusion.20), channel_id=1, source_target_pairs={{0,16},{4,20},{8,24},{12,28},{16,0},{20,4},{24,8},{28,12},{1,17},{... | collective-permute-start | bytes 393224 | tf_op jit(solution)/shard_map/gated_over_4/ppermute | solution.py:517
  26.4 1.8 %collective-permute-start.13 = (f32[2,128,128]{2,1,0:T(8,128)S(1)}, f32[2,128,128]{2,1,0:T(8,128)S(1)}, u32[]{:S(2)}, u32[]{:S(2)}) collective-permute-start(f32[2,128,128]{2,1,0:T(8,128)S(1)} %pad_maximum_fusion.21), channel_id=1, source_target_pairs={{0,24},{4,28},{8,16},{12,20},{16,8},{20,12},{24,0},{28,4},{1,25},{... | collective-permute-start | bytes 393224 | tf_op jit(solution)/shard_map/gated_over_6/ppermute | solution.py:517
  28.2 1.2 %collective-permute-start.2 = (f32[576,128]{1,0:T(8,128)S(1)}, f32[576,128]{1,0:T(8,128)S(1)}, u32[]{:S(2)}, u32[]{:S(2)}) collective-permute-start(f32[576,128]{1,0:T(8,128)S(1)} %pad_maximum_fusion.3), channel_id=1, source_target_pairs={{0,4},{4,0},{8,12},{12,8},{16,20},{20,16},{24,28},{28,24},{1,5},{5... | collective-permute-start | bytes 884744 | tf_op jit(solution)/shard_map/carried_over_1/ppermute | solution.py:517
  29.5 1.1 %collective-permute-done.10 = f32[4,128,128]{2,1,0:T(8,128)S(1)} collective-permute-done((f32[4,128,128]{2,1,0:T(8,128)S(1)}, f32[4,128,128]{2,1,0:T(8,128)S(1)}, u32[]{:S(2)}, u32[]{:S(2)}) %collective-permute-start.10) | collective-permute-done | bytes 262176 | tf_op jit(solution)/shard_map/filter_over_1/ppermute | solution.py:517
  30.6 0.0 copy-start.1
  30.6 0.0 copy-start.4
  30.6 0.0 copy-start.5
  30.7 0.8 copy-done.1
  31.5 0.0 copy-done.5
  31.5 1.1 %filter_spectrum.1.spec_ref = f32[9,256,128]{2,1,0:T(8,128)S(1)} custom-call(s32[1]{0:T(128)} %bitcast.own_ref, f32[8,128,128]{2,1,0:T(8,128)S(1)} %bitcast.64, bf16[256,256]{1,0:T(8,128)(2,1)S(1)} %copy-done.1, bf16[256,128]{1,0:T(8,128)(2,1)S(1)} %copy-done.5, f32[128,128]{1,0:T(8,128)S(1)} %copy-done.4), custom_call_target="tpu_custom_call" | custom-call | bytes 4059000 | tf_op jit(solution)/shard_map/filter_spectrum/pallas_call | solution.py:205
  32.6 0.0 collective-permute-done.3
  32.6 3.7 %collective-permute-done.12 = f32[2,128,128]{2,1,0:T(8,128)S(1)} collective-permute-done((f32[2,128,128]{2,1,0:T(8,128)S(1)}, f32[2,128,128]{2,1,0:T(8,128)S(1)}, u32[]{:S(2)}, u32[]{:S(2)}) %collective-permute-start.12) | collective-permute-done | bytes 131104 | tf_op jit(solution)/shard_map/gated_over_4/ppermute | solution.py:517
  36.3 0.0 collective-permute-done.13
  36.4 2.0 %convolution.1 = f32[8,136,128]{2,1,0:T(8,128)S(1)} custom-call(s32[1]{0:T(128)} %bitcast.own_ref, f32[8,128,128]{2,1,0:T(8,128)S(1)} %bitcast.66, f32[9,256,128]{2,1,0:T(8,128)S(1)} %filter_spectrum.1.spec_ref, bf16[256,256]{1,0:T(8,128)(2,1)S(1)} %copy-done.1, bf16[256,128]{1,0:T(8,128)(2,1)S(1)} %copy-done.5, f32[128,128]{1,0:T(8,128)S(1)} %copy-done.4), custom_call_target="tpu_custom_call" | custom-call | bytes 73800000 | tf_op jit(solution)/shard_map/convolution/pallas_call | solution.py:219
  38.4 0.8 %collective-permute-start.14 = (f32[4,136,128]{2,1,0:T(8,128)S(1)}, f32[4,136,128]{2,1,0:T(8,128)S(1)}, u32[]{:S(2)}, u32[]{:S(2)}) collective-permute-start(f32[4,136,128]{2,1,0:T(8,128)S(1)} %slice.350), channel_id=1, source_target_pairs={{0,4},{4,0},{8,12},{12,8},{16,20},{20,16},{24,28},{28,24},{1,5},{5... | collective-permute-start | bytes 835592 | tf_op jit(solution)/shard_map/conv_over_1/ppermute | solution.py:517
  39.3 0.0 collective-permute-done.2
  39.4 2.9 %collective-permute-start.5 = (f32[2,128,128]{2,1,0:T(8,128)S(1)}, f32[2,128,128]{2,1,0:T(8,128)S(1)}, u32[]{:S(2)}, u32[]{:S(2)}) collective-permute-start(f32[2,128,128]{2,1,0:T(8,128)S(1)} %get-tuple-element.42), channel_id=1, source_target_pairs={{0,16},{4,20},{8,24},{12,28},{16,0},{20,4},{24,8},{28,12},{1,17},{... | collective-permute-start | bytes 393224 | tf_op jit(solution)/shard_map/carried_over_4/ppermute | solution.py:517
  42.3 0.1 collective-permute-start.4
  42.5 1.5 %collective-permute-start.6 = (f32[320,128]{1,0:T(8,128)S(1)}, f32[320,128]{1,0:T(8,128)S(1)}, u32[]{:S(2)}, u32[]{:S(2)}) collective-permute-start(f32[320,128]{1,0:T(8,128)S(1)} %get-tuple-element.119), channel_id=1, source_target_pairs={{0,24},{4,28},{8,16},{12,20},{16,8},{20,12},{24,0},{28,4},{1,25},{... | collective-permute-start | bytes 491528 | tf_op jit(solution)/shard_map/carried_over_6/ppermute | solution.py:517
  43.9 1.1 %collective-permute-done.14 = f32[4,136,128]{2,1,0:T(8,128)S(1)} collective-permute-done((f32[4,136,128]{2,1,0:T(8,128)S(1)}, f32[4,136,128]{2,1,0:T(8,128)S(1)}, u32[]{:S(2)}, u32[]{:S(2)}) %collective-permute-start.14) | collective-permute-done | bytes 278560 | tf_op jit(solution)/shard_map/conv_over_1/ppermute | solution.py:517
  45.1 2.8 %collective-permute-start.15 = (f32[2,136,128]{2,1,0:T(8,128)S(1)}, f32[2,136,128]{2,1,0:T(8,128)S(1)}, u32[]{:S(2)}, u32[]{:S(2)}) collective-permute-start(f32[2,136,128]{2,1,0:T(8,128)S(1)} %pad_maximum_fusion.11), channel_id=1, source_target_pairs={{0,16},{4,20},{8,24},{12,28},{16,0},{20,4},{24,8},{28,12},{1,17},{... | collective-permute-start | bytes 417800 | tf_op jit(solution)/shard_map/conv_over_4/ppermute | solution.py:517
  47.9 0.1 collective-permute-start.16
  48.0 2.7 %collective-permute-done.4 = f32[320,128]{1,0:T(8,128)S(1)} collective-permute-done((f32[320,128]{1,0:T(8,128)S(1)}, f32[320,128]{1,0:T(8,128)S(1)}, u32[]{:S(2)}, u32[]{:S(2)}) %collective-permute-start.4) | collective-permute-done | bytes 163872 | tf_op jit(solution)/shard_map/carried_over_2/ppermute | solution.py:517
  50.8 4.5 %collective-permute-done.6 = f32[320,128]{1,0:T(8,128)S(1)} collective-permute-done((f32[320,128]{1,0:T(8,128)S(1)}, f32[320,128]{1,0:T(8,128)S(1)}, u32[]{:S(2)}, u32[]{:S(2)}) %collective-permute-start.6) | collective-permute-done | bytes 163872 | tf_op jit(solution)/shard_map/carried_over_6/ppermute | solution.py:517
  55.2 0.0 collective-permute-done.5
  55.3 2.0 %correlation.1 = f32[8,136,128]{2,1,0:T(8,128)S(1)} custom-call(s32[1]{0:T(128)} %bitcast.own_ref, f32[8,128,128]{2,1,0:T(8,128)S(1)} %bitcast.65, f32[9,256,128]{2,1,0:T(8,128)S(1)} %filter_spectrum.1.spec_ref, bf16[256,256]{1,0:T(8,128)(2,1)S(1)} %copy-done.1, bf16[256,128]{1,0:T(8,128)(2,1)S(1)} %copy-done.5, f32[128,128]{1,0:T(8,128)S(1)} %copy-done.4), custom_call_target="tpu_custom_call" | custom-call | bytes 184500 | tf_op jit(solution)/shard_map/correlation/pallas_call | solution.py:219
  57.3 0.0 copy-start.7
  57.4 1.3 %collective-permute-start.11 = (f32[4,136,128]{2,1,0:T(8,128)S(1)}, f32[4,136,128]{2,1,0:T(8,128)S(1)}, u32[]{:S(2)}, u32[]{:S(2)}) collective-permute-start(f32[4,136,128]{2,1,0:T(8,128)S(1)} %slice.341), channel_id=1, source_target_pairs={{0,4},{4,0},{8,12},{12,8},{16,20},{20,16},{24,28},{28,24},{1,5},{5... | collective-permute-start | bytes 835592 | tf_op jit(solution)/shard_map/corr_over_1/ppermute | solution.py:517
  58.7 0.0 collective-permute-done.16.refs_1_
  58.8 1.9 %rows_with_rim.1 = (f32[128,1024]{1,0:T(8,128)S(1)}, f32[136,1024]{1,0:T(8,128)S(1)}, f32[136,1024]{1,0:T(8,128)S(1)}, f32[136,1024]{1,0:T(8,128)S(1)}, f32[136,...) custom-call(s32[1]{0:T(128)} %bitcast.own_ref, bf16[3,128,1024]{2,1,0:T(8,128)(2,1)S(1)} %copy-done, ...), custom_call_target="tpu_custom_call" | custom-call | bytes 147600 | tf_op jit(solution)/shard_map/rows_with_rim/pallas_call | solution.py:284
  60.6 3.3 %collective-permute-done.11 = f32[4,136,128]{2,1,0:T(8,128)S(1)} collective-permute-done((f32[4,136,128]{2,1,0:T(8,128)S(1)}, f32[4,136,128]{2,1,0:T(8,128)S(1)}, u32[]{:S(2)}, u32[]{:S(2)}) %collective-permute-start.11) | collective-permute-done | bytes 278560 | tf_op jit(solution)/shard_map/corr_over_1/ppermute | solution.py:517
  64.1 0.0 collective-permute-done.15.refs_2_
  64.1 3.5 %collective-permute-start.17 = (f32[2,136,128]{2,1,0:T(8,128)S(1)}, f32[2,136,128]{2,1,0:T(8,128)S(1)}, u32[]{:S(2)}, u32[]{:S(2)}) collective-permute-start(f32[2,136,128]{2,1,0:T(8,128)S(1)} %pad_maximum_fusion.8), channel_id=1, source_target_pairs={{0,8},{4,12},{8,0},{12,4},{16,24},{20,28},{24,16},{28,20},{1,9},{5... | collective-permute-start | bytes 417800 | tf_op jit(solution)/shard_map/corr_over_2/ppermute | solution.py:517
  67.6 2.1 %collective-permute-start.18 = (f32[2,136,128]{2,1,0:T(8,128)S(1)}, f32[2,136,128]{2,1,0:T(8,128)S(1)}, u32[]{:S(2)}, u32[]{:S(2)}) collective-permute-start(f32[2,136,128]{2,1,0:T(8,128)S(1)} %pad_maximum_fusion.14), channel_id=1, source_target_pairs={{0,24},{4,28},{8,16},{12,20},{16,8},{20,12},{24,0},{28,4},{1,25},{... | collective-permute-start | bytes 417800 | tf_op jit(solution)/shard_map/conv_over_6/ppermute | solution.py:517
  69.7 0.0 collective-permute-start.22
  69.7 1.8 %collective-permute-start.23 = (f32[2,136,128]{2,1,0:T(8,128)S(1)}, f32[2,136,128]{2,1,0:T(8,128)S(1)}, u32[]{:S(2)}, u32[]{:S(2)}) collective-permute-start(f32[2,136,128]{2,1,0:T(8,128)S(1)} %pad_maximum_fusion.10), channel_id=1, source_target_pairs={{0,24},{4,28},{8,16},{12,20},{16,8},{20,12},{24,0},{28,4},{1,25},{... | collective-permute-start | bytes 417800 | tf_op jit(solution)/shard_map/corr_over_6/ppermute | solution.py:517
  71.5 0.0 collective-permute-done.17.refs_1_
  71.5 3.0 %collective-permute-done.18.refs_3_ = f32[2,136,128]{2,1,0:T(8,128)S(1)} collective-permute-done((f32[2,136,128]{2,1,0:T(8,128)S(1)}, f32[2,136,128]{2,1,0:T(8,128)S(1)}, u32[]{:S(2)}, u32[]{:S(2)}) %collective-permute-start.18) | collective-permute-done | bytes 139296 | tf_op jit(solution)/shard_map/conv_over_6/ppermute | solution.py:517
  74.5 0.5 mixed_squares.1
  75.1 0.0 collective-permute-start.21
  75.1 1.6 %collective-permute-start.20 = (f32[1,128]{1,0:T(1,128)S(1)}, f32[1,128]{1,0:T(1,128)S(1)}, u32[]{:S(2)}, u32[]{:S(2)}) collective-permute-start(f32[1,128]{1,0:T(1,128)S(1)} %get-tuple-element.59), channel_id=1, source_target_pairs={{0,2},{1,3},{2,0},{3,1},{4,6},{5,7},{6,4},{7,5},{8,10},{9,11},{10,... | collective-permute-start | bytes 1544 | tf_op jit(solution)/shard_map/squares_over_2/ppermute | solution.py:527
  76.6 0.3 collective-permute-start.19
  76.9 2.0 %collective-permute-done.22.refs_2_ = f32[2,136,128]{2,1,0:T(8,128)S(1)} collective-permute-done((f32[2,136,128]{2,1,0:T(8,128)S(1)}, f32[2,136,128]{2,1,0:T(8,128)S(1)}, u32[]{:S(2)}, u32[]{:S(2)}) %collective-permute-start.22) | collective-permute-done | bytes 139296 | tf_op jit(solution)/shard_map/corr_over_4/ppermute | solution.py:517
  79.0 0.0 collective-permute-done.23.refs_3_
  79.0 1.3 %stream_grads.1 = bf16[3,128,1024]{2,1,0:T(8,128)(2,1)} custom-call(s32[1]{0:T(128)} %bitcast.own_ref, f32[136,1024]{1,0:T(8,128)S(1)} %get-tuple-element.60.key_ref, f32[136,1024]{1,0:T(8,128)S(1)} %get-tuple-element.61.value_ref, f32[136,1024]{1,0:T(8,128)S(1)} %get-tuple-element.62.carried_ref, f32[3,3,1024]{2,1,0:T(4,128)S(1)} %copy-done.3, ...), custom_call_target="tpu_custom_call" | custom-call | bytes 184500 | tf_op jit(solution)/shard_map/stream_grads/pallas_call | solution.py:498
  80.3 0.0 collective-permute-done.21
  80.3 0.0 collective-permute-done.20
  80.3 0.0 collective-permute-done.19
  80.4 0.8 %norm.1 = bf16[128,1024]{1,0:T(8,128)(2,1)} custom-call(f32[128,1024]{1,0:T(8,128)S(1)} %get-tuple-element.58.mixed_ref, f32[1,128]{1,0:T(1,128)S(1)} %add_add_fusion.square_ref, f32[1,1024]{1,0:T(1,128)S(1)} %bitcast.68), custom_call_target="tpu_custom_call" | custom-call | bytes 73800 | tf_op jit(solution)/shard_map/norm/pallas_call | solution.py:467
  (61 shorter events, 0.9 us)
Async XLA Ops:
  0.6 1.4 %copy-start = (bf16[3,128,1024]{2,1,0:T(8,128)(2,1)S(1)}, bf16[3,128,1024]{2,1,0:T(8,128)(2,1)}, u32[]{:S(2)}) copy-start(bf16[3,128,1024]{2,1,0:T(8,128)(2,1)} %streams_ref.3) | copy-start | bytes 2359300
  0.6 10.6 %copy-start.2 = (bf16[128,1024]{1,0:T(8,128)(2,1)S(1)}, bf16[128,1024]{1,0:T(8,128)(2,1)}, u32[]{:S(2)}) copy-start(bf16[128,1024]{1,0:T(8,128)(2,1)} %cot_ref.3) | copy-start | bytes 786436
  0.7 1.1 %copy-start.6 = (f32[128,1024]{1,0:T(8,128)S(1)}, f32[128,1024]{1,0:T(8,128)}, u32[]{:S(2)}) copy-start(f32[128,1024]{1,0:T(8,128)} %x_ref.1) | copy-start | bytes 1572868
  1.8 9.6 %copy-start.3 = (f32[3,3,1024]{2,1,0:T(4,128)S(1)}, f32[3,3,1024]{2,1,0:T(4,128)}, u32[]{:S(2)}) copy-start(f32[3,3,1024]{2,1,0:T(4,128)} %taps_ref.7) | copy-start | bytes 110596
  2.1 9.2 %collective-permute-start = (f32[3,2,1024]{2,1,0:T(2,128)S(1)}, f32[3,2,1024]{2,1,0:T(2,128)S(1)}, u32[]{:S(2)}, u32[]{:S(2)}) collective-permute-start(f32[3,2,1024]{2,1,0:T(2,128)S(1)} %get-tuple-element.68), channel_id=1, source_target_pairs={{0,4},{4,8},{8,12},{12,16},{16,20},{20,24},{24,28},{1,5},{5,9},{9,... | collective-permute-start | bytes 73736 | tf_op jit(solution)/shard_map/ppermute | solution.py:21
  7.0 7.2 %collective-permute-start.7 = (f32[2,128,128]{2,1,0:T(8,128)S(1)}, f32[2,128,128]{2,1,0:T(8,128)S(1)}, u32[]{:S(2)}, u32[]{:S(2)}) collective-permute-start(f32[2,128,128]{2,1,0:T(8,128)S(1)} %get-tuple-element.82), channel_id=1, source_target_pairs={{0,8},{4,12},{8,0},{12,4},{16,24},{20,28},{24,16},{28,20},{1,9},{5... | collective-permute-start | bytes 393224 | tf_op jit(solution)/shard_map/filter_over_2/ppermute | solution.py:517
  8.6 9.6 %collective-permute-start.9 = (f32[2,128,128]{2,1,0:T(8,128)S(1)}, f32[2,128,128]{2,1,0:T(8,128)S(1)}, u32[]{:S(2)}, u32[]{:S(2)}) collective-permute-start(f32[2,128,128]{2,1,0:T(8,128)S(1)} %get-tuple-element.83), channel_id=1, source_target_pairs={{0,24},{4,28},{8,16},{12,20},{16,8},{20,12},{24,0},{28,4},{1,25},{... | collective-permute-start | bytes 393224 | tf_op jit(solution)/shard_map/filter_over_6/ppermute | solution.py:517
  11.1 11.5 %collective-permute-start.8 = (f32[2,128,128]{2,1,0:T(8,128)S(1)}, f32[2,128,128]{2,1,0:T(8,128)S(1)}, u32[]{:S(2)}, u32[]{:S(2)}) collective-permute-start(f32[2,128,128]{2,1,0:T(8,128)S(1)} %get-tuple-element.84), channel_id=1, source_target_pairs={{0,16},{4,20},{8,24},{12,28},{16,0},{20,4},{24,8},{28,12},{1,17},{... | collective-permute-start | bytes 393224 | tf_op jit(solution)/shard_map/filter_over_4/ppermute | solution.py:517
  12.6 10.9 %collective-permute-start.1 = (f32[4,128,128]{2,1,0:T(8,128)S(1)}, f32[4,128,128]{2,1,0:T(8,128)S(1)}, u32[]{:S(2)}, u32[]{:S(2)}) collective-permute-start(f32[4,128,128]{2,1,0:T(8,128)S(1)} %slice_bitcast_fusion), channel_id=1, source_target_pairs={{0,4},{4,0},{8,12},{12,8},{16,20},{20,16},{24,28},{28,24},{1,5},{5... | collective-permute-start | bytes 786440 | tf_op jit(solution)/shard_map/gated_over_1/ppermute | solution.py:517
  22.6 7.9 %collective-permute-start.10 = (f32[4,128,128]{2,1,0:T(8,128)S(1)}, f32[4,128,128]{2,1,0:T(8,128)S(1)}, u32[]{:S(2)}, u32[]{:S(2)}) collective-permute-start(f32[4,128,128]{2,1,0:T(8,128)S(1)} %pad_maximum_fusion.4), channel_id=1, source_target_pairs={{0,4},{4,0},{8,12},{12,8},{16,20},{20,16},{24,28},{28,24},{1,5},{5... | collective-permute-start | bytes 786440 | tf_op jit(solution)/shard_map/filter_over_1/ppermute | solution.py:517
  23.6 9.0 %collective-permute-start.3 = (f32[2,128,128]{2,1,0:T(8,128)S(1)}, f32[2,128,128]{2,1,0:T(8,128)S(1)}, u32[]{:S(2)}, u32[]{:S(2)}) collective-permute-start(f32[2,128,128]{2,1,0:T(8,128)S(1)} %pad_maximum_fusion.19), channel_id=1, source_target_pairs={{0,8},{4,12},{8,0},{12,4},{16,24},{20,28},{24,16},{28,20},{1,9},{5... | collective-permute-start | bytes 393224 | tf_op jit(solution)/shard_map/gated_over_2/ppermute | solution.py:517
  23.7 12.6 %collective-permute-start.12 = (f32[2,128,128]{2,1,0:T(8,128)S(1)}, f32[2,128,128]{2,1,0:T(8,128)S(1)}, u32[]{:S(2)}, u32[]{:S(2)}) collective-permute-start(f32[2,128,128]{2,1,0:T(8,128)S(1)} %pad_maximum_fusion.20), channel_id=1, source_target_pairs={{0,16},{4,20},{8,24},{12,28},{16,0},{20,4},{24,8},{28,12},{1,17},{... | collective-permute-start | bytes 393224 | tf_op jit(solution)/shard_map/gated_over_4/ppermute | solution.py:517
  26.4 9.9 %collective-permute-start.13 = (f32[2,128,128]{2,1,0:T(8,128)S(1)}, f32[2,128,128]{2,1,0:T(8,128)S(1)}, u32[]{:S(2)}, u32[]{:S(2)}) collective-permute-start(f32[2,128,128]{2,1,0:T(8,128)S(1)} %pad_maximum_fusion.21), channel_id=1, source_target_pairs={{0,24},{4,28},{8,16},{12,20},{16,8},{20,12},{24,0},{28,4},{1,25},{... | collective-permute-start | bytes 393224 | tf_op jit(solution)/shard_map/gated_over_6/ppermute | solution.py:517
  28.2 11.1 %collective-permute-start.2 = (f32[576,128]{1,0:T(8,128)S(1)}, f32[576,128]{1,0:T(8,128)S(1)}, u32[]{:S(2)}, u32[]{:S(2)}) collective-permute-start(f32[576,128]{1,0:T(8,128)S(1)} %pad_maximum_fusion.3), channel_id=1, source_target_pairs={{0,4},{4,0},{8,12},{12,8},{16,20},{20,16},{24,28},{28,24},{1,5},{5... | collective-permute-start | bytes 884744 | tf_op jit(solution)/shard_map/carried_over_1/ppermute | solution.py:517
  30.6 0.9 %copy-start.1 = (bf16[256,256]{1,0:T(8,128)(2,1)S(1)}, bf16[256,256]{1,0:T(8,128)(2,1)}, u32[]{:S(2)}) copy-start(bf16[256,256]{1,0:T(8,128)(2,1)} %constant.46.clone.high_ref) | copy-start | bytes 393220
  30.6 0.9 %copy-start.4 = (f32[128,128]{1,0:T(8,128)S(1)}, f32[128,128]{1,0:T(8,128)}, u32[]{:S(2)}) copy-start(f32[128,128]{1,0:T(8,128)} %constant.48.clone.tw_ref) | copy-start | bytes 196612
  30.6 0.9 %copy-start.5 = (bf16[256,128]{1,0:T(8,128)(2,1)S(1)}, bf16[256,128]{1,0:T(8,128)(2,1)}, u32[]{:S(2)}) copy-start(bf16[256,128]{1,0:T(8,128)(2,1)} %constant.47.clone.low_ref) | copy-start | bytes 196612
  38.4 6.6 %collective-permute-start.14 = (f32[4,136,128]{2,1,0:T(8,128)S(1)}, f32[4,136,128]{2,1,0:T(8,128)S(1)}, u32[]{:S(2)}, u32[]{:S(2)}) collective-permute-start(f32[4,136,128]{2,1,0:T(8,128)S(1)} %slice.350), channel_id=1, source_target_pairs={{0,4},{4,0},{8,12},{12,8},{16,20},{20,16},{24,28},{28,24},{1,5},{5... | collective-permute-start | bytes 835592 | tf_op jit(solution)/shard_map/conv_over_1/ppermute | solution.py:517
  39.4 15.9 %collective-permute-start.5 = (f32[2,128,128]{2,1,0:T(8,128)S(1)}, f32[2,128,128]{2,1,0:T(8,128)S(1)}, u32[]{:S(2)}, u32[]{:S(2)}) collective-permute-start(f32[2,128,128]{2,1,0:T(8,128)S(1)} %get-tuple-element.42), channel_id=1, source_target_pairs={{0,16},{4,20},{8,24},{12,28},{16,0},{20,4},{24,8},{28,12},{1,17},{... | collective-permute-start | bytes 393224 | tf_op jit(solution)/shard_map/carried_over_4/ppermute | solution.py:517
  42.3 8.4 %collective-permute-start.4 = (f32[320,128]{1,0:T(8,128)S(1)}, f32[320,128]{1,0:T(8,128)S(1)}, u32[]{:S(2)}, u32[]{:S(2)}) collective-permute-start(f32[320,128]{1,0:T(8,128)S(1)} %get-tuple-element.118), channel_id=1, source_target_pairs={{0,8},{4,12},{8,0},{12,4},{16,24},{20,28},{24,16},{28,20},{1,9},{5... | collective-permute-start | bytes 491528 | tf_op jit(solution)/shard_map/carried_over_2/ppermute | solution.py:517
  42.5 12.8 %collective-permute-start.6 = (f32[320,128]{1,0:T(8,128)S(1)}, f32[320,128]{1,0:T(8,128)S(1)}, u32[]{:S(2)}, u32[]{:S(2)}) collective-permute-start(f32[320,128]{1,0:T(8,128)S(1)} %get-tuple-element.119), channel_id=1, source_target_pairs={{0,24},{4,28},{8,16},{12,20},{16,8},{20,12},{24,0},{28,4},{1,25},{... | collective-permute-start | bytes 491528 | tf_op jit(solution)/shard_map/carried_over_6/ppermute | solution.py:517
  45.1 19.0 %collective-permute-start.15 = (f32[2,136,128]{2,1,0:T(8,128)S(1)}, f32[2,136,128]{2,1,0:T(8,128)S(1)}, u32[]{:S(2)}, u32[]{:S(2)}) collective-permute-start(f32[2,136,128]{2,1,0:T(8,128)S(1)} %pad_maximum_fusion.11), channel_id=1, source_target_pairs={{0,16},{4,20},{8,24},{12,28},{16,0},{20,4},{24,8},{28,12},{1,17},{... | collective-permute-start | bytes 417800 | tf_op jit(solution)/shard_map/conv_over_4/ppermute | solution.py:517
  47.9 10.8 %collective-permute-start.16 = (f32[2,136,128]{2,1,0:T(8,128)S(1)}, f32[2,136,128]{2,1,0:T(8,128)S(1)}, u32[]{:S(2)}, u32[]{:S(2)}) collective-permute-start(f32[2,136,128]{2,1,0:T(8,128)S(1)} %pad_maximum_fusion.12), channel_id=1, source_target_pairs={{0,8},{4,12},{8,0},{12,4},{16,24},{20,28},{24,16},{28,20},{1,9},{5... | collective-permute-start | bytes 417800 | tf_op jit(solution)/shard_map/conv_over_2/ppermute | solution.py:517
  57.3 1.4 %copy-start.7 = (f32[1024]{0:T(1024)S(1)}, f32[1024]{0:T(1024)}, u32[]{:S(2)}) copy-start(f32[1024]{0:T(1024)} %param.12) | copy-start | bytes 12292
  57.4 6.6 %collective-permute-start.11 = (f32[4,136,128]{2,1,0:T(8,128)S(1)}, f32[4,136,128]{2,1,0:T(8,128)S(1)}, u32[]{:S(2)}, u32[]{:S(2)}) collective-permute-start(f32[4,136,128]{2,1,0:T(8,128)S(1)} %slice.341), channel_id=1, source_target_pairs={{0,4},{4,0},{8,12},{12,8},{16,20},{20,16},{24,28},{28,24},{1,5},{5... | collective-permute-start | bytes 835592 | tf_op jit(solution)/shard_map/corr_over_1/ppermute | solution.py:517
  64.1 7.4 %collective-permute-start.17 = (f32[2,136,128]{2,1,0:T(8,128)S(1)}, f32[2,136,128]{2,1,0:T(8,128)S(1)}, u32[]{:S(2)}, u32[]{:S(2)}) collective-permute-start(f32[2,136,128]{2,1,0:T(8,128)S(1)} %pad_maximum_fusion.8), channel_id=1, source_target_pairs={{0,8},{4,12},{8,0},{12,4},{16,24},{20,28},{24,16},{28,20},{1,9},{5... | collective-permute-start | bytes 417800 | tf_op jit(solution)/shard_map/corr_over_2/ppermute | solution.py:517
  67.6 7.0 %collective-permute-start.18 = (f32[2,136,128]{2,1,0:T(8,128)S(1)}, f32[2,136,128]{2,1,0:T(8,128)S(1)}, u32[]{:S(2)}, u32[]{:S(2)}) collective-permute-start(f32[2,136,128]{2,1,0:T(8,128)S(1)} %pad_maximum_fusion.14), channel_id=1, source_target_pairs={{0,24},{4,28},{8,16},{12,20},{16,8},{20,12},{24,0},{28,4},{1,25},{... | collective-permute-start | bytes 417800 | tf_op jit(solution)/shard_map/conv_over_6/ppermute | solution.py:517
  69.7 9.3 %collective-permute-start.22 = (f32[2,136,128]{2,1,0:T(8,128)S(1)}, f32[2,136,128]{2,1,0:T(8,128)S(1)}, u32[]{:S(2)}, u32[]{:S(2)}) collective-permute-start(f32[2,136,128]{2,1,0:T(8,128)S(1)} %pad_maximum_fusion.9), channel_id=1, source_target_pairs={{0,16},{4,20},{8,24},{12,28},{16,0},{20,4},{24,8},{28,12},{1,17},{... | collective-permute-start | bytes 417800 | tf_op jit(solution)/shard_map/corr_over_4/ppermute | solution.py:517
  69.7 9.3 %collective-permute-start.23 = (f32[2,136,128]{2,1,0:T(8,128)S(1)}, f32[2,136,128]{2,1,0:T(8,128)S(1)}, u32[]{:S(2)}, u32[]{:S(2)}) collective-permute-start(f32[2,136,128]{2,1,0:T(8,128)S(1)} %pad_maximum_fusion.10), channel_id=1, source_target_pairs={{0,24},{4,28},{8,16},{12,20},{16,8},{20,12},{24,0},{28,4},{1,25},{... | collective-permute-start | bytes 417800 | tf_op jit(solution)/shard_map/corr_over_6/ppermute | solution.py:517
  75.1 5.3 %collective-permute-start.21 = (f32[1,128]{1,0:T(1,128)S(1)}, f32[1,128]{1,0:T(1,128)S(1)}, u32[]{:S(2)}, u32[]{:S(2)}) collective-permute-start(f32[1,128]{1,0:T(1,128)S(1)} %get-tuple-element.59), channel_id=1, source_target_pairs={{0,3},{1,2},{2,1},{3,0},{4,7},{5,6},{6,5},{7,4},{8,11},{9,10},{10,... | collective-permute-start | bytes 1544 | tf_op jit(solution)/shard_map/squares_over_3/ppermute | solution.py:527
  75.1 5.3 %collective-permute-start.20 = (f32[1,128]{1,0:T(1,128)S(1)}, f32[1,128]{1,0:T(1,128)S(1)}, u32[]{:S(2)}, u32[]{:S(2)}) collective-permute-start(f32[1,128]{1,0:T(1,128)S(1)} %get-tuple-element.59), channel_id=1, source_target_pairs={{0,2},{1,3},{2,0},{3,1},{4,6},{5,7},{6,4},{7,5},{8,10},{9,11},{10,... | collective-permute-start | bytes 1544 | tf_op jit(solution)/shard_map/squares_over_2/ppermute | solution.py:527
  76.6 3.7 %collective-permute-start.19 = (f32[1,128]{1,0:T(1,128)S(1)}, f32[1,128]{1,0:T(1,128)S(1)}, u32[]{:S(2)}, u32[]{:S(2)}) collective-permute-start(f32[1,128]{1,0:T(1,128)S(1)} %get-tuple-element.59), channel_id=1, source_target_pairs={{0,1},{1,0},{2,3},{3,2},{4,5},{5,4},{6,7},{7,6},{8,9},{9,8},{10,11... | collective-permute-start | bytes 1544 | tf_op jit(solution)/shard_map/squares_over_1/ppermute | solution.py:527
  79.0 1.4 %copy-start.8 = (f32[1024]{0:T(1024)S(1)}, f32[1024]{0:T(1024)}, u32[]{:S(2)}) copy-start(f32[1024]{0:T(1024)} %param.13) | copy-start | bytes 12292

commit v4 on v3

--- a/solution.py
+++ b/solution.py
@@ -561,6 +561,13 @@
     return after
 
 
+def in_turn(blocks, earlier):
+    blocks, earlier = list(blocks), list(earlier)
+    for j in range(2, len(blocks)):
+        blocks[j], earlier[j] = tied(blocks[j], earlier[j])
+    return blocks, earlier
+
+
 def sides_of(got):
     return jnp.stack([block[0] for block in got]), jnp.stack([block[1] for block in got])
 
@@ -614,6 +621,7 @@
         carried_got[j], came = apart_again(carried_got[j], alone, edges)
         edges_got.append(came)
     conv_pairs = paired(conv_sent[0], within_pairs("conv", conv_sent[1]))
+    conv_pairs, carried_got = in_turn(conv_pairs, carried_got)
     carried_blocks = jnp.stack(carried_got)
     conv_got = between_pairs("conv", conv_pairs)
     corr_sent = through_filter(own, as_line(carried_blocks), spec, tables, True, True).reshape((2, parts // 2) + shape)

time: 81.4 us -> 80.6 us (level)
  starting transfers between devices: 36.2 us -> 34 us
  waiting for transfers between devices: 30 us -> 31.3 us
    ppermute x20, starting transfers between devices: 29.4 us -> 27.2 us  [swapped(): return lax.ppermute(block, 'seq', route)]
    ppermute x20, waiting for transfers between devices: 30 us -> 31.3 us  [swapped(): return lax.ppermute(block, 'seq', route)]
  transfers between devices with their start and end apart: 24 -> 24, of which waited for: 10 -> 11; matrix products, arithmetic and copies ran while one was open for 1% -> 1% of each run, Pallas kernels for 12% -> 12%
where the time goes in v4:
time: 80.6 us; the launch traced here: 80.4 us
  starting transfers between devices  34 us (42%)
  waiting for transfers between devices  31.3 us (39%)
  Pallas kernels  11 us (14%)
  local copies, waits for them, and re-layouts  2.36 us (3%)
  between operations  1.19 us (1%)
    ppermute x20, waiting for transfers between devices, swapped(): return lax.ppermute(block, 'seq', route)  31.3 us
    ppermute x20, starting transfers between devices, swapped(): return lax.ppermute(block, 'seq', route)  27.2 us
    ppermute x1, starting transfers between devices, shift_along(): return lax.ppermute(block, axis, route)  4.87 us
    pallas_call x2, Pallas kernels, through_filter(): pl.pallas_call(functools.partial(product_kernel, conjugate, by_side), out...  3.99 us
    pallas_call x3, Pallas kernels, over_pairs(): pl.pallas_call(kernel, grid_spec=pltpu.PrefetchScalarGridSpec(num_scalar_...  3.28 us
    unnamed x18, local copies, waits for them, and re-layouts  1.95 us
    ppermute x3, starting transfers between devices, summed_over(): lax.ppermute(block, axis, [(i, i ^ apart) for i in range(count)])  1.89 us
  transfers between devices with their start and end apart: 24, of which 11 were waited for; matrix products, arithmetic and copies ran while one was open for 1% of the time, Pallas kernels for 12%

profile of v4, /device:TPU:0, one launch (start us, length us, event | category | flops | bytes accessed | tf_op | source)
XLA Modules:
  0.0 80.4 jit_solution(5100576267177161385)
XLA Ops:
  0.7 1.1 %copy-done.6 = f32[128,1024]{1,0:T(8,128)S(1)} copy-done((f32[128,1024]{1,0:T(8,128)S(1)}, f32[128,1024]{1,0:T(8,128)}, u32[]{:S(2)}) %copy-start.6) | copy-done | bytes 524312
  1.8 0.2 filter_blocks.1
  2.1 4.9 %collective-permute-start = (f32[3,2,1024]{2,1,0:T(2,128)S(1)}, f32[3,2,1024]{2,1,0:T(2,128)S(1)}, u32[]{:S(2)}, u32[]{:S(2)}) collective-permute-start(f32[3,2,1024]{2,1,0:T(2,128)S(1)} %get-tuple-element.77), channel_id=1, source_target_pairs={{0,4},{4,8},{8,12},{12,16},{16,20},{20,24},{24,28},{1,5},{5,9},{9,... | collective-permute-start | bytes 73736 | tf_op jit(solution)/shard_map/ppermute | solution.py:21
  7.0 1.6 %collective-permute-start.7 = (f32[2,128,128]{2,1,0:T(8,128)S(1)}, f32[2,128,128]{2,1,0:T(8,128)S(1)}, u32[]{:S(2)}, u32[]{:S(2)}) collective-permute-start(f32[2,128,128]{2,1,0:T(8,128)S(1)} %get-tuple-element.90), channel_id=1, source_target_pairs={{0,8},{4,12},{8,0},{12,4},{16,24},{20,28},{24,16},{28,20},{1,9},{5... | collective-permute-start | bytes 393224 | tf_op jit(solution)/shard_map/filter_over_2/ppermute | solution.py:517
  8.6 2.5 %collective-permute-start.9 = (f32[2,128,128]{2,1,0:T(8,128)S(1)}, f32[2,128,128]{2,1,0:T(8,128)S(1)}, u32[]{:S(2)}, u32[]{:S(2)}) collective-permute-start(f32[2,128,128]{2,1,0:T(8,128)S(1)} %get-tuple-element.91), channel_id=1, source_target_pairs={{0,24},{4,28},{8,16},{12,20},{16,8},{20,12},{24,0},{28,4},{1,25},{... | collective-permute-start | bytes 393224 | tf_op jit(solution)/shard_map/filter_over_6/ppermute | solution.py:517
  11.1 0.1 collective-permute-start.8
  11.4 0.0 collective-permute-done.before_ref
  11.4 1.2 %short_filters.1 = (f32[2,4,128,128]{3,2,1,0:T(8,128)S(1)}, f32[2,4,128,128]{3,2,1,0:T(8,128)S(1)}) custom-call(s32[1]{0:T(128)} %bitcast.own_ref, bf16[3,128,1024]{2,1,0:T(8,128)(2,1)S(1)} %copy-done, f32[3,2,1024]{2,1,0:T(2,128)S(1)} %collective-permute-done.before_ref, f32[3,3,1024]{2,1,0:T(4,128)S(1)} %copy-done.3, bf16[128,1024]{1,0:T(8,128)(2,1)S(1)} %copy-done.2), custom_call_target="tpu_custom_call" | custom-call | bytes 88560 | tf_op jit(solution)/shard_map/short_filters/pallas_call | solution.py:284
  12.6 1.5 %collective-permute-start.1 = (f32[4,128,128]{2,1,0:T(8,128)S(1)}, f32[4,128,128]{2,1,0:T(8,128)S(1)}, u32[]{:S(2)}, u32[]{:S(2)}) collective-permute-start(f32[4,128,128]{2,1,0:T(8,128)S(1)} %slice_bitcast_fusion), channel_id=1, source_target_pairs={{0,4},{4,0},{8,12},{12,8},{16,20},{20,16},{24,28},{28,24},{1,5},{5... | collective-permute-start | bytes 786440 | tf_op jit(solution)/shard_map/gated_over_1/ppermute | solution.py:517
  14.1 0.0 collective-permute-done.7
  14.2 4.1 %collective-permute-done.9 = f32[2,128,128]{2,1,0:T(8,128)S(1)} collective-permute-done((f32[2,128,128]{2,1,0:T(8,128)S(1)}, f32[2,128,128]{2,1,0:T(8,128)S(1)}, u32[]{:S(2)}, u32[]{:S(2)}) %collective-permute-start.9) | collective-permute-done | bytes 131104 | tf_op jit(solution)/shard_map/filter_over_6/ppermute | solution.py:517
  18.3 4.3 %collective-permute-done.8 = f32[2,128,128]{2,1,0:T(8,128)S(1)} collective-permute-done((f32[2,128,128]{2,1,0:T(8,128)S(1)}, f32[2,128,128]{2,1,0:T(8,128)S(1)}, u32[]{:S(2)}, u32[]{:S(2)}) %collective-permute-start.8) | collective-permute-done | bytes 131104 | tf_op jit(solution)/shard_map/filter_over_4/ppermute | solution.py:517
  22.6 0.9 %collective-permute-start.10 = (f32[4,128,128]{2,1,0:T(8,128)S(1)}, f32[4,128,128]{2,1,0:T(8,128)S(1)}, u32[]{:S(2)}, u32[]{:S(2)}) collective-permute-start(f32[4,128,128]{2,1,0:T(8,128)S(1)} %pad_maximum_fusion.4), channel_id=1, source_target_pairs={{0,4},{4,0},{8,12},{12,8},{16,20},{20,16},{24,28},{28,24},{1,5},{5... | collective-permute-start | bytes 786440 | tf_op jit(solution)/shard_map/filter_over_1/ppermute | solution.py:517
  23.5 0.0 collective-permute-done.1
  23.6 0.1 collective-permute-start.3
  23.7 2.7 %collective-permute-start.5 = (f32[2,128,128]{2,1,0:T(8,128)S(1)}, f32[2,128,128]{2,1,0:T(8,128)S(1)}, u32[]{:S(2)}, u32[]{:S(2)}) collective-permute-start(f32[2,128,128]{2,1,0:T(8,128)S(1)} %pad_maximum_fusion.20), channel_id=1, source_target_pairs={{0,16},{4,20},{8,24},{12,28},{16,0},{20,4},{24,8},{28,12},{1,17},{... | collective-permute-start | bytes 393224 | tf_op jit(solution)/shard_map/gated_over_4/ppermute | solution.py:517
  26.4 1.8 %collective-permute-start.6 = (f32[2,128,128]{2,1,0:T(8,128)S(1)}, f32[2,128,128]{2,1,0:T(8,128)S(1)}, u32[]{:S(2)}, u32[]{:S(2)}) collective-permute-start(f32[2,128,128]{2,1,0:T(8,128)S(1)} %pad_maximum_fusion.21), channel_id=1, source_target_pairs={{0,24},{4,28},{8,16},{12,20},{16,8},{20,12},{24,0},{28,4},{1,25},{... | collective-permute-start | bytes 393224 | tf_op jit(solution)/shard_map/gated_over_6/ppermute | solution.py:517
  28.2 1.2 %collective-permute-start.2 = (f32[576,128]{1,0:T(8,128)S(1)}, f32[576,128]{1,0:T(8,128)S(1)}, u32[]{:S(2)}, u32[]{:S(2)}) collective-permute-start(f32[576,128]{1,0:T(8,128)S(1)} %pad_maximum_fusion.3), channel_id=1, source_target_pairs={{0,4},{4,0},{8,12},{12,8},{16,20},{20,16},{24,28},{28,24},{1,5},{5... | collective-permute-start | bytes 884744 | tf_op jit(solution)/shard_map/carried_over_1/ppermute | solution.py:517
  29.5 1.1 %collective-permute-done.10 = f32[4,128,128]{2,1,0:T(8,128)S(1)} collective-permute-done((f32[4,128,128]{2,1,0:T(8,128)S(1)}, f32[4,128,128]{2,1,0:T(8,128)S(1)}, u32[]{:S(2)}, u32[]{:S(2)}) %collective-permute-start.10) | collective-permute-done | bytes 262176 | tf_op jit(solution)/shard_map/filter_over_1/ppermute | solution.py:517
  30.6 0.0 copy-start.1
  30.6 0.0 copy-start.4
  30.6 0.0 copy-start.5
  30.7 0.8 copy-done.1
  31.5 0.0 copy-done.5
  31.5 1.1 %filter_spectrum.1.spec_ref = f32[9,256,128]{2,1,0:T(8,128)S(1)} custom-call(s32[1]{0:T(128)} %bitcast.own_ref, f32[8,128,128]{2,1,0:T(8,128)S(1)} %bitcast.65, bf16[256,256]{1,0:T(8,128)(2,1)S(1)} %copy-done.1, bf16[256,128]{1,0:T(8,128)(2,1)S(1)} %copy-done.5, f32[128,128]{1,0:T(8,128)S(1)} %copy-done.4), custom_call_target="tpu_custom_call" | custom-call | bytes 4059000 | tf_op jit(solution)/shard_map/filter_spectrum/pallas_call | solution.py:205
  32.6 0.0 collective-permute-done.3
  32.6 3.7 %collective-permute-done.5 = f32[2,128,128]{2,1,0:T(8,128)S(1)} collective-permute-done((f32[2,128,128]{2,1,0:T(8,128)S(1)}, f32[2,128,128]{2,1,0:T(8,128)S(1)}, u32[]{:S(2)}, u32[]{:S(2)}) %collective-permute-start.5) | collective-permute-done | bytes 131104 | tf_op jit(solution)/shard_map/gated_over_4/ppermute | solution.py:517
  36.3 0.0 collective-permute-done.6
  36.4 2.0 %convolution.1 = f32[8,136,128]{2,1,0:T(8,128)S(1)} custom-call(s32[1]{0:T(128)} %bitcast.own_ref, f32[8,128,128]{2,1,0:T(8,128)S(1)} %bitcast.67, f32[9,256,128]{2,1,0:T(8,128)S(1)} %filter_spectrum.1.spec_ref, bf16[256,256]{1,0:T(8,128)(2,1)S(1)} %copy-done.1, bf16[256,128]{1,0:T(8,128)(2,1)S(1)} %copy-done.5, f32[128,128]{1,0:T(8,128)S(1)} %copy-done.4), custom_call_target="tpu_custom_call" | custom-call | bytes 73800000 | tf_op jit(solution)/shard_map/convolution/pallas_call | solution.py:219
  38.4 0.8 %collective-permute-start.11 = (f32[4,136,128]{2,1,0:T(8,128)S(1)}, f32[4,136,128]{2,1,0:T(8,128)S(1)}, u32[]{:S(2)}, u32[]{:S(2)}) collective-permute-start(f32[4,136,128]{2,1,0:T(8,128)S(1)} %slice.340), channel_id=1, source_target_pairs={{0,4},{4,0},{8,12},{12,8},{16,20},{20,16},{24,28},{28,24},{1,5},{5... | collective-permute-start | bytes 835592 | tf_op jit(solution)/shard_map/conv_over_1/ppermute | solution.py:517
  39.3 0.0 collective-permute-done.2
  39.4 2.9 %collective-permute-start.12 = (f32[2,128,128]{2,1,0:T(8,128)S(1)}, f32[2,128,128]{2,1,0:T(8,128)S(1)}, u32[]{:S(2)}, u32[]{:S(2)}) collective-permute-start(f32[2,128,128]{2,1,0:T(8,128)S(1)} %get-tuple-element.47), channel_id=1, source_target_pairs={{0,16},{4,20},{8,24},{12,28},{16,0},{20,4},{24,8},{28,12},{1,17},{... | collective-permute-start | bytes 393224 | tf_op jit(solution)/shard_map/carried_over_4/ppermute | solution.py:517
  42.3 0.1 collective-permute-start.4
  42.5 1.5 %collective-permute-start.13 = (f32[320,128]{1,0:T(8,128)S(1)}, f32[320,128]{1,0:T(8,128)S(1)}, u32[]{:S(2)}, u32[]{:S(2)}) collective-permute-start(f32[320,128]{1,0:T(8,128)S(1)} %get-tuple-element.127), channel_id=1, source_target_pairs={{0,24},{4,28},{8,16},{12,20},{16,8},{20,12},{24,0},{28,4},{1,25},{... | collective-permute-start | bytes 491528 | tf_op jit(solution)/shard_map/carried_over_6/ppermute | solution.py:517
  43.9 1.1 %collective-permute-done.11 = f32[4,136,128]{2,1,0:T(8,128)S(1)} collective-permute-done((f32[4,136,128]{2,1,0:T(8,128)S(1)}, f32[4,136,128]{2,1,0:T(8,128)S(1)}, u32[]{:S(2)}, u32[]{:S(2)}) %collective-permute-start.11) | collective-permute-done | bytes 278560 | tf_op jit(solution)/shard_map/conv_over_1/ppermute | solution.py:517
  45.1 2.4 %collective-permute-start.16 = (f32[2,136,128]{2,1,0:T(8,128)S(1)}, f32[2,136,128]{2,1,0:T(8,128)S(1)}, u32[]{:S(2)}, u32[]{:S(2)}) collective-permute-start(f32[2,136,128]{2,1,0:T(8,128)S(1)} %pad_maximum_fusion.13), channel_id=1, source_target_pairs={{0,8},{4,12},{8,0},{12,4},{16,24},{20,28},{24,16},{28,20},{1,9},{5... | collective-permute-start | bytes 417800 | tf_op jit(solution)/shard_map/conv_over_2/ppermute | solution.py:517
  47.5 2.4 %collective-permute-done.12 = f32[2,128,128]{2,1,0:T(8,128)S(1)} collective-permute-done((f32[2,128,128]{2,1,0:T(8,128)S(1)}, f32[2,128,128]{2,1,0:T(8,128)S(1)}, u32[]{:S(2)}, u32[]{:S(2)}) %collective-permute-start.12) | collective-permute-done | bytes 131104 | tf_op jit(solution)/shard_map/carried_over_4/ppermute | solution.py:517
  49.9 0.0 collective-permute-start.15
  49.9 5.5 %collective-permute-done.13 = f32[320,128]{1,0:T(8,128)S(1)} collective-permute-done((f32[320,128]{1,0:T(8,128)S(1)}, f32[320,128]{1,0:T(8,128)S(1)}, u32[]{:S(2)}, u32[]{:S(2)}) %collective-permute-start.13) | collective-permute-done | bytes 163872 | tf_op jit(solution)/shard_map/carried_over_6/ppermute | solution.py:517
  55.3 0.0 collective-permute-done.4
  55.4 2.0 %correlation.1 = f32[8,136,128]{2,1,0:T(8,128)S(1)} custom-call(s32[1]{0:T(128)} %bitcast.own_ref, f32[8,128,128]{2,1,0:T(8,128)S(1)} %bitcast.66, f32[9,256,128]{2,1,0:T(8,128)S(1)} %filter_spectrum.1.spec_ref, bf16[256,256]{1,0:T(8,128)(2,1)S(1)} %copy-done.1, bf16[256,128]{1,0:T(8,128)(2,1)S(1)} %copy-done.5, f32[128,128]{1,0:T(8,128)S(1)} %copy-done.4), custom_call_target="tpu_custom_call" | custom-call | bytes 184500 | tf_op jit(solution)/shard_map/correlation/pallas_call | solution.py:219
  57.4 0.0 copy-start.7
  57.5 1.3 %collective-permute-start.14 = (f32[4,136,128]{2,1,0:T(8,128)S(1)}, f32[4,136,128]{2,1,0:T(8,128)S(1)}, u32[]{:S(2)}, u32[]{:S(2)}) collective-permute-start(f32[4,136,128]{2,1,0:T(8,128)S(1)} %slice.346), channel_id=1, source_target_pairs={{0,4},{4,0},{8,12},{12,8},{16,20},{20,16},{24,28},{28,24},{1,5},{5... | collective-permute-start | bytes 835592 | tf_op jit(solution)/shard_map/corr_over_1/ppermute | solution.py:517
  58.8 0.0 collective-permute-done.16.refs_1_
  58.9 1.9 %rows_with_rim.1 = (f32[128,1024]{1,0:T(8,128)S(1)}, f32[136,1024]{1,0:T(8,128)S(1)}, f32[136,1024]{1,0:T(8,128)S(1)}, f32[136,1024]{1,0:T(8,128)S(1)}, f32[136,...) custom-call(s32[1]{0:T(128)} %bitcast.own_ref, bf16[3,128,1024]{2,1,0:T(8,128)(2,1)S(1)} %copy-done, ...), custom_call_target="tpu_custom_call" | custom-call | bytes 147600 | tf_op jit(solution)/shard_map/rows_with_rim/pallas_call | solution.py:284
  60.7 3.3 %collective-permute-done.14 = f32[4,136,128]{2,1,0:T(8,128)S(1)} collective-permute-done((f32[4,136,128]{2,1,0:T(8,128)S(1)}, f32[4,136,128]{2,1,0:T(8,128)S(1)}, u32[]{:S(2)}, u32[]{:S(2)}) %collective-permute-start.14) | collective-permute-done | bytes 278560 | tf_op jit(solution)/shard_map/corr_over_1/ppermute | solution.py:517
  64.2 0.0 collective-permute-done.15.refs_2_
  64.2 1.9 %collective-permute-start.17 = (f32[2,136,128]{2,1,0:T(8,128)S(1)}, f32[2,136,128]{2,1,0:T(8,128)S(1)}, u32[]{:S(2)}, u32[]{:S(2)}) collective-permute-start(f32[2,136,128]{2,1,0:T(8,128)S(1)} %pad_maximum_fusion.10), channel_id=1, source_target_pairs={{0,8},{4,12},{8,0},{12,4},{16,24},{20,28},{24,16},{28,20},{1,9},{5... | collective-permute-start | bytes 417800 | tf_op jit(solution)/shard_map/corr_over_2/ppermute | solution.py:517
  66.1 2.1 %collective-permute-start.18 = (f32[2,136,128]{2,1,0:T(8,128)S(1)}, f32[2,136,128]{2,1,0:T(8,128)S(1)}, u32[]{:S(2)}, u32[]{:S(2)}) collective-permute-start(f32[2,136,128]{2,1,0:T(8,128)S(1)} %pad_maximum_fusion.8), channel_id=1, source_target_pairs={{0,24},{4,28},{8,16},{12,20},{16,8},{20,12},{24,0},{28,4},{1,25},{... | collective-permute-start | bytes 417800 | tf_op jit(solution)/shard_map/conv_over_6/ppermute | solution.py:517
  68.2 0.0 collective-permute-start.22
  68.2 1.8 %collective-permute-start.23 = (f32[2,136,128]{2,1,0:T(8,128)S(1)}, f32[2,136,128]{2,1,0:T(8,128)S(1)}, u32[]{:S(2)}, u32[]{:S(2)}) collective-permute-start(f32[2,136,128]{2,1,0:T(8,128)S(1)} %pad_maximum_fusion.12), channel_id=1, source_target_pairs={{0,24},{4,28},{8,16},{12,20},{16,8},{20,12},{24,0},{28,4},{1,25},{... | collective-permute-start | bytes 417800 | tf_op jit(solution)/shard_map/corr_over_6/ppermute | solution.py:517
  69.9 0.7 collective-permute-done.17.refs_1_
  70.7 2.4 %collective-permute-done.18.refs_3_ = f32[2,136,128]{2,1,0:T(8,128)S(1)} collective-permute-done((f32[2,136,128]{2,1,0:T(8,128)S(1)}, f32[2,136,128]{2,1,0:T(8,128)S(1)}, u32[]{:S(2)}, u32[]{:S(2)}) %collective-permute-start.18) | collective-permute-done | bytes 139296 | tf_op jit(solution)/shard_map/conv_over_6/ppermute | solution.py:517
  73.0 0.5 mixed_squares.1
  73.6 0.0 collective-permute-start.21
  73.6 1.6 %collective-permute-start.20 = (f32[1,128]{1,0:T(1,128)S(1)}, f32[1,128]{1,0:T(1,128)S(1)}, u32[]{:S(2)}, u32[]{:S(2)}) collective-permute-start(f32[1,128]{1,0:T(1,128)S(1)} %get-tuple-element.67), channel_id=1, source_target_pairs={{0,2},{1,3},{2,0},{3,1},{4,6},{5,7},{6,4},{7,5},{8,10},{9,11},{10,... | collective-permute-start | bytes 1544 | tf_op jit(solution)/shard_map/squares_over_2/ppermute | solution.py:527
  75.1 0.3 collective-permute-start.19
  75.5 2.7 %collective-permute-done.22.refs_2_ = f32[2,136,128]{2,1,0:T(8,128)S(1)} collective-permute-done((f32[2,136,128]{2,1,0:T(8,128)S(1)}, f32[2,136,128]{2,1,0:T(8,128)S(1)}, u32[]{:S(2)}, u32[]{:S(2)}) %collective-permute-start.22) | collective-permute-done | bytes 139296 | tf_op jit(solution)/shard_map/corr_over_4/ppermute | solution.py:517
  78.1 0.0 collective-permute-done.23.refs_3_
  78.1 1.3 %stream_grads.1 = bf16[3,128,1024]{2,1,0:T(8,128)(2,1)} custom-call(s32[1]{0:T(128)} %bitcast.own_ref, f32[136,1024]{1,0:T(8,128)S(1)} %get-tuple-element.68.key_ref, f32[136,1024]{1,0:T(8,128)S(1)} %get-tuple-element.69.value_ref, f32[136,1024]{1,0:T(8,128)S(1)} %get-tuple-element.70.carried_ref, f32[3,3,1024]{2,1,0:T(4,128)S(1)} %copy-done.3, ...), custom_call_target="tpu_custom_call" | custom-call | bytes 184500 | tf_op jit(solution)/shard_map/stream_grads/pallas_call | solution.py:498
  79.5 0.0 collective-permute-done.21
  79.5 0.0 collective-permute-done.20
  79.5 0.0 collective-permute-done.19
  79.5 0.8 %norm.1 = bf16[128,1024]{1,0:T(8,128)(2,1)} custom-call(f32[128,1024]{1,0:T(8,128)S(1)} %get-tuple-element.66.mixed_ref, f32[1,128]{1,0:T(1,128)S(1)} %add_add_fusion.square_ref, f32[1,1024]{1,0:T(1,128)S(1)} %bitcast.69), custom_call_target="tpu_custom_call" | custom-call | bytes 73800 | tf_op jit(solution)/shard_map/norm/pallas_call | solution.py:467
  (61 shorter events, 0.9 us)
Async XLA Ops:
  0.6 1.4 %copy-start = (bf16[3,128,1024]{2,1,0:T(8,128)(2,1)S(1)}, bf16[3,128,1024]{2,1,0:T(8,128)(2,1)}, u32[]{:S(2)}) copy-start(bf16[3,128,1024]{2,1,0:T(8,128)(2,1)} %streams_ref.3) | copy-start | bytes 2359300
  0.6 10.6 %copy-start.2 = (bf16[128,1024]{1,0:T(8,128)(2,1)S(1)}, bf16[128,1024]{1,0:T(8,128)(2,1)}, u32[]{:S(2)}) copy-start(bf16[128,1024]{1,0:T(8,128)(2,1)} %cot_ref.3) | copy-start | bytes 786436
  0.7 1.1 %copy-start.6 = (f32[128,1024]{1,0:T(8,128)S(1)}, f32[128,1024]{1,0:T(8,128)}, u32[]{:S(2)}) copy-start(f32[128,1024]{1,0:T(8,128)} %x_ref.1) | copy-start | bytes 1572868
  1.8 9.6 %copy-start.3 = (f32[3,3,1024]{2,1,0:T(4,128)S(1)}, f32[3,3,1024]{2,1,0:T(4,128)}, u32[]{:S(2)}) copy-start(f32[3,3,1024]{2,1,0:T(4,128)} %taps_ref.7) | copy-start | bytes 110596
  2.1 9.2 %collective-permute-start = (f32[3,2,1024]{2,1,0:T(2,128)S(1)}, f32[3,2,1024]{2,1,0:T(2,128)S(1)}, u32[]{:S(2)}, u32[]{:S(2)}) collective-permute-start(f32[3,2,1024]{2,1,0:T(2,128)S(1)} %get-tuple-element.77), channel_id=1, source_target_pairs={{0,4},{4,8},{8,12},{12,16},{16,20},{20,24},{24,28},{1,5},{5,9},{9,... | collective-permute-start | bytes 73736 | tf_op jit(solution)/shard_map/ppermute | solution.py:21
  7.0 7.2 %collective-permute-start.7 = (f32[2,128,128]{2,1,0:T(8,128)S(1)}, f32[2,128,128]{2,1,0:T(8,128)S(1)}, u32[]{:S(2)}, u32[]{:S(2)}) collective-permute-start(f32[2,128,128]{2,1,0:T(8,128)S(1)} %get-tuple-element.90), channel_id=1, source_target_pairs={{0,8},{4,12},{8,0},{12,4},{16,24},{20,28},{24,16},{28,20},{1,9},{5... | collective-permute-start | bytes 393224 | tf_op jit(solution)/shard_map/filter_over_2/ppermute | solution.py:517
  8.6 9.6 %collective-permute-start.9 = (f32[2,128,128]{2,1,0:T(8,128)S(1)}, f32[2,128,128]{2,1,0:T(8,128)S(1)}, u32[]{:S(2)}, u32[]{:S(2)}) collective-permute-start(f32[2,128,128]{2,1,0:T(8,128)S(1)} %get-tuple-element.91), channel_id=1, source_target_pairs={{0,24},{4,28},{8,16},{12,20},{16,8},{20,12},{24,0},{28,4},{1,25},{... | collective-permute-start | bytes 393224 | tf_op jit(solution)/shard_map/filter_over_6/ppermute | solution.py:517
  11.1 11.5 %collective-permute-start.8 = (f32[2,128,128]{2,1,0:T(8,128)S(1)}, f32[2,128,128]{2,1,0:T(8,128)S(1)}, u32[]{:S(2)}, u32[]{:S(2)}) collective-permute-start(f32[2,128,128]{2,1,0:T(8,128)S(1)} %get-tuple-element.92), channel_id=1, source_target_pairs={{0,16},{4,20},{8,24},{12,28},{16,0},{20,4},{24,8},{28,12},{1,17},{... | collective-permute-start | bytes 393224 | tf_op jit(solution)/shard_map/filter_over_4/ppermute | solution.py:517
  12.6 10.9 %collective-permute-start.1 = (f32[4,128,128]{2,1,0:T(8,128)S(1)}, f32[4,128,128]{2,1,0:T(8,128)S(1)}, u32[]{:S(2)}, u32[]{:S(2)}) collective-permute-start(f32[4,128,128]{2,1,0:T(8,128)S(1)} %slice_bitcast_fusion), channel_id=1, source_target_pairs={{0,4},{4,0},{8,12},{12,8},{16,20},{20,16},{24,28},{28,24},{1,5},{5... | collective-permute-start | bytes 786440 | tf_op jit(solution)/shard_map/gated_over_1/ppermute | solution.py:517
  22.6 7.9 %collective-permute-start.10 = (f32[4,128,128]{2,1,0:T(8,128)S(1)}, f32[4,128,128]{2,1,0:T(8,128)S(1)}, u32[]{:S(2)}, u32[]{:S(2)}) collective-permute-start(f32[4,128,128]{2,1,0:T(8,128)S(1)} %pad_maximum_fusion.4), channel_id=1, source_target_pairs={{0,4},{4,0},{8,12},{12,8},{16,20},{20,16},{24,28},{28,24},{1,5},{5... | collective-permute-start | bytes 786440 | tf_op jit(solution)/shard_map/filter_over_1/ppermute | solution.py:517
  23.6 9.0 %collective-permute-start.3 = (f32[2,128,128]{2,1,0:T(8,128)S(1)}, f32[2,128,128]{2,1,0:T(8,128)S(1)}, u32[]{:S(2)}, u32[]{:S(2)}) collective-permute-start(f32[2,128,128]{2,1,0:T(8,128)S(1)} %pad_maximum_fusion.19), channel_id=1, source_target_pairs={{0,8},{4,12},{8,0},{12,4},{16,24},{20,28},{24,16},{28,20},{1,9},{5... | collective-permute-start | bytes 393224 | tf_op jit(solution)/shard_map/gated_over_2/ppermute | solution.py:517
  23.7 12.6 %collective-permute-start.5 = (f32[2,128,128]{2,1,0:T(8,128)S(1)}, f32[2,128,128]{2,1,0:T(8,128)S(1)}, u32[]{:S(2)}, u32[]{:S(2)}) collective-permute-start(f32[2,128,128]{2,1,0:T(8,128)S(1)} %pad_maximum_fusion.20), channel_id=1, source_target_pairs={{0,16},{4,20},{8,24},{12,28},{16,0},{20,4},{24,8},{28,12},{1,17},{... | collective-permute-start | bytes 393224 | tf_op jit(solution)/shard_map/gated_over_4/ppermute | solution.py:517
  26.4 9.9 %collective-permute-start.6 = (f32[2,128,128]{2,1,0:T(8,128)S(1)}, f32[2,128,128]{2,1,0:T(8,128)S(1)}, u32[]{:S(2)}, u32[]{:S(2)}) collective-permute-start(f32[2,128,128]{2,1,0:T(8,128)S(1)} %pad_maximum_fusion.21), channel_id=1, source_target_pairs={{0,24},{4,28},{8,16},{12,20},{16,8},{20,12},{24,0},{28,4},{1,25},{... | collective-permute-start | bytes 393224 | tf_op jit(solution)/shard_map/gated_over_6/ppermute | solution.py:517
  28.2 11.0 %collective-permute-start.2 = (f32[576,128]{1,0:T(8,128)S(1)}, f32[576,128]{1,0:T(8,128)S(1)}, u32[]{:S(2)}, u32[]{:S(2)}) collective-permute-start(f32[576,128]{1,0:T(8,128)S(1)} %pad_maximum_fusion.3), channel_id=1, source_target_pairs={{0,4},{4,0},{8,12},{12,8},{16,20},{20,16},{24,28},{28,24},{1,5},{5... | collective-permute-start | bytes 884744 | tf_op jit(solution)/shard_map/carried_over_1/ppermute | solution.py:517
  30.6 0.9 %copy-start.1 = (bf16[256,256]{1,0:T(8,128)(2,1)S(1)}, bf16[256,256]{1,0:T(8,128)(2,1)}, u32[]{:S(2)}) copy-start(bf16[256,256]{1,0:T(8,128)(2,1)} %constant.46.clone.high_ref) | copy-start | bytes 393220
  30.6 0.9 %copy-start.4 = (f32[128,128]{1,0:T(8,128)S(1)}, f32[128,128]{1,0:T(8,128)}, u32[]{:S(2)}) copy-start(f32[128,128]{1,0:T(8,128)} %constant.48.clone.tw_ref) | copy-start | bytes 196612
  30.6 0.9 %copy-start.5 = (bf16[256,128]{1,0:T(8,128)(2,1)S(1)}, bf16[256,128]{1,0:T(8,128)(2,1)}, u32[]{:S(2)}) copy-start(bf16[256,128]{1,0:T(8,128)(2,1)} %constant.47.clone.low_ref) | copy-start | bytes 196612
  38.4 6.6 %collective-permute-start.11 = (f32[4,136,128]{2,1,0:T(8,128)S(1)}, f32[4,136,128]{2,1,0:T(8,128)S(1)}, u32[]{:S(2)}, u32[]{:S(2)}) collective-permute-start(f32[4,136,128]{2,1,0:T(8,128)S(1)} %slice.340), channel_id=1, source_target_pairs={{0,4},{4,0},{8,12},{12,8},{16,20},{20,16},{24,28},{28,24},{1,5},{5... | collective-permute-start | bytes 835592 | tf_op jit(solution)/shard_map/conv_over_1/ppermute | solution.py:517
  39.4 10.5 %collective-permute-start.12 = (f32[2,128,128]{2,1,0:T(8,128)S(1)}, f32[2,128,128]{2,1,0:T(8,128)S(1)}, u32[]{:S(2)}, u32[]{:S(2)}) collective-permute-start(f32[2,128,128]{2,1,0:T(8,128)S(1)} %get-tuple-element.47), channel_id=1, source_target_pairs={{0,16},{4,20},{8,24},{12,28},{16,0},{20,4},{24,8},{28,12},{1,17},{... | collective-permute-start | bytes 393224 | tf_op jit(solution)/shard_map/carried_over_4/ppermute | solution.py:517
  42.3 13.0 %collective-permute-start.4 = (f32[320,128]{1,0:T(8,128)S(1)}, f32[320,128]{1,0:T(8,128)S(1)}, u32[]{:S(2)}, u32[]{:S(2)}) collective-permute-start(f32[320,128]{1,0:T(8,128)S(1)} %get-tuple-element.126), channel_id=1, source_target_pairs={{0,8},{4,12},{8,0},{12,4},{16,24},{20,28},{24,16},{28,20},{1,9},{5... | collective-permute-start | bytes 491528 | tf_op jit(solution)/shard_map/carried_over_2/ppermute | solution.py:517
  42.5 12.9 %collective-permute-start.13 = (f32[320,128]{1,0:T(8,128)S(1)}, f32[320,128]{1,0:T(8,128)S(1)}, u32[]{:S(2)}, u32[]{:S(2)}) collective-permute-start(f32[320,128]{1,0:T(8,128)S(1)} %get-tuple-element.127), channel_id=1, source_target_pairs={{0,24},{4,28},{8,16},{12,20},{16,8},{20,12},{24,0},{28,4},{1,25},{... | collective-permute-start | bytes 491528 | tf_op jit(solution)/shard_map/carried_over_6/ppermute | solution.py:517
  45.1 13.8 %collective-permute-start.16 = (f32[2,136,128]{2,1,0:T(8,128)S(1)}, f32[2,136,128]{2,1,0:T(8,128)S(1)}, u32[]{:S(2)}, u32[]{:S(2)}) collective-permute-start(f32[2,136,128]{2,1,0:T(8,128)S(1)} %pad_maximum_fusion.13), channel_id=1, source_target_pairs={{0,8},{4,12},{8,0},{12,4},{16,24},{20,28},{24,16},{28,20},{1,9},{5... | collective-permute-start | bytes 417800 | tf_op jit(solution)/shard_map/conv_over_2/ppermute | solution.py:517
  49.9 14.3 %collective-permute-start.15 = (f32[2,136,128]{2,1,0:T(8,128)S(1)}, f32[2,136,128]{2,1,0:T(8,128)S(1)}, u32[]{:S(2)}, u32[]{:S(2)}) collective-permute-start(f32[2,136,128]{2,1,0:T(8,128)S(1)} %pad_maximum_fusion.7), channel_id=1, source_target_pairs={{0,16},{4,20},{8,24},{12,28},{16,0},{20,4},{24,8},{28,12},{1,17},{... | collective-permute-start | bytes 417800 | tf_op jit(solution)/shard_map/conv_over_4/ppermute | solution.py:517
  57.4 1.4 %copy-start.7 = (f32[1024]{0:T(1024)S(1)}, f32[1024]{0:T(1024)}, u32[]{:S(2)}) copy-start(f32[1024]{0:T(1024)} %param.12) | copy-start | bytes 12292
  57.5 6.6 %collective-permute-start.14 = (f32[4,136,128]{2,1,0:T(8,128)S(1)}, f32[4,136,128]{2,1,0:T(8,128)S(1)}, u32[]{:S(2)}, u32[]{:S(2)}) collective-permute-start(f32[4,136,128]{2,1,0:T(8,128)S(1)} %slice.346), channel_id=1, source_target_pairs={{0,4},{4,0},{8,12},{12,8},{16,20},{20,16},{24,28},{28,24},{1,5},{5... | collective-permute-start | bytes 835592 | tf_op jit(solution)/shard_map/corr_over_1/ppermute | solution.py:517
  64.2 6.5 %collective-permute-start.17 = (f32[2,136,128]{2,1,0:T(8,128)S(1)}, f32[2,136,128]{2,1,0:T(8,128)S(1)}, u32[]{:S(2)}, u32[]{:S(2)}) collective-permute-start(f32[2,136,128]{2,1,0:T(8,128)S(1)} %pad_maximum_fusion.10), channel_id=1, source_target_pairs={{0,8},{4,12},{8,0},{12,4},{16,24},{20,28},{24,16},{28,20},{1,9},{5... | collective-permute-start | bytes 417800 | tf_op jit(solution)/shard_map/corr_over_2/ppermute | solution.py:517
  66.1 7.0 %collective-permute-start.18 = (f32[2,136,128]{2,1,0:T(8,128)S(1)}, f32[2,136,128]{2,1,0:T(8,128)S(1)}, u32[]{:S(2)}, u32[]{:S(2)}) collective-permute-start(f32[2,136,128]{2,1,0:T(8,128)S(1)} %pad_maximum_fusion.8), channel_id=1, source_target_pairs={{0,24},{4,28},{8,16},{12,20},{16,8},{20,12},{24,0},{28,4},{1,25},{... | collective-permute-start | bytes 417800 | tf_op jit(solution)/shard_map/conv_over_6/ppermute | solution.py:517
  68.2 10.0 %collective-permute-start.22 = (f32[2,136,128]{2,1,0:T(8,128)S(1)}, f32[2,136,128]{2,1,0:T(8,128)S(1)}, u32[]{:S(2)}, u32[]{:S(2)}) collective-permute-start(f32[2,136,128]{2,1,0:T(8,128)S(1)} %pad_maximum_fusion.11), channel_id=1, source_target_pairs={{0,16},{4,20},{8,24},{12,28},{16,0},{20,4},{24,8},{28,12},{1,17},{... | collective-permute-start | bytes 417800 | tf_op jit(solution)/shard_map/corr_over_4/ppermute | solution.py:517
  68.2 10.0 %collective-permute-start.23 = (f32[2,136,128]{2,1,0:T(8,128)S(1)}, f32[2,136,128]{2,1,0:T(8,128)S(1)}, u32[]{:S(2)}, u32[]{:S(2)}) collective-permute-start(f32[2,136,128]{2,1,0:T(8,128)S(1)} %pad_maximum_fusion.12), channel_id=1, source_target_pairs={{0,24},{4,28},{8,16},{12,20},{16,8},{20,12},{24,0},{28,4},{1,25},{... | collective-permute-start | bytes 417800 | tf_op jit(solution)/shard_map/corr_over_6/ppermute | solution.py:517
  73.6 5.9 %collective-permute-start.21 = (f32[1,128]{1,0:T(1,128)S(1)}, f32[1,128]{1,0:T(1,128)S(1)}, u32[]{:S(2)}, u32[]{:S(2)}) collective-permute-start(f32[1,128]{1,0:T(1,128)S(1)} %get-tuple-element.67), channel_id=1, source_target_pairs={{0,3},{1,2},{2,1},{3,0},{4,7},{5,6},{6,5},{7,4},{8,11},{9,10},{10,... | collective-permute-start | bytes 1544 | tf_op jit(solution)/shard_map/squares_over_3/ppermute | solution.py:527
  73.6 5.9 %collective-permute-start.20 = (f32[1,128]{1,0:T(1,128)S(1)}, f32[1,128]{1,0:T(1,128)S(1)}, u32[]{:S(2)}, u32[]{:S(2)}) collective-permute-start(f32[1,128]{1,0:T(1,128)S(1)} %get-tuple-element.67), channel_id=1, source_target_pairs={{0,2},{1,3},{2,0},{3,1},{4,6},{5,7},{6,4},{7,5},{8,10},{9,11},{10,... | collective-permute-start | bytes 1544 | tf_op jit(solution)/shard_map/squares_over_2/ppermute | solution.py:527
  75.1 4.4 %collective-permute-start.19 = (f32[1,128]{1,0:T(1,128)S(1)}, f32[1,128]{1,0:T(1,128)S(1)}, u32[]{:S(2)}, u32[]{:S(2)}) collective-permute-start(f32[1,128]{1,0:T(1,128)S(1)} %get-tuple-element.67), channel_id=1, source_target_pairs={{0,1},{1,0},{2,3},{3,2},{4,5},{5,4},{6,7},{7,6},{8,9},{9,8},{10,11... | collective-permute-start | bytes 1544 | tf_op jit(solution)/shard_map/squares_over_1/ppermute | solution.py:527
  78.1 1.4 %copy-start.8 = (f32[1024]{0:T(1024)S(1)}, f32[1024]{0:T(1024)}, u32[]{:S(2)}) copy-start(f32[1024]{0:T(1024)} %param.13) | copy-start | bytes 12292

commit v5 on v4

--- a/solution.py
+++ b/solution.py
@@ -300,16 +300,32 @@
     return slice(part * block, (part + 1) * block)
 
 
-def arrange_kernel(own_ref, x_ref, out_ref):
-    block = out_ref.shape[3]
-    for part in range(2):
-        out_ref[0, place_of_part(own_ref, part)] = x_ref[:, lanes_of(part, block)]
-
-
-def arrange(own, x, parts, specs):
+def arrange_kernel(own_ref, x_ref, out_ref, sems):
+    blocks, _, block = out_ref.shape
+    copies = [
+        pltpu.make_async_copy(x_ref.at[:, lanes_of(part, block)], out_ref.at[part ^ own_ref[0]], sems.at[part])
+        for part in range(blocks)
+    ]
+    for copy in copies:
+        copy.start()
+    for copy in copies:
+        copy.wait()
+
+
+def arrange(own, x, parts):
     rows, width = x.shape
-    out = jax.ShapeDtypeStruct((parts // 2, 2, rows, width // parts), F32)
-    return over_pairs(arrange_kernel, own, parts, specs, ["flat"], ["by_pair"], [out], [x], "filter_blocks", 0.3)[0]
+    block = width // parts
+    blocks = pl.pallas_call(
+        arrange_kernel,
+        in_specs=[pl.BlockSpec(memory_space=pltpu.SMEM), pl.BlockSpec(memory_space=pl.ANY)],
+        out_specs=pl.BlockSpec(memory_space=pl.ANY),
+        out_shape=jax.ShapeDtypeStruct((parts, rows, block), F32),
+        scratch_shapes=[pltpu.SemaphoreType.DMA((parts,))],
+        compiler_params=pltpu.CompilerParams(vmem_limit_bytes=24 * 1024 * 1024),
+        cost_estimate=measured(0.02),
+        name="filter_blocks",
+    )(own, x)
+    return blocks.reshape(parts // 2, 2, rows, block)
 
 
 def shorts_of(streams_ref, before_ref, taps_ref, lanes):
@@ -453,13 +469,20 @@
     )(own, query, cotangent, gated, taps, *conv)
 
 
-def norm_kernel(channels, mixed_ref, square_ref, gain_ref, normed_ref):
+def norm_kernel(channels, mixed_ref, square_ref, gain_ref, normed_ref, sent_ref, sems):
     rows, width = mixed_ref.shape
     squares = jnp.broadcast_to(square_ref[...], (128, rows)).T
     scaling = lax.rsqrt(squares / channels + 1e-06)
+    copies = []
     for start in range(0, width, 128):
         lanes = slice(start, start + 128)
-        normed_ref[:, lanes] = (mixed_ref[:, lanes] * scaling * gain_ref[:, lanes]).astype(BF16)
+        sent_ref[:, lanes] = (mixed_ref[:, lanes] * scaling * gain_ref[:, lanes]).astype(BF16)
+        copies.append(
+            pltpu.make_async_copy(sent_ref.at[:, lanes], normed_ref.at[:, lanes], sems.at[start // 128])
+        )
+        copies[-1].start()
+    for copy in copies:
+        copy.wait()
 
 
 def norm(channels, mixed, squares, gain):
@@ -467,6 +490,8 @@
     return pl.pallas_call(
         functools.partial(norm_kernel, float(channels)),
         out_shape=jax.ShapeDtypeStruct((rows, width), BF16),
+        out_specs=pl.BlockSpec(memory_space=pl.ANY),
+        scratch_shapes=[pltpu.VMEM((rows, width), BF16), pltpu.SemaphoreType.DMA((width // 128,))],
         compiler_params=params(),
         cost_estimate=measured(0.02),
         name="norm",
@@ -589,7 +614,7 @@
     own = lax.axis_index("seq").astype(jnp.int32)[None]
     bias, gain = skip_bias[None], norm_gain[None]
 
-    filter_sent = arrange(own, long_filter, parts, specs)
+    filter_sent = arrange(own, long_filter, parts)
     filter_got = between_pairs("filter", filter_sent)
     streams_later, filter_got[0] = tied(streams, filter_got[0])
     before = shift_along(streams_later[:, rows - rim :].astype(F32), "seq", 1)

time: 80.6 us -> 80.5 us (level)
    pallas_call x3 -> x2, Pallas kernels: 3.28 us -> 3.04 us  [over_pairs(): pl.pallas_call(kernel, grid_spec=pltpu.PrefetchScalarGridSpec(num_scalar_...]
where the time goes in v5:
time: 80.5 us; the launch traced here: 80.3 us
  starting transfers between devices  34 us (42%)
  waiting for transfers between devices  31.3 us (39%)
  Pallas kernels  11 us (14%)
  local copies, waits for them, and re-layouts  2.36 us (3%)
  between operations  1.19 us (1%)
    ppermute x20, waiting for transfers between devices, swapped(): return lax.ppermute(block, 'seq', route)  31.3 us
    ppermute x20, starting transfers between devices, swapped(): return lax.ppermute(block, 'seq', route)  27.2 us
    ppermute x1, starting transfers between devices, shift_along(): return lax.ppermute(block, axis, route)  4.87 us
    pallas_call x2, Pallas kernels, through_filter(): pl.pallas_call(functools.partial(product_kernel, conjugate, by_side), out...  3.99 us
    pallas_call x2, Pallas kernels, over_pairs(): pl.pallas_call(kernel, grid_spec=pltpu.PrefetchScalarGridSpec(num_scalar_...  3.04 us
    unnamed x18, local copies, waits for them, and re-layouts  1.95 us
    ppermute x3, starting transfers between devices, summed_over(): lax.ppermute(block, axis, [(i, i ^ apart) for i in range(count)])  1.89 us
  transfers between devices with their start and end apart: 24, of which 11 were waited for; matrix products, arithmetic and copies ran while one was open for 1% of the time, Pallas kernels for 12%

profile of v5, /device:TPU:0, one launch (start us, length us, event | category | flops | bytes accessed | tf_op | source)
XLA Modules:
  0.0 80.3 jit_solution(8876602440788417128)
XLA Ops:
  0.7 1.1 %copy-done.6 = f32[128,1024]{1,0:T(8,128)S(1)} copy-done((f32[128,1024]{1,0:T(8,128)S(1)}, f32[128,1024]{1,0:T(8,128)}, u32[]{:S(2)}) %copy-start.6) | copy-done | bytes 524312
  1.8 0.2 filter_blocks.1
  2.0 4.9 %collective-permute-start = (f32[3,2,1024]{2,1,0:T(2,128)S(1)}, f32[3,2,1024]{2,1,0:T(2,128)S(1)}, u32[]{:S(2)}, u32[]{:S(2)}) collective-permute-start(f32[3,2,1024]{2,1,0:T(2,128)S(1)} %get-tuple-element.77), channel_id=1, source_target_pairs={{0,4},{4,8},{8,12},{12,16},{16,20},{20,24},{24,28},{1,5},{5,9},{9,... | collective-permute-start | bytes 73736 | tf_op jit(solution)/shard_map/ppermute | solution.py:21
  6.9 1.6 %collective-permute-start.7 = (f32[2,128,128]{2,1,0:T(8,128)S(1)}, f32[2,128,128]{2,1,0:T(8,128)S(1)}, u32[]{:S(2)}, u32[]{:S(2)}) collective-permute-start(f32[2,128,128]{2,1,0:T(8,128)S(1)} %get-tuple-element.90), channel_id=1, source_target_pairs={{0,8},{4,12},{8,0},{12,4},{16,24},{20,28},{24,16},{28,20},{1,9},{5... | collective-permute-start | bytes 393224 | tf_op jit(solution)/shard_map/filter_over_2/ppermute | solution.py:542
  8.6 2.5 %collective-permute-start.9 = (f32[2,128,128]{2,1,0:T(8,128)S(1)}, f32[2,128,128]{2,1,0:T(8,128)S(1)}, u32[]{:S(2)}, u32[]{:S(2)}) collective-permute-start(f32[2,128,128]{2,1,0:T(8,128)S(1)} %get-tuple-element.91), channel_id=1, source_target_pairs={{0,24},{4,28},{8,16},{12,20},{16,8},{20,12},{24,0},{28,4},{1,25},{... | collective-permute-start | bytes 393224 | tf_op jit(solution)/shard_map/filter_over_6/ppermute | solution.py:542
  11.0 0.1 collective-permute-start.8
  11.3 0.0 collective-permute-done.before_ref
  11.3 1.2 %short_filters.1 = (f32[2,4,128,128]{3,2,1,0:T(8,128)S(1)}, f32[2,4,128,128]{3,2,1,0:T(8,128)S(1)}) custom-call(s32[1]{0:T(128)} %bitcast.own_ref, bf16[3,128,1024]{2,1,0:T(8,128)(2,1)S(1)} %copy-done, f32[3,2,1024]{2,1,0:T(2,128)S(1)} %collective-permute-done.before_ref, f32[3,3,1024]{2,1,0:T(4,128)S(1)} %copy-done.3, bf16[128,1024]{1,0:T(8,128)(2,1)S(1)} %copy-done.2), custom_call_target="tpu_custom_call" | custom-call | bytes 88560 | tf_op jit(solution)/shard_map/short_filters/pallas_call | solution.py:284
  12.6 1.5 %collective-permute-start.1 = (f32[4,128,128]{2,1,0:T(8,128)S(1)}, f32[4,128,128]{2,1,0:T(8,128)S(1)}, u32[]{:S(2)}, u32[]{:S(2)}) collective-permute-start(f32[4,128,128]{2,1,0:T(8,128)S(1)} %slice_bitcast_fusion), channel_id=1, source_target_pairs={{0,4},{4,0},{8,12},{12,8},{16,20},{20,16},{24,28},{28,24},{1,5},{5... | collective-permute-start | bytes 786440 | tf_op jit(solution)/shard_map/gated_over_1/ppermute | solution.py:542
  14.1 0.0 collective-permute-done.7
  14.1 4.1 %collective-permute-done.9 = f32[2,128,128]{2,1,0:T(8,128)S(1)} collective-permute-done((f32[2,128,128]{2,1,0:T(8,128)S(1)}, f32[2,128,128]{2,1,0:T(8,128)S(1)}, u32[]{:S(2)}, u32[]{:S(2)}) %collective-permute-start.9) | collective-permute-done | bytes 131104 | tf_op jit(solution)/shard_map/filter_over_6/ppermute | solution.py:542
  18.2 4.3 %collective-permute-done.8 = f32[2,128,128]{2,1,0:T(8,128)S(1)} collective-permute-done((f32[2,128,128]{2,1,0:T(8,128)S(1)}, f32[2,128,128]{2,1,0:T(8,128)S(1)}, u32[]{:S(2)}, u32[]{:S(2)}) %collective-permute-start.8) | collective-permute-done | bytes 131104 | tf_op jit(solution)/shard_map/filter_over_4/ppermute | solution.py:542
  22.6 0.9 %collective-permute-start.10 = (f32[4,128,128]{2,1,0:T(8,128)S(1)}, f32[4,128,128]{2,1,0:T(8,128)S(1)}, u32[]{:S(2)}, u32[]{:S(2)}) collective-permute-start(f32[4,128,128]{2,1,0:T(8,128)S(1)} %pad_maximum_fusion.4), channel_id=1, source_target_pairs={{0,4},{4,0},{8,12},{12,8},{16,20},{20,16},{24,28},{28,24},{1,5},{5... | collective-permute-start | bytes 786440 | tf_op jit(solution)/shard_map/filter_over_1/ppermute | solution.py:542
  23.5 0.0 collective-permute-done.1
  23.5 0.1 collective-permute-start.3
  23.6 2.7 %collective-permute-start.5 = (f32[2,128,128]{2,1,0:T(8,128)S(1)}, f32[2,128,128]{2,1,0:T(8,128)S(1)}, u32[]{:S(2)}, u32[]{:S(2)}) collective-permute-start(f32[2,128,128]{2,1,0:T(8,128)S(1)} %pad_maximum_fusion.20), channel_id=1, source_target_pairs={{0,16},{4,20},{8,24},{12,28},{16,0},{20,4},{24,8},{28,12},{1,17},{... | collective-permute-start | bytes 393224 | tf_op jit(solution)/shard_map/gated_over_4/ppermute | solution.py:542
  26.3 1.8 %collective-permute-start.6 = (f32[2,128,128]{2,1,0:T(8,128)S(1)}, f32[2,128,128]{2,1,0:T(8,128)S(1)}, u32[]{:S(2)}, u32[]{:S(2)}) collective-permute-start(f32[2,128,128]{2,1,0:T(8,128)S(1)} %pad_maximum_fusion.21), channel_id=1, source_target_pairs={{0,24},{4,28},{8,16},{12,20},{16,8},{20,12},{24,0},{28,4},{1,25},{... | collective-permute-start | bytes 393224 | tf_op jit(solution)/shard_map/gated_over_6/ppermute | solution.py:542
  28.1 1.2 %collective-permute-start.2 = (f32[576,128]{1,0:T(8,128)S(1)}, f32[576,128]{1,0:T(8,128)S(1)}, u32[]{:S(2)}, u32[]{:S(2)}) collective-permute-start(f32[576,128]{1,0:T(8,128)S(1)} %pad_maximum_fusion.3), channel_id=1, source_target_pairs={{0,4},{4,0},{8,12},{12,8},{16,20},{20,16},{24,28},{28,24},{1,5},{5... | collective-permute-start | bytes 884744 | tf_op jit(solution)/shard_map/carried_over_1/ppermute | solution.py:542
  29.4 1.1 %collective-permute-done.10 = f32[4,128,128]{2,1,0:T(8,128)S(1)} collective-permute-done((f32[4,128,128]{2,1,0:T(8,128)S(1)}, f32[4,128,128]{2,1,0:T(8,128)S(1)}, u32[]{:S(2)}, u32[]{:S(2)}) %collective-permute-start.10) | collective-permute-done | bytes 262176 | tf_op jit(solution)/shard_map/filter_over_1/ppermute | solution.py:542
  30.5 0.0 copy-start.1
  30.5 0.0 copy-start.4
  30.5 0.0 copy-start.5
  30.7 0.8 copy-done.1
  31.4 0.0 copy-done.5
  31.5 1.1 %filter_spectrum.1.spec_ref = f32[9,256,128]{2,1,0:T(8,128)S(1)} custom-call(s32[1]{0:T(128)} %bitcast.own_ref, f32[8,128,128]{2,1,0:T(8,128)S(1)} %bitcast.57, bf16[256,256]{1,0:T(8,128)(2,1)S(1)} %copy-done.1, bf16[256,128]{1,0:T(8,128)(2,1)S(1)} %copy-done.5, f32[128,128]{1,0:T(8,128)S(1)} %copy-done.4), custom_call_target="tpu_custom_call" | custom-call | bytes 4059000 | tf_op jit(solution)/shard_map/filter_spectrum/pallas_call | solution.py:205
  32.5 0.0 collective-permute-done.3
  32.5 3.7 %collective-permute-done.5 = f32[2,128,128]{2,1,0:T(8,128)S(1)} collective-permute-done((f32[2,128,128]{2,1,0:T(8,128)S(1)}, f32[2,128,128]{2,1,0:T(8,128)S(1)}, u32[]{:S(2)}, u32[]{:S(2)}) %collective-permute-start.5) | collective-permute-done | bytes 131104 | tf_op jit(solution)/shard_map/gated_over_4/ppermute | solution.py:542
  36.3 0.0 collective-permute-done.6
  36.3 2.0 %convolution.1 = f32[8,136,128]{2,1,0:T(8,128)S(1)} custom-call(s32[1]{0:T(128)} %bitcast.own_ref, f32[8,128,128]{2,1,0:T(8,128)S(1)} %bitcast.59, f32[9,256,128]{2,1,0:T(8,128)S(1)} %filter_spectrum.1.spec_ref, bf16[256,256]{1,0:T(8,128)(2,1)S(1)} %copy-done.1, bf16[256,128]{1,0:T(8,128)(2,1)S(1)} %copy-done.5, f32[128,128]{1,0:T(8,128)S(1)} %copy-done.4), custom_call_target="tpu_custom_call" | custom-call | bytes 73800000 | tf_op jit(solution)/shard_map/convolution/pallas_call | solution.py:219
  38.3 0.8 %collective-permute-start.11 = (f32[4,136,128]{2,1,0:T(8,128)S(1)}, f32[4,136,128]{2,1,0:T(8,128)S(1)}, u32[]{:S(2)}, u32[]{:S(2)}) collective-permute-start(f32[4,136,128]{2,1,0:T(8,128)S(1)} %slice.344), channel_id=1, source_target_pairs={{0,4},{4,0},{8,12},{12,8},{16,20},{20,16},{24,28},{28,24},{1,5},{5... | collective-permute-start | bytes 835592 | tf_op jit(solution)/shard_map/conv_over_1/ppermute | solution.py:542
  39.2 0.0 collective-permute-done.2
  39.3 2.9 %collective-permute-start.12 = (f32[2,128,128]{2,1,0:T(8,128)S(1)}, f32[2,128,128]{2,1,0:T(8,128)S(1)}, u32[]{:S(2)}, u32[]{:S(2)}) collective-permute-start(f32[2,128,128]{2,1,0:T(8,128)S(1)} %get-tuple-element.47), channel_id=1, source_target_pairs={{0,16},{4,20},{8,24},{12,28},{16,0},{20,4},{24,8},{28,12},{1,17},{... | collective-permute-start | bytes 393224 | tf_op jit(solution)/shard_map/carried_over_4/ppermute | solution.py:542
  42.3 0.1 collective-permute-start.4
  42.4 1.5 %collective-permute-start.13 = (f32[320,128]{1,0:T(8,128)S(1)}, f32[320,128]{1,0:T(8,128)S(1)}, u32[]{:S(2)}, u32[]{:S(2)}) collective-permute-start(f32[320,128]{1,0:T(8,128)S(1)} %get-tuple-element.127), channel_id=1, source_target_pairs={{0,24},{4,28},{8,16},{12,20},{16,8},{20,12},{24,0},{28,4},{1,25},{... | collective-permute-start | bytes 491528 | tf_op jit(solution)/shard_map/carried_over_6/ppermute | solution.py:542
  43.8 1.1 %collective-permute-done.11 = f32[4,136,128]{2,1,0:T(8,128)S(1)} collective-permute-done((f32[4,136,128]{2,1,0:T(8,128)S(1)}, f32[4,136,128]{2,1,0:T(8,128)S(1)}, u32[]{:S(2)}, u32[]{:S(2)}) %collective-permute-start.11) | collective-permute-done | bytes 278560 | tf_op jit(solution)/shard_map/conv_over_1/ppermute | solution.py:542
  45.0 2.4 %collective-permute-start.16 = (f32[2,136,128]{2,1,0:T(8,128)S(1)}, f32[2,136,128]{2,1,0:T(8,128)S(1)}, u32[]{:S(2)}, u32[]{:S(2)}) collective-permute-start(f32[2,136,128]{2,1,0:T(8,128)S(1)} %pad_maximum_fusion.13), channel_id=1, source_target_pairs={{0,8},{4,12},{8,0},{12,4},{16,24},{20,28},{24,16},{28,20},{1,9},{5... | collective-permute-start | bytes 417800 | tf_op jit(solution)/shard_map/conv_over_2/ppermute | solution.py:542
  47.4 2.4 %collective-permute-done.12 = f32[2,128,128]{2,1,0:T(8,128)S(1)} collective-permute-done((f32[2,128,128]{2,1,0:T(8,128)S(1)}, f32[2,128,128]{2,1,0:T(8,128)S(1)}, u32[]{:S(2)}, u32[]{:S(2)}) %collective-permute-start.12) | collective-permute-done | bytes 131104 | tf_op jit(solution)/shard_map/carried_over_4/ppermute | solution.py:542
  49.8 0.0 collective-permute-start.15
  49.8 5.5 %collective-permute-done.13 = f32[320,128]{1,0:T(8,128)S(1)} collective-permute-done((f32[320,128]{1,0:T(8,128)S(1)}, f32[320,128]{1,0:T(8,128)S(1)}, u32[]{:S(2)}, u32[]{:S(2)}) %collective-permute-start.13) | collective-permute-done | bytes 163872 | tf_op jit(solution)/shard_map/carried_over_6/ppermute | solution.py:542
  55.3 0.0 collective-permute-done.4
  55.3 2.0 %correlation.1 = f32[8,136,128]{2,1,0:T(8,128)S(1)} custom-call(s32[1]{0:T(128)} %bitcast.own_ref, f32[8,128,128]{2,1,0:T(8,128)S(1)} %bitcast.58, f32[9,256,128]{2,1,0:T(8,128)S(1)} %filter_spectrum.1.spec_ref, bf16[256,256]{1,0:T(8,128)(2,1)S(1)} %copy-done.1, bf16[256,128]{1,0:T(8,128)(2,1)S(1)} %copy-done.5, f32[128,128]{1,0:T(8,128)S(1)} %copy-done.4), custom_call_target="tpu_custom_call" | custom-call | bytes 184500 | tf_op jit(solution)/shard_map/correlation/pallas_call | solution.py:219
  57.3 0.0 copy-start.7
  57.4 1.3 %collective-permute-start.14 = (f32[4,136,128]{2,1,0:T(8,128)S(1)}, f32[4,136,128]{2,1,0:T(8,128)S(1)}, u32[]{:S(2)}, u32[]{:S(2)}) collective-permute-start(f32[4,136,128]{2,1,0:T(8,128)S(1)} %slice.350), channel_id=1, source_target_pairs={{0,4},{4,0},{8,12},{12,8},{16,20},{20,16},{24,28},{28,24},{1,5},{5... | collective-permute-start | bytes 835592 | tf_op jit(solution)/shard_map/corr_over_1/ppermute | solution.py:542
  58.8 0.0 collective-permute-done.16.refs_1_
  58.8 1.9 %rows_with_rim.1 = (f32[128,1024]{1,0:T(8,128)S(1)}, f32[136,1024]{1,0:T(8,128)S(1)}, f32[136,1024]{1,0:T(8,128)S(1)}, f32[136,1024]{1,0:T(8,128)S(1)}, f32[136,...) custom-call(s32[1]{0:T(128)} %bitcast.own_ref, bf16[3,128,1024]{2,1,0:T(8,128)(2,1)S(1)} %copy-done, ...), custom_call_target="tpu_custom_call" | custom-call | bytes 147600 | tf_op jit(solution)/shard_map/rows_with_rim/pallas_call | solution.py:284
  60.7 3.3 %collective-permute-done.14 = f32[4,136,128]{2,1,0:T(8,128)S(1)} collective-permute-done((f32[4,136,128]{2,1,0:T(8,128)S(1)}, f32[4,136,128]{2,1,0:T(8,128)S(1)}, u32[]{:S(2)}, u32[]{:S(2)}) %collective-permute-start.14) | collective-permute-done | bytes 278560 | tf_op jit(solution)/shard_map/corr_over_1/ppermute | solution.py:542
  64.1 0.0 collective-permute-done.15.refs_2_
  64.1 1.9 %collective-permute-start.17 = (f32[2,136,128]{2,1,0:T(8,128)S(1)}, f32[2,136,128]{2,1,0:T(8,128)S(1)}, u32[]{:S(2)}, u32[]{:S(2)}) collective-permute-start(f32[2,136,128]{2,1,0:T(8,128)S(1)} %pad_maximum_fusion.10), channel_id=1, source_target_pairs={{0,8},{4,12},{8,0},{12,4},{16,24},{20,28},{24,16},{28,20},{1,9},{5... | collective-permute-start | bytes 417800 | tf_op jit(solution)/shard_map/corr_over_2/ppermute | solution.py:542
  66.0 2.1 %collective-permute-start.18 = (f32[2,136,128]{2,1,0:T(8,128)S(1)}, f32[2,136,128]{2,1,0:T(8,128)S(1)}, u32[]{:S(2)}, u32[]{:S(2)}) collective-permute-start(f32[2,136,128]{2,1,0:T(8,128)S(1)} %pad_maximum_fusion.8), channel_id=1, source_target_pairs={{0,24},{4,28},{8,16},{12,20},{16,8},{20,12},{24,0},{28,4},{1,25},{... | collective-permute-start | bytes 417800 | tf_op jit(solution)/shard_map/conv_over_6/ppermute | solution.py:542
  68.1 0.0 collective-permute-start.22
  68.1 1.8 %collective-permute-start.23 = (f32[2,136,128]{2,1,0:T(8,128)S(1)}, f32[2,136,128]{2,1,0:T(8,128)S(1)}, u32[]{:S(2)}, u32[]{:S(2)}) collective-permute-start(f32[2,136,128]{2,1,0:T(8,128)S(1)} %pad_maximum_fusion.12), channel_id=1, source_target_pairs={{0,24},{4,28},{8,16},{12,20},{16,8},{20,12},{24,0},{28,4},{1,25},{... | collective-permute-start | bytes 417800 | tf_op jit(solution)/shard_map/corr_over_6/ppermute | solution.py:542
  69.9 0.7 collective-permute-done.17.refs_1_
  70.6 2.4 %collective-permute-done.18.refs_3_ = f32[2,136,128]{2,1,0:T(8,128)S(1)} collective-permute-done((f32[2,136,128]{2,1,0:T(8,128)S(1)}, f32[2,136,128]{2,1,0:T(8,128)S(1)}, u32[]{:S(2)}, u32[]{:S(2)}) %collective-permute-start.18) | collective-permute-done | bytes 139296 | tf_op jit(solution)/shard_map/conv_over_6/ppermute | solution.py:542
  73.0 0.5 mixed_squares.1
  73.5 0.0 collective-permute-start.21
  73.5 1.6 %collective-permute-start.20 = (f32[1,128]{1,0:T(1,128)S(1)}, f32[1,128]{1,0:T(1,128)S(1)}, u32[]{:S(2)}, u32[]{:S(2)}) collective-permute-start(f32[1,128]{1,0:T(1,128)S(1)} %get-tuple-element.67), channel_id=1, source_target_pairs={{0,2},{1,3},{2,0},{3,1},{4,6},{5,7},{6,4},{7,5},{8,10},{9,11},{10,... | collective-permute-start | bytes 1544 | tf_op jit(solution)/shard_map/squares_over_2/ppermute | solution.py:552
  75.0 0.3 collective-permute-start.19
  75.4 2.7 %collective-permute-done.22.refs_2_ = f32[2,136,128]{2,1,0:T(8,128)S(1)} collective-permute-done((f32[2,136,128]{2,1,0:T(8,128)S(1)}, f32[2,136,128]{2,1,0:T(8,128)S(1)}, u32[]{:S(2)}, u32[]{:S(2)}) %collective-permute-start.22) | collective-permute-done | bytes 139296 | tf_op jit(solution)/shard_map/corr_over_4/ppermute | solution.py:542
  78.1 0.0 collective-permute-done.23.refs_3_
  78.1 1.3 %stream_grads.1 = bf16[3,128,1024]{2,1,0:T(8,128)(2,1)} custom-call(s32[1]{0:T(128)} %bitcast.own_ref, f32[136,1024]{1,0:T(8,128)S(1)} %get-tuple-element.68.key_ref, f32[136,1024]{1,0:T(8,128)S(1)} %get-tuple-element.69.value_ref, f32[136,1024]{1,0:T(8,128)S(1)} %get-tuple-element.70.carried_ref, f32[3,3,1024]{2,1,0:T(4,128)S(1)} %copy-done.3, ...), custom_call_target="tpu_custom_call" | custom-call | bytes 184500 | tf_op jit(solution)/shard_map/stream_grads/pallas_call | solution.py:523
  79.4 0.0 collective-permute-done.21
  79.4 0.0 collective-permute-done.20
  79.4 0.0 collective-permute-done.19
  79.4 0.9 %norm.1 = bf16[128,1024]{1,0:T(8,128)(2,1)} custom-call(f32[128,1024]{1,0:T(8,128)S(1)} %get-tuple-element.66.mixed_ref, f32[1,128]{1,0:T(1,128)S(1)} %add_add_fusion.square_ref, f32[1,1024]{1,0:T(1,128)S(1)} %bitcast.61), custom_call_target="tpu_custom_call" | custom-call | bytes 73800 | tf_op jit(solution)/shard_map/norm/pallas_call | solution.py:490
  (61 shorter events, 0.9 us)
Async XLA Ops:
  0.6 1.4 %copy-start = (bf16[3,128,1024]{2,1,0:T(8,128)(2,1)S(1)}, bf16[3,128,1024]{2,1,0:T(8,128)(2,1)}, u32[]{:S(2)}) copy-start(bf16[3,128,1024]{2,1,0:T(8,128)(2,1)} %streams_ref.3) | copy-start | bytes 2359300
  0.6 10.5 %copy-start.2 = (bf16[128,1024]{1,0:T(8,128)(2,1)S(1)}, bf16[128,1024]{1,0:T(8,128)(2,1)}, u32[]{:S(2)}) copy-start(bf16[128,1024]{1,0:T(8,128)(2,1)} %cot_ref.3) | copy-start | bytes 786436
  0.7 1.1 %copy-start.6 = (f32[128,1024]{1,0:T(8,128)S(1)}, f32[128,1024]{1,0:T(8,128)}, u32[]{:S(2)}) copy-start(f32[128,1024]{1,0:T(8,128)} %x_ref.1) | copy-start | bytes 1572868
  1.8 9.5 %copy-start.3 = (f32[3,3,1024]{2,1,0:T(4,128)S(1)}, f32[3,3,1024]{2,1,0:T(4,128)}, u32[]{:S(2)}) copy-start(f32[3,3,1024]{2,1,0:T(4,128)} %taps_ref.7) | copy-start | bytes 110596
  2.0 9.2 %collective-permute-start = (f32[3,2,1024]{2,1,0:T(2,128)S(1)}, f32[3,2,1024]{2,1,0:T(2,128)S(1)}, u32[]{:S(2)}, u32[]{:S(2)}) collective-permute-start(f32[3,2,1024]{2,1,0:T(2,128)S(1)} %get-tuple-element.77), channel_id=1, source_target_pairs={{0,4},{4,8},{8,12},{12,16},{16,20},{20,24},{24,28},{1,5},{5,9},{9,... | collective-permute-start | bytes 73736 | tf_op jit(solution)/shard_map/ppermute | solution.py:21
  6.9 7.2 %collective-permute-start.7 = (f32[2,128,128]{2,1,0:T(8,128)S(1)}, f32[2,128,128]{2,1,0:T(8,128)S(1)}, u32[]{:S(2)}, u32[]{:S(2)}) collective-permute-start(f32[2,128,128]{2,1,0:T(8,128)S(1)} %get-tuple-element.90), channel_id=1, source_target_pairs={{0,8},{4,12},{8,0},{12,4},{16,24},{20,28},{24,16},{28,20},{1,9},{5... | collective-permute-start | bytes 393224 | tf_op jit(solution)/shard_map/filter_over_2/ppermute | solution.py:542
  8.6 9.6 %collective-permute-start.9 = (f32[2,128,128]{2,1,0:T(8,128)S(1)}, f32[2,128,128]{2,1,0:T(8,128)S(1)}, u32[]{:S(2)}, u32[]{:S(2)}) collective-permute-start(f32[2,128,128]{2,1,0:T(8,128)S(1)} %get-tuple-element.91), channel_id=1, source_target_pairs={{0,24},{4,28},{8,16},{12,20},{16,8},{20,12},{24,0},{28,4},{1,25},{... | collective-permute-start | bytes 393224 | tf_op jit(solution)/shard_map/filter_over_6/ppermute | solution.py:542
  11.0 11.5 %collective-permute-start.8 = (f32[2,128,128]{2,1,0:T(8,128)S(1)}, f32[2,128,128]{2,1,0:T(8,128)S(1)}, u32[]{:S(2)}, u32[]{:S(2)}) collective-permute-start(f32[2,128,128]{2,1,0:T(8,128)S(1)} %get-tuple-element.92), channel_id=1, source_target_pairs={{0,16},{4,20},{8,24},{12,28},{16,0},{20,4},{24,8},{28,12},{1,17},{... | collective-permute-start | bytes 393224 | tf_op jit(solution)/shard_map/filter_over_4/ppermute | solution.py:542
  12.6 10.9 %collective-permute-start.1 = (f32[4,128,128]{2,1,0:T(8,128)S(1)}, f32[4,128,128]{2,1,0:T(8,128)S(1)}, u32[]{:S(2)}, u32[]{:S(2)}) collective-permute-start(f32[4,128,128]{2,1,0:T(8,128)S(1)} %slice_bitcast_fusion), channel_id=1, source_target_pairs={{0,4},{4,0},{8,12},{12,8},{16,20},{20,16},{24,28},{28,24},{1,5},{5... | collective-permute-start | bytes 786440 | tf_op jit(solution)/shard_map/gated_over_1/ppermute | solution.py:542
  22.6 7.9 %collective-permute-start.10 = (f32[4,128,128]{2,1,0:T(8,128)S(1)}, f32[4,128,128]{2,1,0:T(8,128)S(1)}, u32[]{:S(2)}, u32[]{:S(2)}) collective-permute-start(f32[4,128,128]{2,1,0:T(8,128)S(1)} %pad_maximum_fusion.4), channel_id=1, source_target_pairs={{0,4},{4,0},{8,12},{12,8},{16,20},{20,16},{24,28},{28,24},{1,5},{5... | collective-permute-start | bytes 786440 | tf_op jit(solution)/shard_map/filter_over_1/ppermute | solution.py:542
  23.5 9.0 %collective-permute-start.3 = (f32[2,128,128]{2,1,0:T(8,128)S(1)}, f32[2,128,128]{2,1,0:T(8,128)S(1)}, u32[]{:S(2)}, u32[]{:S(2)}) collective-permute-start(f32[2,128,128]{2,1,0:T(8,128)S(1)} %pad_maximum_fusion.19), channel_id=1, source_target_pairs={{0,8},{4,12},{8,0},{12,4},{16,24},{20,28},{24,16},{28,20},{1,9},{5... | collective-permute-start | bytes 393224 | tf_op jit(solution)/shard_map/gated_over_2/ppermute | solution.py:542
  23.6 12.6 %collective-permute-start.5 = (f32[2,128,128]{2,1,0:T(8,128)S(1)}, f32[2,128,128]{2,1,0:T(8,128)S(1)}, u32[]{:S(2)}, u32[]{:S(2)}) collective-permute-start(f32[2,128,128]{2,1,0:T(8,128)S(1)} %pad_maximum_fusion.20), channel_id=1, source_target_pairs={{0,16},{4,20},{8,24},{12,28},{16,0},{20,4},{24,8},{28,12},{1,17},{... | collective-permute-start | bytes 393224 | tf_op jit(solution)/shard_map/gated_over_4/ppermute | solution.py:542
  26.3 9.9 %collective-permute-start.6 = (f32[2,128,128]{2,1,0:T(8,128)S(1)}, f32[2,128,128]{2,1,0:T(8,128)S(1)}, u32[]{:S(2)}, u32[]{:S(2)}) collective-permute-start(f32[2,128,128]{2,1,0:T(8,128)S(1)} %pad_maximum_fusion.21), channel_id=1, source_target_pairs={{0,24},{4,28},{8,16},{12,20},{16,8},{20,12},{24,0},{28,4},{1,25},{... | collective-permute-start | bytes 393224 | tf_op jit(solution)/shard_map/gated_over_6/ppermute | solution.py:542
  28.1 11.0 %collective-permute-start.2 = (f32[576,128]{1,0:T(8,128)S(1)}, f32[576,128]{1,0:T(8,128)S(1)}, u32[]{:S(2)}, u32[]{:S(2)}) collective-permute-start(f32[576,128]{1,0:T(8,128)S(1)} %pad_maximum_fusion.3), channel_id=1, source_target_pairs={{0,4},{4,0},{8,12},{12,8},{16,20},{20,16},{24,28},{28,24},{1,5},{5... | collective-permute-start | bytes 884744 | tf_op jit(solution)/shard_map/carried_over_1/ppermute | solution.py:542
  30.5 0.9 %copy-start.1 = (bf16[256,256]{1,0:T(8,128)(2,1)S(1)}, bf16[256,256]{1,0:T(8,128)(2,1)}, u32[]{:S(2)}) copy-start(bf16[256,256]{1,0:T(8,128)(2,1)} %constant.46.clone.high_ref) | copy-start | bytes 393220
  30.5 0.9 %copy-start.4 = (f32[128,128]{1,0:T(8,128)S(1)}, f32[128,128]{1,0:T(8,128)}, u32[]{:S(2)}) copy-start(f32[128,128]{1,0:T(8,128)} %constant.48.clone.tw_ref) | copy-start | bytes 196612
  30.5 0.9 %copy-start.5 = (bf16[256,128]{1,0:T(8,128)(2,1)S(1)}, bf16[256,128]{1,0:T(8,128)(2,1)}, u32[]{:S(2)}) copy-start(bf16[256,128]{1,0:T(8,128)(2,1)} %constant.47.clone.low_ref) | copy-start | bytes 196612
  38.3 6.6 %collective-permute-start.11 = (f32[4,136,128]{2,1,0:T(8,128)S(1)}, f32[4,136,128]{2,1,0:T(8,128)S(1)}, u32[]{:S(2)}, u32[]{:S(2)}) collective-permute-start(f32[4,136,128]{2,1,0:T(8,128)S(1)} %slice.344), channel_id=1, source_target_pairs={{0,4},{4,0},{8,12},{12,8},{16,20},{20,16},{24,28},{28,24},{1,5},{5... | collective-permute-start | bytes 835592 | tf_op jit(solution)/shard_map/conv_over_1/ppermute | solution.py:542
  39.3 10.5 %collective-permute-start.12 = (f32[2,128,128]{2,1,0:T(8,128)S(1)}, f32[2,128,128]{2,1,0:T(8,128)S(1)}, u32[]{:S(2)}, u32[]{:S(2)}) collective-permute-start(f32[2,128,128]{2,1,0:T(8,128)S(1)} %get-tuple-element.47), channel_id=1, source_target_pairs={{0,16},{4,20},{8,24},{12,28},{16,0},{20,4},{24,8},{28,12},{1,17},{... | collective-permute-start | bytes 393224 | tf_op jit(solution)/shard_map/carried_over_4/ppermute | solution.py:542
  42.3 13.0 %collective-permute-start.4 = (f32[320,128]{1,0:T(8,128)S(1)}, f32[320,128]{1,0:T(8,128)S(1)}, u32[]{:S(2)}, u32[]{:S(2)}) collective-permute-start(f32[320,128]{1,0:T(8,128)S(1)} %get-tuple-element.126), channel_id=1, source_target_pairs={{0,8},{4,12},{8,0},{12,4},{16,24},{20,28},{24,16},{28,20},{1,9},{5... | collective-permute-start | bytes 491528 | tf_op jit(solution)/shard_map/carried_over_2/ppermute | solution.py:542
  42.4 12.9 %collective-permute-start.13 = (f32[320,128]{1,0:T(8,128)S(1)}, f32[320,128]{1,0:T(8,128)S(1)}, u32[]{:S(2)}, u32[]{:S(2)}) collective-permute-start(f32[320,128]{1,0:T(8,128)S(1)} %get-tuple-element.127), channel_id=1, source_target_pairs={{0,24},{4,28},{8,16},{12,20},{16,8},{20,12},{24,0},{28,4},{1,25},{... | collective-permute-start | bytes 491528 | tf_op jit(solution)/shard_map/carried_over_6/ppermute | solution.py:542
  45.0 13.8 %collective-permute-start.16 = (f32[2,136,128]{2,1,0:T(8,128)S(1)}, f32[2,136,128]{2,1,0:T(8,128)S(1)}, u32[]{:S(2)}, u32[]{:S(2)}) collective-permute-start(f32[2,136,128]{2,1,0:T(8,128)S(1)} %pad_maximum_fusion.13), channel_id=1, source_target_pairs={{0,8},{4,12},{8,0},{12,4},{16,24},{20,28},{24,16},{28,20},{1,9},{5... | collective-permute-start | bytes 417800 | tf_op jit(solution)/shard_map/conv_over_2/ppermute | solution.py:542
  49.8 14.3 %collective-permute-start.15 = (f32[2,136,128]{2,1,0:T(8,128)S(1)}, f32[2,136,128]{2,1,0:T(8,128)S(1)}, u32[]{:S(2)}, u32[]{:S(2)}) collective-permute-start(f32[2,136,128]{2,1,0:T(8,128)S(1)} %pad_maximum_fusion.7), channel_id=1, source_target_pairs={{0,16},{4,20},{8,24},{12,28},{16,0},{20,4},{24,8},{28,12},{1,17},{... | collective-permute-start | bytes 417800 | tf_op jit(solution)/shard_map/conv_over_4/ppermute | solution.py:542
  57.3 1.4 %copy-start.7 = (f32[1024]{0:T(1024)S(1)}, f32[1024]{0:T(1024)}, u32[]{:S(2)}) copy-start(f32[1024]{0:T(1024)} %param.12) | copy-start | bytes 12292
  57.4 6.6 %collective-permute-start.14 = (f32[4,136,128]{2,1,0:T(8,128)S(1)}, f32[4,136,128]{2,1,0:T(8,128)S(1)}, u32[]{:S(2)}, u32[]{:S(2)}) collective-permute-start(f32[4,136,128]{2,1,0:T(8,128)S(1)} %slice.350), channel_id=1, source_target_pairs={{0,4},{4,0},{8,12},{12,8},{16,20},{20,16},{24,28},{28,24},{1,5},{5... | collective-permute-start | bytes 835592 | tf_op jit(solution)/shard_map/corr_over_1/ppermute | solution.py:542
  64.1 6.5 %collective-permute-start.17 = (f32[2,136,128]{2,1,0:T(8,128)S(1)}, f32[2,136,128]{2,1,0:T(8,128)S(1)}, u32[]{:S(2)}, u32[]{:S(2)}) collective-permute-start(f32[2,136,128]{2,1,0:T(8,128)S(1)} %pad_maximum_fusion.10), channel_id=1, source_target_pairs={{0,8},{4,12},{8,0},{12,4},{16,24},{20,28},{24,16},{28,20},{1,9},{5... | collective-permute-start | bytes 417800 | tf_op jit(solution)/shard_map/corr_over_2/ppermute | solution.py:542
  66.0 7.0 %collective-permute-start.18 = (f32[2,136,128]{2,1,0:T(8,128)S(1)}, f32[2,136,128]{2,1,0:T(8,128)S(1)}, u32[]{:S(2)}, u32[]{:S(2)}) collective-permute-start(f32[2,136,128]{2,1,0:T(8,128)S(1)} %pad_maximum_fusion.8), channel_id=1, source_target_pairs={{0,24},{4,28},{8,16},{12,20},{16,8},{20,12},{24,0},{28,4},{1,25},{... | collective-permute-start | bytes 417800 | tf_op jit(solution)/shard_map/conv_over_6/ppermute | solution.py:542
  68.1 10.0 %collective-permute-start.22 = (f32[2,136,128]{2,1,0:T(8,128)S(1)}, f32[2,136,128]{2,1,0:T(8,128)S(1)}, u32[]{:S(2)}, u32[]{:S(2)}) collective-permute-start(f32[2,136,128]{2,1,0:T(8,128)S(1)} %pad_maximum_fusion.11), channel_id=1, source_target_pairs={{0,16},{4,20},{8,24},{12,28},{16,0},{20,4},{24,8},{28,12},{1,17},{... | collective-permute-start | bytes 417800 | tf_op jit(solution)/shard_map/corr_over_4/ppermute | solution.py:542
  68.1 10.0 %collective-permute-start.23 = (f32[2,136,128]{2,1,0:T(8,128)S(1)}, f32[2,136,128]{2,1,0:T(8,128)S(1)}, u32[]{:S(2)}, u32[]{:S(2)}) collective-permute-start(f32[2,136,128]{2,1,0:T(8,128)S(1)} %pad_maximum_fusion.12), channel_id=1, source_target_pairs={{0,24},{4,28},{8,16},{12,20},{16,8},{20,12},{24,0},{28,4},{1,25},{... | collective-permute-start | bytes 417800 | tf_op jit(solution)/shard_map/corr_over_6/ppermute | solution.py:542
  73.5 5.9 %collective-permute-start.21 = (f32[1,128]{1,0:T(1,128)S(1)}, f32[1,128]{1,0:T(1,128)S(1)}, u32[]{:S(2)}, u32[]{:S(2)}) collective-permute-start(f32[1,128]{1,0:T(1,128)S(1)} %get-tuple-element.67), channel_id=1, source_target_pairs={{0,3},{1,2},{2,1},{3,0},{4,7},{5,6},{6,5},{7,4},{8,11},{9,10},{10,... | collective-permute-start | bytes 1544 | tf_op jit(solution)/shard_map/squares_over_3/ppermute | solution.py:552
  73.5 5.9 %collective-permute-start.20 = (f32[1,128]{1,0:T(1,128)S(1)}, f32[1,128]{1,0:T(1,128)S(1)}, u32[]{:S(2)}, u32[]{:S(2)}) collective-permute-start(f32[1,128]{1,0:T(1,128)S(1)} %get-tuple-element.67), channel_id=1, source_target_pairs={{0,2},{1,3},{2,0},{3,1},{4,6},{5,7},{6,4},{7,5},{8,10},{9,11},{10,... | collective-permute-start | bytes 1544 | tf_op jit(solution)/shard_map/squares_over_2/ppermute | solution.py:552
  75.0 4.4 %collective-permute-start.19 = (f32[1,128]{1,0:T(1,128)S(1)}, f32[1,128]{1,0:T(1,128)S(1)}, u32[]{:S(2)}, u32[]{:S(2)}) collective-permute-start(f32[1,128]{1,0:T(1,128)S(1)} %get-tuple-element.67), channel_id=1, source_target_pairs={{0,1},{1,0},{2,3},{3,2},{4,5},{5,4},{6,7},{7,6},{8,9},{9,8},{10,11... | collective-permute-start | bytes 1544 | tf_op jit(solution)/shard_map/squares_over_1/ppermute | solution.py:552
  78.1 1.4 %copy-start.8 = (f32[1024]{0:T(1024)S(1)}, f32[1024]{0:T(1024)}, u32[]{:S(2)}) copy-start(f32[1024]{0:T(1024)} %param.13) | copy-start | bytes 12292

commit v6 on v5

--- a/solution.py
+++ b/solution.py
@@ -222,7 +222,7 @@
         in_specs=whole_operands(5),
         scratch_shapes=[split_scratch(blocks, rows, width), part, part],
         compiler_params=params(),
-        cost_estimate=measured(0.05 if conjugate else 20),
+        cost_estimate=measured(0.05),
         name="correlation" if conjugate else "convolution",
     )(own, x, spec, *tables)
 

time: 80.5 us -> 80.5 us (level)
  no operation moved by 1% of the time
where the time goes in v6:
time: 80.5 us; the launch traced here: 80.3 us
  starting transfers between devices  34 us (42%)
  waiting for transfers between devices  31.3 us (39%)
  Pallas kernels  11 us (14%)
  local copies, waits for them, and re-layouts  2.36 us (3%)
  between operations  1.19 us (1%)
    ppermute x20, waiting for transfers between devices, swapped(): return lax.ppermute(block, 'seq', route)  31.3 us
    ppermute x20, starting transfers between devices, swapped(): return lax.ppermute(block, 'seq', route)  27.2 us
    ppermute x1, starting transfers between devices, shift_along(): return lax.ppermute(block, axis, route)  4.87 us
    pallas_call x2, Pallas kernels, through_filter(): pl.pallas_call(functools.partial(product_kernel, conjugate, by_side), out...  3.99 us
    pallas_call x2, Pallas kernels, over_pairs(): pl.pallas_call(kernel, grid_spec=pltpu.PrefetchScalarGridSpec(num_scalar_...  3.04 us
    unnamed x18, local copies, waits for them, and re-layouts  1.95 us
    ppermute x3, starting transfers between devices, summed_over(): lax.ppermute(block, axis, [(i, i ^ apart) for i in range(count)])  1.89 us
  transfers between devices with their start and end apart: 24, of which 11 were waited for; matrix products, arithmetic and copies ran while one was open for 1% of the time, Pallas kernels for 12%

profile of v6, /device:TPU:0, one launch (start us, length us, event | category | flops | bytes accessed | tf_op | source)
XLA Modules:
  0.0 80.3 jit_solution(8876602440788417128)
XLA Ops:
  0.7 1.1 %copy-done.6 = f32[128,1024]{1,0:T(8,128)S(1)} copy-done((f32[128,1024]{1,0:T(8,128)S(1)}, f32[128,1024]{1,0:T(8,128)}, u32[]{:S(2)}) %copy-start.6) | copy-done | bytes 524312
  1.8 0.2 filter_blocks.1
  2.0 4.9 %collective-permute-start = (f32[3,2,1024]{2,1,0:T(2,128)S(1)}, f32[3,2,1024]{2,1,0:T(2,128)S(1)}, u32[]{:S(2)}, u32[]{:S(2)}) collective-permute-start(f32[3,2,1024]{2,1,0:T(2,128)S(1)} %get-tuple-element.77), channel_id=1, source_target_pairs={{0,4},{4,8},{8,12},{12,16},{16,20},{20,24},{24,28},{1,5},{5,9},{9,... | collective-permute-start | bytes 73736 | tf_op jit(solution)/shard_map/ppermute | solution.py:21
  6.9 1.6 %collective-permute-start.7 = (f32[2,128,128]{2,1,0:T(8,128)S(1)}, f32[2,128,128]{2,1,0:T(8,128)S(1)}, u32[]{:S(2)}, u32[]{:S(2)}) collective-permute-start(f32[2,128,128]{2,1,0:T(8,128)S(1)} %get-tuple-element.90), channel_id=1, source_target_pairs={{0,8},{4,12},{8,0},{12,4},{16,24},{20,28},{24,16},{28,20},{1,9},{5... | collective-permute-start | bytes 393224 | tf_op jit(solution)/shard_map/filter_over_2/ppermute | solution.py:542
  8.6 2.5 %collective-permute-start.9 = (f32[2,128,128]{2,1,0:T(8,128)S(1)}, f32[2,128,128]{2,1,0:T(8,128)S(1)}, u32[]{:S(2)}, u32[]{:S(2)}) collective-permute-start(f32[2,128,128]{2,1,0:T(8,128)S(1)} %get-tuple-element.91), channel_id=1, source_target_pairs={{0,24},{4,28},{8,16},{12,20},{16,8},{20,12},{24,0},{28,4},{1,25},{... | collective-permute-start | bytes 393224 | tf_op jit(solution)/shard_map/filter_over_6/ppermute | solution.py:542
  11.0 0.1 collective-permute-start.8
  11.3 0.0 collective-permute-done.before_ref
  11.3 1.2 %short_filters.1 = (f32[2,4,128,128]{3,2,1,0:T(8,128)S(1)}, f32[2,4,128,128]{3,2,1,0:T(8,128)S(1)}) custom-call(s32[1]{0:T(128)} %bitcast.own_ref, bf16[3,128,1024]{2,1,0:T(8,128)(2,1)S(1)} %copy-done, f32[3,2,1024]{2,1,0:T(2,128)S(1)} %collective-permute-done.before_ref, f32[3,3,1024]{2,1,0:T(4,128)S(1)} %copy-done.3, bf16[128,1024]{1,0:T(8,128)(2,1)S(1)} %copy-done.2), custom_call_target="tpu_custom_call" | custom-call | bytes 88560 | tf_op jit(solution)/shard_map/short_filters/pallas_call | solution.py:284
  12.6 1.5 %collective-permute-start.1 = (f32[4,128,128]{2,1,0:T(8,128)S(1)}, f32[4,128,128]{2,1,0:T(8,128)S(1)}, u32[]{:S(2)}, u32[]{:S(2)}) collective-permute-start(f32[4,128,128]{2,1,0:T(8,128)S(1)} %slice_bitcast_fusion), channel_id=1, source_target_pairs={{0,4},{4,0},{8,12},{12,8},{16,20},{20,16},{24,28},{28,24},{1,5},{5... | collective-permute-start | bytes 786440 | tf_op jit(solution)/shard_map/gated_over_1/ppermute | solution.py:542
  14.1 0.0 collective-permute-done.7
  14.1 4.1 %collective-permute-done.9 = f32[2,128,128]{2,1,0:T(8,128)S(1)} collective-permute-done((f32[2,128,128]{2,1,0:T(8,128)S(1)}, f32[2,128,128]{2,1,0:T(8,128)S(1)}, u32[]{:S(2)}, u32[]{:S(2)}) %collective-permute-start.9) | collective-permute-done | bytes 131104 | tf_op jit(solution)/shard_map/filter_over_6/ppermute | solution.py:542
  18.2 4.3 %collective-permute-done.8 = f32[2,128,128]{2,1,0:T(8,128)S(1)} collective-permute-done((f32[2,128,128]{2,1,0:T(8,128)S(1)}, f32[2,128,128]{2,1,0:T(8,128)S(1)}, u32[]{:S(2)}, u32[]{:S(2)}) %collective-permute-start.8) | collective-permute-done | bytes 131104 | tf_op jit(solution)/shard_map/filter_over_4/ppermute | solution.py:542
  22.6 0.9 %collective-permute-start.10 = (f32[4,128,128]{2,1,0:T(8,128)S(1)}, f32[4,128,128]{2,1,0:T(8,128)S(1)}, u32[]{:S(2)}, u32[]{:S(2)}) collective-permute-start(f32[4,128,128]{2,1,0:T(8,128)S(1)} %pad_maximum_fusion.4), channel_id=1, source_target_pairs={{0,4},{4,0},{8,12},{12,8},{16,20},{20,16},{24,28},{28,24},{1,5},{5... | collective-permute-start | bytes 786440 | tf_op jit(solution)/shard_map/filter_over_1/ppermute | solution.py:542
  23.5 0.0 collective-permute-done.1
  23.5 0.1 collective-permute-start.3
  23.6 2.7 %collective-permute-start.5 = (f32[2,128,128]{2,1,0:T(8,128)S(1)}, f32[2,128,128]{2,1,0:T(8,128)S(1)}, u32[]{:S(2)}, u32[]{:S(2)}) collective-permute-start(f32[2,128,128]{2,1,0:T(8,128)S(1)} %pad_maximum_fusion.20), channel_id=1, source_target_pairs={{0,16},{4,20},{8,24},{12,28},{16,0},{20,4},{24,8},{28,12},{1,17},{... | collective-permute-start | bytes 393224 | tf_op jit(solution)/shard_map/gated_over_4/ppermute | solution.py:542
  26.3 1.8 %collective-permute-start.6 = (f32[2,128,128]{2,1,0:T(8,128)S(1)}, f32[2,128,128]{2,1,0:T(8,128)S(1)}, u32[]{:S(2)}, u32[]{:S(2)}) collective-permute-start(f32[2,128,128]{2,1,0:T(8,128)S(1)} %pad_maximum_fusion.21), channel_id=1, source_target_pairs={{0,24},{4,28},{8,16},{12,20},{16,8},{20,12},{24,0},{28,4},{1,25},{... | collective-permute-start | bytes 393224 | tf_op jit(solution)/shard_map/gated_over_6/ppermute | solution.py:542
  28.1 1.2 %collective-permute-start.2 = (f32[576,128]{1,0:T(8,128)S(1)}, f32[576,128]{1,0:T(8,128)S(1)}, u32[]{:S(2)}, u32[]{:S(2)}) collective-permute-start(f32[576,128]{1,0:T(8,128)S(1)} %pad_maximum_fusion.3), channel_id=1, source_target_pairs={{0,4},{4,0},{8,12},{12,8},{16,20},{20,16},{24,28},{28,24},{1,5},{5... | collective-permute-start | bytes 884744 | tf_op jit(solution)/shard_map/carried_over_1/ppermute | solution.py:542
  29.4 1.1 %collective-permute-done.10 = f32[4,128,128]{2,1,0:T(8,128)S(1)} collective-permute-done((f32[4,128,128]{2,1,0:T(8,128)S(1)}, f32[4,128,128]{2,1,0:T(8,128)S(1)}, u32[]{:S(2)}, u32[]{:S(2)}) %collective-permute-start.10) | collective-permute-done | bytes 262176 | tf_op jit(solution)/shard_map/filter_over_1/ppermute | solution.py:542
  30.5 0.0 copy-start.1
  30.5 0.0 copy-start.4
  30.5 0.0 copy-start.5
  30.7 0.8 copy-done.1
  31.4 0.0 copy-done.5
  31.5 1.1 %filter_spectrum.1.spec_ref = f32[9,256,128]{2,1,0:T(8,128)S(1)} custom-call(s32[1]{0:T(128)} %bitcast.own_ref, f32[8,128,128]{2,1,0:T(8,128)S(1)} %bitcast.57, bf16[256,256]{1,0:T(8,128)(2,1)S(1)} %copy-done.1, bf16[256,128]{1,0:T(8,128)(2,1)S(1)} %copy-done.5, f32[128,128]{1,0:T(8,128)S(1)} %copy-done.4), custom_call_target="tpu_custom_call" | custom-call | bytes 4059000 | tf_op jit(solution)/shard_map/filter_spectrum/pallas_call | solution.py:205
  32.5 0.0 collective-permute-done.3
  32.5 3.7 %collective-permute-done.5 = f32[2,128,128]{2,1,0:T(8,128)S(1)} collective-permute-done((f32[2,128,128]{2,1,0:T(8,128)S(1)}, f32[2,128,128]{2,1,0:T(8,128)S(1)}, u32[]{:S(2)}, u32[]{:S(2)}) %collective-permute-start.5) | collective-permute-done | bytes 131104 | tf_op jit(solution)/shard_map/gated_over_4/ppermute | solution.py:542
  36.3 0.0 collective-permute-done.6
  36.3 2.0 %convolution.1 = f32[8,136,128]{2,1,0:T(8,128)S(1)} custom-call(s32[1]{0:T(128)} %bitcast.own_ref, f32[8,128,128]{2,1,0:T(8,128)S(1)} %bitcast.59, f32[9,256,128]{2,1,0:T(8,128)S(1)} %filter_spectrum.1.spec_ref, bf16[256,256]{1,0:T(8,128)(2,1)S(1)} %copy-done.1, bf16[256,128]{1,0:T(8,128)(2,1)S(1)} %copy-done.5, f32[128,128]{1,0:T(8,128)S(1)} %copy-done.4), custom_call_target="tpu_custom_call" | custom-call | bytes 184500 | tf_op jit(solution)/shard_map/convolution/pallas_call | solution.py:219
  38.3 0.8 %collective-permute-start.11 = (f32[4,136,128]{2,1,0:T(8,128)S(1)}, f32[4,136,128]{2,1,0:T(8,128)S(1)}, u32[]{:S(2)}, u32[]{:S(2)}) collective-permute-start(f32[4,136,128]{2,1,0:T(8,128)S(1)} %slice.344), channel_id=1, source_target_pairs={{0,4},{4,0},{8,12},{12,8},{16,20},{20,16},{24,28},{28,24},{1,5},{5... | collective-permute-start | bytes 835592 | tf_op jit(solution)/shard_map/conv_over_1/ppermute | solution.py:542
  39.2 0.0 collective-permute-done.2
  39.3 2.9 %collective-permute-start.12 = (f32[2,128,128]{2,1,0:T(8,128)S(1)}, f32[2,128,128]{2,1,0:T(8,128)S(1)}, u32[]{:S(2)}, u32[]{:S(2)}) collective-permute-start(f32[2,128,128]{2,1,0:T(8,128)S(1)} %get-tuple-element.47), channel_id=1, source_target_pairs={{0,16},{4,20},{8,24},{12,28},{16,0},{20,4},{24,8},{28,12},{1,17},{... | collective-permute-start | bytes 393224 | tf_op jit(solution)/shard_map/carried_over_4/ppermute | solution.py:542
  42.3 0.1 collective-permute-start.4
  42.4 1.5 %collective-permute-start.13 = (f32[320,128]{1,0:T(8,128)S(1)}, f32[320,128]{1,0:T(8,128)S(1)}, u32[]{:S(2)}, u32[]{:S(2)}) collective-permute-start(f32[320,128]{1,0:T(8,128)S(1)} %get-tuple-element.127), channel_id=1, source_target_pairs={{0,24},{4,28},{8,16},{12,20},{16,8},{20,12},{24,0},{28,4},{1,25},{... | collective-permute-start | bytes 491528 | tf_op jit(solution)/shard_map/carried_over_6/ppermute | solution.py:542
  43.8 1.1 %collective-permute-done.11 = f32[4,136,128]{2,1,0:T(8,128)S(1)} collective-permute-done((f32[4,136,128]{2,1,0:T(8,128)S(1)}, f32[4,136,128]{2,1,0:T(8,128)S(1)}, u32[]{:S(2)}, u32[]{:S(2)}) %collective-permute-start.11) | collective-permute-done | bytes 278560 | tf_op jit(solution)/shard_map/conv_over_1/ppermute | solution.py:542
  45.0 2.4 %collective-permute-start.16 = (f32[2,136,128]{2,1,0:T(8,128)S(1)}, f32[2,136,128]{2,1,0:T(8,128)S(1)}, u32[]{:S(2)}, u32[]{:S(2)}) collective-permute-start(f32[2,136,128]{2,1,0:T(8,128)S(1)} %pad_maximum_fusion.13), channel_id=1, source_target_pairs={{0,8},{4,12},{8,0},{12,4},{16,24},{20,28},{24,16},{28,20},{1,9},{5... | collective-permute-start | bytes 417800 | tf_op jit(solution)/shard_map/conv_over_2/ppermute | solution.py:542
  47.4 2.4 %collective-permute-done.12 = f32[2,128,128]{2,1,0:T(8,128)S(1)} collective-permute-done((f32[2,128,128]{2,1,0:T(8,128)S(1)}, f32[2,128,128]{2,1,0:T(8,128)S(1)}, u32[]{:S(2)}, u32[]{:S(2)}) %collective-permute-start.12) | collective-permute-done | bytes 131104 | tf_op jit(solution)/shard_map/carried_over_4/ppermute | solution.py:542
  49.8 0.0 collective-permute-start.15
  49.8 5.5 %collective-permute-done.13 = f32[320,128]{1,0:T(8,128)S(1)} collective-permute-done((f32[320,128]{1,0:T(8,128)S(1)}, f32[320,128]{1,0:T(8,128)S(1)}, u32[]{:S(2)}, u32[]{:S(2)}) %collective-permute-start.13) | collective-permute-done | bytes 163872 | tf_op jit(solution)/shard_map/carried_over_6/ppermute | solution.py:542
  55.3 0.0 collective-permute-done.4
  55.3 2.0 %correlation.1 = f32[8,136,128]{2,1,0:T(8,128)S(1)} custom-call(s32[1]{0:T(128)} %bitcast.own_ref, f32[8,128,128]{2,1,0:T(8,128)S(1)} %bitcast.58, f32[9,256,128]{2,1,0:T(8,128)S(1)} %filter_spectrum.1.spec_ref, bf16[256,256]{1,0:T(8,128)(2,1)S(1)} %copy-done.1, bf16[256,128]{1,0:T(8,128)(2,1)S(1)} %copy-done.5, f32[128,128]{1,0:T(8,128)S(1)} %copy-done.4), custom_call_target="tpu_custom_call" | custom-call | bytes 184500 | tf_op jit(solution)/shard_map/correlation/pallas_call | solution.py:219
  57.3 0.0 copy-start.7
  57.4 1.3 %collective-permute-start.14 = (f32[4,136,128]{2,1,0:T(8,128)S(1)}, f32[4,136,128]{2,1,0:T(8,128)S(1)}, u32[]{:S(2)}, u32[]{:S(2)}) collective-permute-start(f32[4,136,128]{2,1,0:T(8,128)S(1)} %slice.350), channel_id=1, source_target_pairs={{0,4},{4,0},{8,12},{12,8},{16,20},{20,16},{24,28},{28,24},{1,5},{5... | collective-permute-start | bytes 835592 | tf_op jit(solution)/shard_map/corr_over_1/ppermute | solution.py:542
  58.8 0.0 collective-permute-done.16.refs_1_
  58.8 1.9 %rows_with_rim.1 = (f32[128,1024]{1,0:T(8,128)S(1)}, f32[136,1024]{1,0:T(8,128)S(1)}, f32[136,1024]{1,0:T(8,128)S(1)}, f32[136,1024]{1,0:T(8,128)S(1)}, f32[136,...) custom-call(s32[1]{0:T(128)} %bitcast.own_ref, bf16[3,128,1024]{2,1,0:T(8,128)(2,1)S(1)} %copy-done, ...), custom_call_target="tpu_custom_call" | custom-call | bytes 147600 | tf_op jit(solution)/shard_map/rows_with_rim/pallas_call | solution.py:284
  60.7 3.3 %collective-permute-done.14 = f32[4,136,128]{2,1,0:T(8,128)S(1)} collective-permute-done((f32[4,136,128]{2,1,0:T(8,128)S(1)}, f32[4,136,128]{2,1,0:T(8,128)S(1)}, u32[]{:S(2)}, u32[]{:S(2)}) %collective-permute-start.14) | collective-permute-done | bytes 278560 | tf_op jit(solution)/shard_map/corr_over_1/ppermute | solution.py:542
  64.1 0.0 collective-permute-done.15.refs_2_
  64.1 1.9 %collective-permute-start.17 = (f32[2,136,128]{2,1,0:T(8,128)S(1)}, f32[2,136,128]{2,1,0:T(8,128)S(1)}, u32[]{:S(2)}, u32[]{:S(2)}) collective-permute-start(f32[2,136,128]{2,1,0:T(8,128)S(1)} %pad_maximum_fusion.10), channel_id=1, source_target_pairs={{0,8},{4,12},{8,0},{12,4},{16,24},{20,28},{24,16},{28,20},{1,9},{5... | collective-permute-start | bytes 417800 | tf_op jit(solution)/shard_map/corr_over_2/ppermute | solution.py:542
  66.0 2.1 %collective-permute-start.18 = (f32[2,136,128]{2,1,0:T(8,128)S(1)}, f32[2,136,128]{2,1,0:T(8,128)S(1)}, u32[]{:S(2)}, u32[]{:S(2)}) collective-permute-start(f32[2,136,128]{2,1,0:T(8,128)S(1)} %pad_maximum_fusion.8), channel_id=1, source_target_pairs={{0,24},{4,28},{8,16},{12,20},{16,8},{20,12},{24,0},{28,4},{1,25},{... | collective-permute-start | bytes 417800 | tf_op jit(solution)/shard_map/conv_over_6/ppermute | solution.py:542
  68.1 0.0 collective-permute-start.22
  68.1 1.8 %collective-permute-start.23 = (f32[2,136,128]{2,1,0:T(8,128)S(1)}, f32[2,136,128]{2,1,0:T(8,128)S(1)}, u32[]{:S(2)}, u32[]{:S(2)}) collective-permute-start(f32[2,136,128]{2,1,0:T(8,128)S(1)} %pad_maximum_fusion.12), channel_id=1, source_target_pairs={{0,24},{4,28},{8,16},{12,20},{16,8},{20,12},{24,0},{28,4},{1,25},{... | collective-permute-start | bytes 417800 | tf_op jit(solution)/shard_map/corr_over_6/ppermute | solution.py:542
  69.9 0.7 collective-permute-done.17.refs_1_
  70.6 2.4 %collective-permute-done.18.refs_3_ = f32[2,136,128]{2,1,0:T(8,128)S(1)} collective-permute-done((f32[2,136,128]{2,1,0:T(8,128)S(1)}, f32[2,136,128]{2,1,0:T(8,128)S(1)}, u32[]{:S(2)}, u32[]{:S(2)}) %collective-permute-start.18) | collective-permute-done | bytes 139296 | tf_op jit(solution)/shard_map/conv_over_6/ppermute | solution.py:542
  73.0 0.5 mixed_squares.1
  73.5 0.0 collective-permute-start.21
  73.5 1.6 %collective-permute-start.20 = (f32[1,128]{1,0:T(1,128)S(1)}, f32[1,128]{1,0:T(1,128)S(1)}, u32[]{:S(2)}, u32[]{:S(2)}) collective-permute-start(f32[1,128]{1,0:T(1,128)S(1)} %get-tuple-element.67), channel_id=1, source_target_pairs={{0,2},{1,3},{2,0},{3,1},{4,6},{5,7},{6,4},{7,5},{8,10},{9,11},{10,... | collective-permute-start | bytes 1544 | tf_op jit(solution)/shard_map/squares_over_2/ppermute | solution.py:552
  75.0 0.3 collective-permute-start.19
  75.4 2.7 %collective-permute-done.22.refs_2_ = f32[2,136,128]{2,1,0:T(8,128)S(1)} collective-permute-done((f32[2,136,128]{2,1,0:T(8,128)S(1)}, f32[2,136,128]{2,1,0:T(8,128)S(1)}, u32[]{:S(2)}, u32[]{:S(2)}) %collective-permute-start.22) | collective-permute-done | bytes 139296 | tf_op jit(solution)/shard_map/corr_over_4/ppermute | solution.py:542
  78.1 0.0 collective-permute-done.23.refs_3_
  78.1 1.3 %stream_grads.1 = bf16[3,128,1024]{2,1,0:T(8,128)(2,1)} custom-call(s32[1]{0:T(128)} %bitcast.own_ref, f32[136,1024]{1,0:T(8,128)S(1)} %get-tuple-element.68.key_ref, f32[136,1024]{1,0:T(8,128)S(1)} %get-tuple-element.69.value_ref, f32[136,1024]{1,0:T(8,128)S(1)} %get-tuple-element.70.carried_ref, f32[3,3,1024]{2,1,0:T(4,128)S(1)} %copy-done.3, ...), custom_call_target="tpu_custom_call" | custom-call | bytes 184500 | tf_op jit(solution)/shard_map/stream_grads/pallas_call | solution.py:523
  79.4 0.0 collective-permute-done.21
  79.4 0.0 collective-permute-done.20
  79.4 0.0 collective-permute-done.19
  79.4 0.9 %norm.1 = bf16[128,1024]{1,0:T(8,128)(2,1)} custom-call(f32[128,1024]{1,0:T(8,128)S(1)} %get-tuple-element.66.mixed_ref, f32[1,128]{1,0:T(1,128)S(1)} %add_add_fusion.square_ref, f32[1,1024]{1,0:T(1,128)S(1)} %bitcast.61), custom_call_target="tpu_custom_call" | custom-call | bytes 73800 | tf_op jit(solution)/shard_map/norm/pallas_call | solution.py:490
  (61 shorter events, 0.9 us)
Async XLA Ops:
  0.6 1.4 %copy-start = (bf16[3,128,1024]{2,1,0:T(8,128)(2,1)S(1)}, bf16[3,128,1024]{2,1,0:T(8,128)(2,1)}, u32[]{:S(2)}) copy-start(bf16[3,128,1024]{2,1,0:T(8,128)(2,1)} %streams_ref.3) | copy-start | bytes 2359300
  0.6 10.5 %copy-start.2 = (bf16[128,1024]{1,0:T(8,128)(2,1)S(1)}, bf16[128,1024]{1,0:T(8,128)(2,1)}, u32[]{:S(2)}) copy-start(bf16[128,1024]{1,0:T(8,128)(2,1)} %cot_ref.3) | copy-start | bytes 786436
  0.7 1.1 %copy-start.6 = (f32[128,1024]{1,0:T(8,128)S(1)}, f32[128,1024]{1,0:T(8,128)}, u32[]{:S(2)}) copy-start(f32[128,1024]{1,0:T(8,128)} %x_ref.1) | copy-start | bytes 1572868
  1.8 9.5 %copy-start.3 = (f32[3,3,1024]{2,1,0:T(4,128)S(1)}, f32[3,3,1024]{2,1,0:T(4,128)}, u32[]{:S(2)}) copy-start(f32[3,3,1024]{2,1,0:T(4,128)} %taps_ref.7) | copy-start | bytes 110596
  2.0 9.2 %collective-permute-start = (f32[3,2,1024]{2,1,0:T(2,128)S(1)}, f32[3,2,1024]{2,1,0:T(2,128)S(1)}, u32[]{:S(2)}, u32[]{:S(2)}) collective-permute-start(f32[3,2,1024]{2,1,0:T(2,128)S(1)} %get-tuple-element.77), channel_id=1, source_target_pairs={{0,4},{4,8},{8,12},{12,16},{16,20},{20,24},{24,28},{1,5},{5,9},{9,... | collective-permute-start | bytes 73736 | tf_op jit(solution)/shard_map/ppermute | solution.py:21
  6.9 7.2 %collective-permute-start.7 = (f32[2,128,128]{2,1,0:T(8,128)S(1)}, f32[2,128,128]{2,1,0:T(8,128)S(1)}, u32[]{:S(2)}, u32[]{:S(2)}) collective-permute-start(f32[2,128,128]{2,1,0:T(8,128)S(1)} %get-tuple-element.90), channel_id=1, source_target_pairs={{0,8},{4,12},{8,0},{12,4},{16,24},{20,28},{24,16},{28,20},{1,9},{5... | collective-permute-start | bytes 393224 | tf_op jit(solution)/shard_map/filter_over_2/ppermute | solution.py:542
  8.6 9.6 %collective-permute-start.9 = (f32[2,128,128]{2,1,0:T(8,128)S(1)}, f32[2,128,128]{2,1,0:T(8,128)S(1)}, u32[]{:S(2)}, u32[]{:S(2)}) collective-permute-start(f32[2,128,128]{2,1,0:T(8,128)S(1)} %get-tuple-element.91), channel_id=1, source_target_pairs={{0,24},{4,28},{8,16},{12,20},{16,8},{20,12},{24,0},{28,4},{1,25},{... | collective-permute-start | bytes 393224 | tf_op jit(solution)/shard_map/filter_over_6/ppermute | solution.py:542
  11.0 11.5 %collective-permute-start.8 = (f32[2,128,128]{2,1,0:T(8,128)S(1)}, f32[2,128,128]{2,1,0:T(8,128)S(1)}, u32[]{:S(2)}, u32[]{:S(2)}) collective-permute-start(f32[2,128,128]{2,1,0:T(8,128)S(1)} %get-tuple-element.92), channel_id=1, source_target_pairs={{0,16},{4,20},{8,24},{12,28},{16,0},{20,4},{24,8},{28,12},{1,17},{... | collective-permute-start | bytes 393224 | tf_op jit(solution)/shard_map/filter_over_4/ppermute | solution.py:542
  12.6 10.9 %collective-permute-start.1 = (f32[4,128,128]{2,1,0:T(8,128)S(1)}, f32[4,128,128]{2,1,0:T(8,128)S(1)}, u32[]{:S(2)}, u32[]{:S(2)}) collective-permute-start(f32[4,128,128]{2,1,0:T(8,128)S(1)} %slice_bitcast_fusion), channel_id=1, source_target_pairs={{0,4},{4,0},{8,12},{12,8},{16,20},{20,16},{24,28},{28,24},{1,5},{5... | collective-permute-start | bytes 786440 | tf_op jit(solution)/shard_map/gated_over_1/ppermute | solution.py:542
  22.6 7.9 %collective-permute-start.10 = (f32[4,128,128]{2,1,0:T(8,128)S(1)}, f32[4,128,128]{2,1,0:T(8,128)S(1)}, u32[]{:S(2)}, u32[]{:S(2)}) collective-permute-start(f32[4,128,128]{2,1,0:T(8,128)S(1)} %pad_maximum_fusion.4), channel_id=1, source_target_pairs={{0,4},{4,0},{8,12},{12,8},{16,20},{20,16},{24,28},{28,24},{1,5},{5... | collective-permute-start | bytes 786440 | tf_op jit(solution)/shard_map/filter_over_1/ppermute | solution.py:542
  23.5 9.0 %collective-permute-start.3 = (f32[2,128,128]{2,1,0:T(8,128)S(1)}, f32[2,128,128]{2,1,0:T(8,128)S(1)}, u32[]{:S(2)}, u32[]{:S(2)}) collective-permute-start(f32[2,128,128]{2,1,0:T(8,128)S(1)} %pad_maximum_fusion.19), channel_id=1, source_target_pairs={{0,8},{4,12},{8,0},{12,4},{16,24},{20,28},{24,16},{28,20},{1,9},{5... | collective-permute-start | bytes 393224 | tf_op jit(solution)/shard_map/gated_over_2/ppermute | solution.py:542
  23.6 12.6 %collective-permute-start.5 = (f32[2,128,128]{2,1,0:T(8,128)S(1)}, f32[2,128,128]{2,1,0:T(8,128)S(1)}, u32[]{:S(2)}, u32[]{:S(2)}) collective-permute-start(f32[2,128,128]{2,1,0:T(8,128)S(1)} %pad_maximum_fusion.20), channel_id=1, source_target_pairs={{0,16},{4,20},{8,24},{12,28},{16,0},{20,4},{24,8},{28,12},{1,17},{... | collective-permute-start | bytes 393224 | tf_op jit(solution)/shard_map/gated_over_4/ppermute | solution.py:542
  26.3 9.9 %collective-permute-start.6 = (f32[2,128,128]{2,1,0:T(8,128)S(1)}, f32[2,128,128]{2,1,0:T(8,128)S(1)}, u32[]{:S(2)}, u32[]{:S(2)}) collective-permute-start(f32[2,128,128]{2,1,0:T(8,128)S(1)} %pad_maximum_fusion.21), channel_id=1, source_target_pairs={{0,24},{4,28},{8,16},{12,20},{16,8},{20,12},{24,0},{28,4},{1,25},{... | collective-permute-start | bytes 393224 | tf_op jit(solution)/shard_map/gated_over_6/ppermute | solution.py:542
  28.1 11.0 %collective-permute-start.2 = (f32[576,128]{1,0:T(8,128)S(1)}, f32[576,128]{1,0:T(8,128)S(1)}, u32[]{:S(2)}, u32[]{:S(2)}) collective-permute-start(f32[576,128]{1,0:T(8,128)S(1)} %pad_maximum_fusion.3), channel_id=1, source_target_pairs={{0,4},{4,0},{8,12},{12,8},{16,20},{20,16},{24,28},{28,24},{1,5},{5... | collective-permute-start | bytes 884744 | tf_op jit(solution)/shard_map/carried_over_1/ppermute | solution.py:542
  30.5 0.9 %copy-start.1 = (bf16[256,256]{1,0:T(8,128)(2,1)S(1)}, bf16[256,256]{1,0:T(8,128)(2,1)}, u32[]{:S(2)}) copy-start(bf16[256,256]{1,0:T(8,128)(2,1)} %constant.46.clone.high_ref) | copy-start | bytes 393220
  30.5 0.9 %copy-start.4 = (f32[128,128]{1,0:T(8,128)S(1)}, f32[128,128]{1,0:T(8,128)}, u32[]{:S(2)}) copy-start(f32[128,128]{1,0:T(8,128)} %constant.48.clone.tw_ref) | copy-start | bytes 196612
  30.5 0.9 %copy-start.5 = (bf16[256,128]{1,0:T(8,128)(2,1)S(1)}, bf16[256,128]{1,0:T(8,128)(2,1)}, u32[]{:S(2)}) copy-start(bf16[256,128]{1,0:T(8,128)(2,1)} %constant.47.clone.low_ref) | copy-start | bytes 196612
  38.3 6.6 %collective-permute-start.11 = (f32[4,136,128]{2,1,0:T(8,128)S(1)}, f32[4,136,128]{2,1,0:T(8,128)S(1)}, u32[]{:S(2)}, u32[]{:S(2)}) collective-permute-start(f32[4,136,128]{2,1,0:T(8,128)S(1)} %slice.344), channel_id=1, source_target_pairs={{0,4},{4,0},{8,12},{12,8},{16,20},{20,16},{24,28},{28,24},{1,5},{5... | collective-permute-start | bytes 835592 | tf_op jit(solution)/shard_map/conv_over_1/ppermute | solution.py:542
  39.3 10.5 %collective-permute-start.12 = (f32[2,128,128]{2,1,0:T(8,128)S(1)}, f32[2,128,128]{2,1,0:T(8,128)S(1)}, u32[]{:S(2)}, u32[]{:S(2)}) collective-permute-start(f32[2,128,128]{2,1,0:T(8,128)S(1)} %get-tuple-element.47), channel_id=1, source_target_pairs={{0,16},{4,20},{8,24},{12,28},{16,0},{20,4},{24,8},{28,12},{1,17},{... | collective-permute-start | bytes 393224 | tf_op jit(solution)/shard_map/carried_over_4/ppermute | solution.py:542
  42.3 13.0 %collective-permute-start.4 = (f32[320,128]{1,0:T(8,128)S(1)}, f32[320,128]{1,0:T(8,128)S(1)}, u32[]{:S(2)}, u32[]{:S(2)}) collective-permute-start(f32[320,128]{1,0:T(8,128)S(1)} %get-tuple-element.126), channel_id=1, source_target_pairs={{0,8},{4,12},{8,0},{12,4},{16,24},{20,28},{24,16},{28,20},{1,9},{5... | collective-permute-start | bytes 491528 | tf_op jit(solution)/shard_map/carried_over_2/ppermute | solution.py:542
  42.4 12.9 %collective-permute-start.13 = (f32[320,128]{1,0:T(8,128)S(1)}, f32[320,128]{1,0:T(8,128)S(1)}, u32[]{:S(2)}, u32[]{:S(2)}) collective-permute-start(f32[320,128]{1,0:T(8,128)S(1)} %get-tuple-element.127), channel_id=1, source_target_pairs={{0,24},{4,28},{8,16},{12,20},{16,8},{20,12},{24,0},{28,4},{1,25},{... | collective-permute-start | bytes 491528 | tf_op jit(solution)/shard_map/carried_over_6/ppermute | solution.py:542
  45.0 13.8 %collective-permute-start.16 = (f32[2,136,128]{2,1,0:T(8,128)S(1)}, f32[2,136,128]{2,1,0:T(8,128)S(1)}, u32[]{:S(2)}, u32[]{:S(2)}) collective-permute-start(f32[2,136,128]{2,1,0:T(8,128)S(1)} %pad_maximum_fusion.13), channel_id=1, source_target_pairs={{0,8},{4,12},{8,0},{12,4},{16,24},{20,28},{24,16},{28,20},{1,9},{5... | collective-permute-start | bytes 417800 | tf_op jit(solution)/shard_map/conv_over_2/ppermute | solution.py:542
  49.8 14.3 %collective-permute-start.15 = (f32[2,136,128]{2,1,0:T(8,128)S(1)}, f32[2,136,128]{2,1,0:T(8,128)S(1)}, u32[]{:S(2)}, u32[]{:S(2)}) collective-permute-start(f32[2,136,128]{2,1,0:T(8,128)S(1)} %pad_maximum_fusion.7), channel_id=1, source_target_pairs={{0,16},{4,20},{8,24},{12,28},{16,0},{20,4},{24,8},{28,12},{1,17},{... | collective-permute-start | bytes 417800 | tf_op jit(solution)/shard_map/conv_over_4/ppermute | solution.py:542
  57.3 1.4 %copy-start.7 = (f32[1024]{0:T(1024)S(1)}, f32[1024]{0:T(1024)}, u32[]{:S(2)}) copy-start(f32[1024]{0:T(1024)} %param.12) | copy-start | bytes 12292
  57.4 6.6 %collective-permute-start.14 = (f32[4,136,128]{2,1,0:T(8,128)S(1)}, f32[4,136,128]{2,1,0:T(8,128)S(1)}, u32[]{:S(2)}, u32[]{:S(2)}) collective-permute-start(f32[4,136,128]{2,1,0:T(8,128)S(1)} %slice.350), channel_id=1, source_target_pairs={{0,4},{4,0},{8,12},{12,8},{16,20},{20,16},{24,28},{28,24},{1,5},{5... | collective-permute-start | bytes 835592 | tf_op jit(solution)/shard_map/corr_over_1/ppermute | solution.py:542
  64.1 6.5 %collective-permute-start.17 = (f32[2,136,128]{2,1,0:T(8,128)S(1)}, f32[2,136,128]{2,1,0:T(8,128)S(1)}, u32[]{:S(2)}, u32[]{:S(2)}) collective-permute-start(f32[2,136,128]{2,1,0:T(8,128)S(1)} %pad_maximum_fusion.10), channel_id=1, source_target_pairs={{0,8},{4,12},{8,0},{12,4},{16,24},{20,28},{24,16},{28,20},{1,9},{5... | collective-permute-start | bytes 417800 | tf_op jit(solution)/shard_map/corr_over_2/ppermute | solution.py:542
  66.0 7.0 %collective-permute-start.18 = (f32[2,136,128]{2,1,0:T(8,128)S(1)}, f32[2,136,128]{2,1,0:T(8,128)S(1)}, u32[]{:S(2)}, u32[]{:S(2)}) collective-permute-start(f32[2,136,128]{2,1,0:T(8,128)S(1)} %pad_maximum_fusion.8), channel_id=1, source_target_pairs={{0,24},{4,28},{8,16},{12,20},{16,8},{20,12},{24,0},{28,4},{1,25},{... | collective-permute-start | bytes 417800 | tf_op jit(solution)/shard_map/conv_over_6/ppermute | solution.py:542
  68.1 10.0 %collective-permute-start.22 = (f32[2,136,128]{2,1,0:T(8,128)S(1)}, f32[2,136,128]{2,1,0:T(8,128)S(1)}, u32[]{:S(2)}, u32[]{:S(2)}) collective-permute-start(f32[2,136,128]{2,1,0:T(8,128)S(1)} %pad_maximum_fusion.11), channel_id=1, source_target_pairs={{0,16},{4,20},{8,24},{12,28},{16,0},{20,4},{24,8},{28,12},{1,17},{... | collective-permute-start | bytes 417800 | tf_op jit(solution)/shard_map/corr_over_4/ppermute | solution.py:542
  68.1 10.0 %collective-permute-start.23 = (f32[2,136,128]{2,1,0:T(8,128)S(1)}, f32[2,136,128]{2,1,0:T(8,128)S(1)}, u32[]{:S(2)}, u32[]{:S(2)}) collective-permute-start(f32[2,136,128]{2,1,0:T(8,128)S(1)} %pad_maximum_fusion.12), channel_id=1, source_target_pairs={{0,24},{4,28},{8,16},{12,20},{16,8},{20,12},{24,0},{28,4},{1,25},{... | collective-permute-start | bytes 417800 | tf_op jit(solution)/shard_map/corr_over_6/ppermute | solution.py:542
  73.5 5.9 %collective-permute-start.21 = (f32[1,128]{1,0:T(1,128)S(1)}, f32[1,128]{1,0:T(1,128)S(1)}, u32[]{:S(2)}, u32[]{:S(2)}) collective-permute-start(f32[1,128]{1,0:T(1,128)S(1)} %get-tuple-element.67), channel_id=1, source_target_pairs={{0,3},{1,2},{2,1},{3,0},{4,7},{5,6},{6,5},{7,4},{8,11},{9,10},{10,... | collective-permute-start | bytes 1544 | tf_op jit(solution)/shard_map/squares_over_3/ppermute | solution.py:552
  73.5 5.9 %collective-permute-start.20 = (f32[1,128]{1,0:T(1,128)S(1)}, f32[1,128]{1,0:T(1,128)S(1)}, u32[]{:S(2)}, u32[]{:S(2)}) collective-permute-start(f32[1,128]{1,0:T(1,128)S(1)} %get-tuple-element.67), channel_id=1, source_target_pairs={{0,2},{1,3},{2,0},{3,1},{4,6},{5,7},{6,4},{7,5},{8,10},{9,11},{10,... | collective-permute-start | bytes 1544 | tf_op jit(solution)/shard_map/squares_over_2/ppermute | solution.py:552
  75.0 4.4 %collective-permute-start.19 = (f32[1,128]{1,0:T(1,128)S(1)}, f32[1,128]{1,0:T(1,128)S(1)}, u32[]{:S(2)}, u32[]{:S(2)}) collective-permute-start(f32[1,128]{1,0:T(1,128)S(1)} %get-tuple-element.67), channel_id=1, source_target_pairs={{0,1},{1,0},{2,3},{3,2},{4,5},{5,4},{6,7},{7,6},{8,9},{9,8},{10,11... | collective-permute-start | bytes 1544 | tf_op jit(solution)/shard_map/squares_over_1/ppermute | solution.py:552
  78.1 1.4 %copy-start.8 = (f32[1024]{0:T(1024)S(1)}, f32[1024]{0:T(1024)}, u32[]{:S(2)}) copy-start(f32[1024]{0:T(1024)} %param.13) | copy-start | bytes 12292
